TPU v7x, 32 devices: a whole 2x2x4 slice. The times are simulated.
32 devices in a mesh: dp: 8 (over y, x, core), tensor: 4 (over z).
Axes of the slice: x: 2, y: 2, z: 4, core: 2. Of those that a mesh axis runs over, the one named last changes fastest.
Arguments:
- hidden_in: float32 [16384, 1024], P(('dp', 'tensor')), may hold values from -6 to 6
- ln1_gain: bfloat16 [1024], P(('dp', 'tensor')), may hold values from 0.25 to 1.75
- ln1_bias: bfloat16 [1024], P(('dp', 'tensor')), may hold values from -3 to 3
- qkv_weight: bfloat16 [1024, 3072], P('dp', 'tensor'), may hold values from -0.1875 to 0.1875
- qkv_bias: bfloat16 [16, 128], P('tensor', 'dp'), may hold values from -3 to 3
- out_weight: bfloat16 [1024, 1024], P('tensor', 'dp'), may hold values from -0.75 to 0.75
- out_bias: bfloat16 [1024], P(('dp', 'tensor')), may hold values from -3 to 3
- ln2_gain: bfloat16 [1024], P(('dp', 'tensor')), may hold values from 0.25 to 1.75
- ln2_bias: bfloat16 [1024], P(('dp', 'tensor')), may hold values from -3 to 3
- up_weight: bfloat16 [1024, 4096], P('dp', 'tensor'), may hold values from -0.1875 to 0.1875
- up_bias: bfloat16 [16, 256], P('tensor', 'dp'), may hold values from -3 to 3
- down_weight: bfloat16 [4096, 1024], P('tensor', 'dp'), may hold values from -0.09375 to 0.09375
- down_bias: bfloat16 [1024], P(('dp', 'tensor')), may hold values from -3 to 3
- cotangent: float32 [16384, 1024], P(('dp', 'tensor')), may hold values from -6 to 6
Outputs:
- output: float32 [16384, 1024], P(('dp', 'tensor'))
- grad_in: float32 [16384, 1024], P(('dp', 'tensor'))
- grad_ln1_gain: float32 [1024], P(('dp', 'tensor'))
- grad_ln1_bias: float32 [1024], P(('dp', 'tensor'))
- grad_qkv_weight: float32 [1024, 3072], P('dp', 'tensor')
- grad_qkv_bias: float32 [16, 128], P('tensor', 'dp')
- grad_out_weight: float32 [1024, 1024], P('tensor', 'dp')
- grad_out_bias: float32 [1024], P(('dp', 'tensor'))
- grad_ln2_gain: float32 [1024], P(('dp', 'tensor'))
- grad_ln2_bias: float32 [1024], P(('dp', 'tensor'))
- grad_up_weight: float32 [1024, 4096], P('dp', 'tensor')
- grad_up_bias: float32 [16, 256], P('tensor', 'dp')
- grad_down_weight: float32 [4096, 1024], P('tensor', 'dp')
- grad_down_bias: float32 [1024], P(('dp', 'tensor'))
All inputs are finite; a program needn't handle non-finite values.
Results may differ from a plain program's by a relative error of at most 0.023.
Values may be sent and summed in bfloat16 or wider, within the bound.
No kernel may reach another device: no remote copies, remote signals or barrier semaphores. Data moves between devices by JAX's collectives and lax.ppermute only.
A program may use at most 128 MiB of HBM per device.

v0:
```python
import jax
import jax.numpy as jnp
from jax import lax
from jax.sharding import PartitionSpec as P

H = 16
HD = 64
FF = 4096
SEQ_LEN = 1024


EPSILON = 1e-05
MASKED = -1e30


def layer_norm(values, gain, shift):
    mean_row = jnp.mean(values, axis=-1, keepdims=True)
    centred = values - mean_row
    spread = jnp.mean(centred * centred, axis=-1, keepdims=True)
    return centred * lax.rsqrt(spread + EPSILON) * gain + shift


def gelu_tanh(values):
    inner = 0.7978845608028654 * (values + 0.044715 * values * values * values)
    return 0.5 * values * (1.0 + jnp.tanh(inner))


def contract_rows(left, right):
    return lax.dot_general(
        left, right, (((0,), (0,)), ((), ())), preferred_element_type=jnp.float32
    )


def contract_cols(left, right):
    return lax.dot_general(
        left, right, (((1,), (1,)), ((), ())), preferred_element_type=jnp.float32
    )


def block_scores(query_blk, keys_seq, slopes, row_start):
    query_count = query_blk.shape[0]
    key_count = keys_seq.shape[0]
    raw_scores = jnp.einsum("qhe,khe->hqk", query_blk, keys_seq, preferred_element_type=jnp.float32)
    query_pos = row_start + jnp.arange(query_count)
    key_pos = jnp.arange(key_count)
    offset = (key_pos[None, :] - query_pos[:, None]).astype(jnp.float32)
    scores = raw_scores * HD ** (-0.5) + slopes[:, None, None] * offset[None]
    return jnp.where((key_pos[None, :] <= query_pos[:, None])[None], scores, MASKED)


def local(
    hidden_in,
    ln1_gain,
    ln1_bias,
    qkv_weight,
    qkv_bias,
    out_weight,
    out_bias,
    ln2_gain,
    ln2_bias,
    up_weight,
    up_bias,
    down_weight,
    down_bias,
    cotangent,
):
    vectors = (
        lax.all_gather(ln1_gain, ("dp", "tensor"), axis=0, tiled=True),
        lax.all_gather(ln1_bias, ("dp", "tensor"), axis=0, tiled=True),
        lax.all_gather(out_bias, ("dp", "tensor"), axis=0, tiled=True),
        lax.all_gather(ln2_gain, ("dp", "tensor"), axis=0, tiled=True),
        lax.all_gather(ln2_bias, ("dp", "tensor"), axis=0, tiled=True),
        lax.all_gather(down_bias, ("dp", "tensor"), axis=0, tiled=True),
    )
    gain_one, shift_one, bias_out, gain_two, shift_two, bias_down = [
        vector.astype(jnp.float32) for vector in vectors
    ]
    w_qkv, b_qkv, w_out, w_up, b_up, w_down = (
        lax.all_gather(qkv_weight, "dp", axis=0, tiled=True),
        lax.all_gather(qkv_bias, "dp", axis=1, tiled=True),
        lax.all_gather(out_weight, "dp", axis=1, tiled=True),
        lax.all_gather(up_weight, "dp", axis=0, tiled=True),
        lax.all_gather(up_bias, "dp", axis=1, tiled=True),
        lax.all_gather(down_weight, "dp", axis=1, tiled=True),
    )
    tok_rows = hidden_in.shape[0]
    heads_here = w_qkv.shape[1] // (3 * HD)
    group_rows = tok_rows * lax.axis_size("tensor")
    seq_count = group_rows // SEQ_LEN
    block_rows = min(512, SEQ_LEN)
    block_count = SEQ_LEN // block_rows
    score_scale = HD ** (-0.5)
    bias_qkv = b_qkv.astype(jnp.float32)
    bias_full = jnp.concatenate(
        [bias_qkv[:, :HD], jnp.zeros((heads_here, HD), jnp.float32), bias_qkv[:, HD:]], axis=1
    ).reshape(-1)
    bias_up = b_up.astype(jnp.float32).reshape(-1)
    head_ids = lax.axis_index("tensor") * heads_here + jnp.arange(heads_here)
    slopes = jnp.exp2(-8.0 * (head_ids + 1).astype(jnp.float32) / H)
    normed_one = layer_norm(hidden_in, gain_one, shift_one)
    rows_one = lax.all_gather(normed_one.astype(jnp.bfloat16), "tensor", axis=0, tiled=True)
    qkv_full = jnp.dot(rows_one, w_qkv, preferred_element_type=jnp.float32) + bias_full
    qkv_low = qkv_full.astype(jnp.bfloat16).reshape(seq_count, SEQ_LEN, heads_here, 3, HD)
    queries = qkv_low[:, :, :, 0]
    keys_all = qkv_low[:, :, :, 1]
    values_all = qkv_low[:, :, :, 2]

    def forward_sequence(seq_parts):
        query_seq, keys_seq, values_seq = seq_parts

        def forward_block(block_index):
            row_start = block_index * block_rows
            query_blk = lax.dynamic_slice_in_dim(query_seq, row_start, block_rows, 0)
            scores = block_scores(query_blk, keys_seq, slopes, row_start)
            row_max = jnp.max(scores, axis=2, keepdims=True)
            exp_scores = jnp.exp(scores - row_max)
            exp_total = jnp.sum(exp_scores, axis=2, keepdims=True)
            attn_probs = (exp_scores / exp_total).astype(jnp.bfloat16)
            attended = jnp.einsum(
                "hqk,khe->qhe", attn_probs, values_seq, preferred_element_type=jnp.float32
            )
            return (attended, (row_max + jnp.log(exp_total))[:, :, 0])

        attended, log_sums = lax.map(forward_block, jnp.arange(block_count))
        return (
            attended.reshape(SEQ_LEN, heads_here, HD),
            jnp.moveaxis(log_sums, 0, 1).reshape(heads_here, SEQ_LEN),
        )

    attended, log_sums = lax.map(forward_sequence, (queries, keys_all, values_all))
    context = attended.reshape(group_rows, heads_here * HD).astype(jnp.bfloat16)
    residual_mid = (
        hidden_in
        + lax.psum_scatter(
            jnp.dot(context, w_out, preferred_element_type=jnp.float32).astype(jnp.bfloat16),
            "tensor",
            scatter_dimension=0,
            tiled=True,
        ).astype(jnp.float32)
        + bias_out
    )
    normed_two = layer_norm(residual_mid, gain_two, shift_two)
    rows_two = lax.all_gather(normed_two.astype(jnp.bfloat16), "tensor", axis=0, tiled=True)
    up_pre = jnp.dot(rows_two, w_up, preferred_element_type=jnp.float32) + bias_up
    active = gelu_tanh(up_pre).astype(jnp.bfloat16)
    output = (
        residual_mid
        + lax.psum_scatter(
            jnp.dot(active, w_down, preferred_element_type=jnp.float32).astype(jnp.bfloat16),
            "tensor",
            scatter_dimension=0,
            tiled=True,
        ).astype(jnp.float32)
        + bias_down
    )
    grad_down_bias = jnp.sum(cotangent, axis=0)
    cot_rows = lax.all_gather(cotangent.astype(jnp.bfloat16), "tensor", axis=0, tiled=True)
    grad_w_down = contract_rows(active, cot_rows)
    grad_active = contract_cols(cot_rows, w_down)
    gelu_value, gelu_back = jax.vjp(gelu_tanh, up_pre)
    grad_pre = gelu_back(grad_active)[0].astype(jnp.bfloat16)
    grad_b_up = jnp.sum(grad_pre.astype(jnp.float32), axis=0).reshape(-1, FF // H)
    grad_w_up = contract_rows(rows_two, grad_pre)
    grad_normed_two = lax.psum_scatter(
        contract_cols(grad_pre, w_up).astype(jnp.bfloat16),
        "tensor",
        scatter_dimension=0,
        tiled=True,
    ).astype(jnp.float32)
    norm_value, norm_back_two = jax.vjp(layer_norm, residual_mid, gain_two, shift_two)
    grad_mid_part, grad_gain_two, grad_shift_two = norm_back_two(grad_normed_two)
    grad_mid = cotangent + grad_mid_part
    grad_bias_out = jnp.sum(grad_mid, axis=0)
    mid_rows = lax.all_gather(grad_mid.astype(jnp.bfloat16), "tensor", axis=0, tiled=True)
    grad_w_out = contract_rows(context, mid_rows)
    grad_context = (
        contract_cols(mid_rows, w_out)
        .astype(jnp.bfloat16)
        .reshape(seq_count, SEQ_LEN, heads_here, HD)
    )

    def backward_sequence(seq_parts):
        query_seq, keys_seq, values_seq, grad_seq, lse_seq = seq_parts

        def backward_block(running, block_index):
            grad_keys, grad_values = running
            row_start = block_index * block_rows
            query_blk = lax.dynamic_slice_in_dim(query_seq, row_start, block_rows, 0)
            grad_blk = lax.dynamic_slice_in_dim(grad_seq, row_start, block_rows, 0)
            lse_blk = lax.dynamic_slice_in_dim(lse_seq, row_start, block_rows, 1)
            scores = block_scores(query_blk, keys_seq, slopes, row_start)
            full_probs = jnp.exp(scores - lse_blk[:, :, None])
            grad_probs = jnp.einsum(
                "qhe,khe->hqk", grad_blk, values_seq, preferred_element_type=jnp.float32
            )
            inner_sum = jnp.sum(full_probs * grad_probs, axis=2, keepdims=True)
            grad_scores = (full_probs * (grad_probs - inner_sum)).astype(jnp.bfloat16)
            grad_query = (
                jnp.einsum(
                    "hqk,khe->qhe", grad_scores, keys_seq, preferred_element_type=jnp.float32
                )
                * score_scale
            )
            grad_keys = (
                grad_keys
                + jnp.einsum(
                    "hqk,qhe->khe", grad_scores, query_blk, preferred_element_type=jnp.float32
                )
                * score_scale
            )
            grad_values = grad_values + jnp.einsum(
                "hqk,qhe->khe",
                full_probs.astype(jnp.bfloat16),
                grad_blk,
                preferred_element_type=jnp.float32,
            )
            return ((grad_keys, grad_values), grad_query)

        zero_grads = jnp.zeros((SEQ_LEN, heads_here, HD), jnp.float32)
        (grad_keys, grad_values), grad_query = lax.scan(
            backward_block, (zero_grads, zero_grads), jnp.arange(block_count)
        )
        grad_query = grad_query.reshape(SEQ_LEN, heads_here, HD)
        return jnp.stack([grad_query, grad_keys, grad_values], axis=2)

    grad_qkv = lax.map(backward_sequence, (queries, keys_all, values_all, grad_context, log_sums))
    grad_qkv = grad_qkv.reshape(group_rows, heads_here * 3 * HD).astype(jnp.bfloat16)
    qkv_sums = jnp.sum(grad_qkv.astype(jnp.float32), axis=0).reshape(heads_here, 3, HD)
    grad_b_qkv = jnp.concatenate([qkv_sums[:, 0], qkv_sums[:, 2]], axis=1)
    grad_w_qkv = contract_rows(rows_one, grad_qkv)
    grad_normed_one = lax.psum_scatter(
        contract_cols(grad_qkv, w_qkv).astype(jnp.bfloat16),
        "tensor",
        scatter_dimension=0,
        tiled=True,
    ).astype(jnp.float32)
    first_value, norm_back_one = jax.vjp(layer_norm, hidden_in, gain_one, shift_one)
    grad_in_part, grad_gain_one, grad_shift_one = norm_back_one(grad_normed_one)
    grad_in = grad_mid + grad_in_part
    vector_sums = (
        lax.psum_scatter(grad_gain_one, ("dp", "tensor"), scatter_dimension=0, tiled=True),
        lax.psum_scatter(grad_shift_one, ("dp", "tensor"), scatter_dimension=0, tiled=True),
        lax.psum_scatter(grad_bias_out, ("dp", "tensor"), scatter_dimension=0, tiled=True),
        lax.psum_scatter(grad_gain_two, ("dp", "tensor"), scatter_dimension=0, tiled=True),
        lax.psum_scatter(grad_shift_two, ("dp", "tensor"), scatter_dimension=0, tiled=True),
        lax.psum_scatter(grad_down_bias, ("dp", "tensor"), scatter_dimension=0, tiled=True),
    )
    all_sums = (
        lax.psum_scatter(grad_w_qkv, "dp", scatter_dimension=0, tiled=True),
        lax.psum_scatter(grad_b_qkv, "dp", scatter_dimension=1, tiled=True),
        lax.psum_scatter(grad_w_out, "dp", scatter_dimension=1, tiled=True),
        lax.psum_scatter(grad_w_up, "dp", scatter_dimension=0, tiled=True),
        lax.psum_scatter(grad_b_up, "dp", scatter_dimension=1, tiled=True),
        lax.psum_scatter(grad_w_down, "dp", scatter_dimension=1, tiled=True),
    )
    sum_w_qkv, sum_b_qkv, sum_w_out, sum_w_up, sum_b_up, sum_w_down = all_sums
    return (
        output,
        grad_in,
        vector_sums[0],
        vector_sums[1],
        sum_w_qkv,
        sum_b_qkv,
        sum_w_out,
        vector_sums[2],
        vector_sums[3],
        vector_sums[4],
        sum_w_up,
        sum_b_up,
        sum_w_down,
        vector_sums[5],
    )


def solution(mesh):
    placed = (
        P(("dp", "tensor"), None),
        P(("dp", "tensor")),
        P(("dp", "tensor")),
        P("dp", "tensor"),
        P("tensor", "dp"),
        P("tensor", "dp"),
        P(("dp", "tensor")),
        P(("dp", "tensor")),
        P(("dp", "tensor")),
        P("dp", "tensor"),
        P("tensor", "dp"),
        P("tensor", "dp"),
        P(("dp", "tensor")),
        P(("dp", "tensor"), None),
    )
    return jax.shard_map(
        local,
        mesh=mesh,
        in_specs=placed,
        out_specs=(
            P(("dp", "tensor"), None),
            P(("dp", "tensor"), None),
            P(("dp", "tensor")),
            P(("dp", "tensor")),
            P("dp", "tensor"),
            P("tensor", "dp"),
            P("tensor", "dp"),
            P(("dp", "tensor")),
            P(("dp", "tensor")),
            P(("dp", "tensor")),
            P("dp", "tensor"),
            P("tensor", "dp"),
            P("tensor", "dp"),
            P(("dp", "tensor")),
        ),
        check_vma=False,
    )
```

profile of v0, /device:TPU:1, one launch (start us, length us, event | category | flops | bytes accessed | tf_op | source)
XLA Modules:
  0.0 1242.1 jit_solution(15610893041203511617)
XLA Ops:
  13.0 41.2 %all-reduce.13 = (bf16[1024]{0:T(1024)(128)(2,1)S(1)}, bf16[1024]{0:T(1024)(128)(2,1)S(1)}, bf16[1024]{0:T(1024)(128)(2,1)}, bf16[1024]{0:T(1024)(128)(2,1)}, bf...) all-reduce(bf16[1024]{0:T(1024)(128)(2,1)S(1)} %dynamic-update-slic, ...), channel_id=1, replica_groups=mesh['dp'=8,'tensor'=4] {'dp','tensor'}, use_global_device_ids=true, to_apply=%add.1 | all-reduce | flops 6144 | bytes 24576
  60.6 11.0 all-gather
  71.9 10.1 all_gather.53
  82.0 60.1 %all-gather.10.cloned.1.call-done = bf16[2048,1024]{1,0:T(8,128)(2,1)} async-done(((bf16[512,1024]{1,0:T(8,128)(2,1)}), bf16[2048,1024]{1,0:T(8,128)(2,1)}) %all-gather.10.cloned.1.call-update) | async-done | bytes 4194320 | tf_op jit(solution)/shard_map/all_gather | solution.py:101
  142.1 6.1 add_convert_fusion
  148.3 3.2 copy.67
  151.4 4.8 reshape.236
  161.2 53.3 %while.54 = (s32[]{:T(128)}, bf16[2,1024,4,64]{3,2,1,0:T(4,128)(2,1)}, f32[2,4,1024]{2,1,0:T(4,128)S(1)}, bf16[2,1024,4,64]{1,3,2,0:T(8,128)(2,1)}, bf16[2,1024,...) while((s32[]{:T(128)}, ...), condition=%wide.region_7.8_spmd.clone, body=%wide.region_2.7_spmd.clone.sunk | while | flops 576190976 | bytes 43359724 | solution.py:130
  163.5 22.3 %while.57 = (s32[]{:T(128)}, bf16[2,512,4,64]{1,3,2,0:T(8,128)(2,1)S(1)}, f32[2,4,512]{2,1,0:T(4,128)S(1)}, s32[2]{0:T(128)S(1)}, bf16[1024,4,64]{0,2,1:T(8,128)...) while((s32[]{:T(128)}, ...), condition=%wide.region_6.6_spmd, body=%wide.region_3.5_spmd.sunk | while | flops 576190976 | bytes 37559508 | solution.py:124
  165.3 2.9 fusion.131
  168.2 3.0 fusion.132
  171.2 3.4 fusion.133
  176.5 2.9 fusion.131
  179.4 3.0 fusion.132
  182.4 3.4 fusion.133
  190.1 22.3 %while.57 = (s32[]{:T(128)}, bf16[2,512,4,64]{1,3,2,0:T(8,128)(2,1)S(1)}, f32[2,4,512]{2,1,0:T(4,128)S(1)}, s32[2]{0:T(128)S(1)}, bf16[1024,4,64]{0,2,1:T(8,128)...) while((s32[]{:T(128)}, ...), condition=%wide.region_6.6_spmd, body=%wide.region_3.5_spmd.sunk | while | flops 576190976 | bytes 37559508 | solution.py:124
  192.0 2.9 fusion.131
  194.9 3.0 fusion.132
  197.9 3.4 fusion.133
  203.1 2.9 fusion.131
  206.0 3.0 fusion.132
  209.0 3.4 fusion.133
  214.5 3.9 reshape.259
  219.4 4.2 convolution_convert_fusion
  224.4 74.8 %reduce-scatter.15.cloned.1.call-done = bf16[512,1024]{1,0:T(8,128)(2,1)} async-done(((bf16[2048,1024]{1,0:T(8,128)(2,1)}), bf16[512,1024]{1,0:T(8,128)(2,1)}) %reduce-scatter.15.cloned.1.call-update) | async-done | bytes 1048592 | tf_op jit(solution)/shard_map/reduce_scatter | solution.py:134
  305.9 9.3 all-gather.1
  315.3 14.5 %all-gather.16.cloned.1.call-done = bf16[1024,1024]{1,0:T(8,128)(2,1)} async-done(((bf16[128,1024]{1,0:T(8,128)(2,1)}), bf16[1024,1024]{1,0:T(8,128)(2,1)}) %all-gather.16.cloned.1.call-update) | async-done | bytes 2097168 | tf_op jit(solution)/shard_map/all_gather | solution.py:82
  329.9 82.4 %all-gather.14.cloned.1.call-done = bf16[2048,1024]{1,0:T(8,128)(2,1)} async-done(((bf16[512,1024]{1,0:T(8,128)(2,1)}), bf16[2048,1024]{1,0:T(8,128)(2,1)}) %all-gather.14.cloned.1.call-update) | async-done | bytes 4194320 | tf_op jit(solution)/shard_map/all_gather | solution.py:143
  412.3 10.6 fusion.63
  423.0 18.4 %all-gather.18.cloned.1.call-done = bf16[1024,1024]{1,0:T(8,128)(2,1)} async-done(((bf16[1024,128]{1,0:T(8,128)(2,1)}), bf16[1024,1024]{1,0:T(8,128)(2,1)}) %all-gather.18.cloned.1.call-update) | async-done | bytes 2097168 | tf_op jit(solution)/shard_map/all_gather | solution.py:84
  441.4 82.0 %all-gather.20.cloned.1.call-done = bf16[2048,1024]{1,0:T(8,128)(2,1)} async-done(((bf16[512,1024]{1,0:T(8,128)(2,1)}), bf16[2048,1024]{1,0:T(8,128)(2,1)}) %all-gather.20.cloned.1.call-update) | async-done | bytes 4194320 | tf_op jit(solution)/shard_map/all_gather | solution.py:157
  523.4 15.0 %convert_reduce_fusion = (f32[1024]{0:T(1024)S(1)}, bf16[2048,1024]{1,0:T(8,128)(2,1)S(1)}) fusion(f32[2048,1024]{1,0:T(8,128)} %fusion.63, f32[1024]{0:T(1024)S(1)} %bitcast.177, bf16[2048,1024]{1,0:T(8,128)(2,1)} %all-gather.20.cloned.1.call-done, bf16[1024,1024]{1,0:T(8,128)(2,1)} %all-gather.18.cloned.1.call-done), kind=kOutput, calls=%fused_computation.68 | convolution fusion | flops 4351589376 | bytes 18882560 | tf_op jit(solution)/shard_map/dot_general | solution.py:35
  540.4 6.2 convolution_convert_fusion.2
  548.3 11.1 convolution_convert_fusion.3
  560.0 62.1 %reduce-scatter.19.cloned.1.call-done = bf16[512,1024]{1,0:T(8,128)(2,1)} async-done(((bf16[2048,1024]{1,0:T(8,128)(2,1)}), bf16[512,1024]{1,0:T(8,128)(2,1)}) %reduce-scatter.19.cloned.1.call-update) | async-done | bytes 1048592 | tf_op jit(solution)/shard_map/reduce_scatter | solution.py:164
  624.7 2.9 fusion.49
  627.6 74.1 %reduce-scatter.17.cloned.1.call-done = bf16[512,1024]{1,0:T(8,128)(2,1)} async-done(((bf16[2048,1024]{1,0:T(8,128)(2,1)}), bf16[512,1024]{1,0:T(8,128)(2,1)}) %reduce-scatter.17.cloned.1.call-update) | async-done | bytes 1048592 | tf_op jit(solution)/shard_map/reduce_scatter | solution.py:148
  701.8 4.7 fusion.59
  710.0 80.3 %all-gather.22.cloned.1.call-done = bf16[2048,1024]{1,0:T(8,128)(2,1)} async-done(((bf16[512,1024]{1,0:T(8,128)(2,1)}), bf16[2048,1024]{1,0:T(8,128)(2,1)}) %all-gather.22.cloned.1.call-update) | async-done | bytes 4194320 | tf_op jit(solution)/shard_map/all_gather | solution.py:174
  790.3 3.5 convolution_convert_fusion.4
  797.1 117.8 %while.56 = (s32[]{:T(128)}, bf16[2,1024,4,3,64]{1,4,2,3,0:T(8,128)(2,1)}, bf16[2,1024,4,64]{1,3,2,0:T(8,128)(2,1)}, bf16[2,1024,4,64]{1,3,2,0:T(8,128)(2,1)}, f...) while((s32[]{:T(128)}, ...), condition=%wide.region_19.20_spmd.clone, body=%wide.region_15.19_spmd.clone.sunk | while | flops 1373108736 | bytes 85801528 | solution.py:226
  801.5 51.5 %while.58 = (s32[]{:T(128)}, f32[1024,4,64]{0,2,1:T(8,128)S(1)}, f32[1024,4,64]{0,2,1:T(8,128)S(1)}, bf16[2,512,4,64]{1,0,3,2:T(2,128)(2,1)}, s32[2]{0:T(128)S(1...) while((s32[]{:T(128)}, f32[1024,4,64]{0,2,1:T(8,128)S(1)}, ...), condition=%wide.region_18.18_spmd.clone, body=%wide.region_16.17_spmd.clone.sunk | while | flops 1368390144 | bytes 76331264 | solution.py:220
  805.8 5.0 multiply_reduce_fusion.4
  817.5 9.8 dynamic_update_slice.41
  831.5 5.0 multiply_reduce_fusion.4
  843.2 9.8 dynamic_update_slice.41
  860.3 51.5 %while.58 = (s32[]{:T(128)}, f32[1024,4,64]{0,2,1:T(8,128)S(1)}, f32[1024,4,64]{0,2,1:T(8,128)S(1)}, bf16[2,512,4,64]{1,0,3,2:T(2,128)(2,1)}, s32[2]{0:T(128)S(1...) while((s32[]{:T(128)}, f32[1024,4,64]{0,2,1:T(8,128)S(1)}, ...), condition=%wide.region_18.18_spmd.clone, body=%wide.region_16.17_spmd.clone.sunk | while | flops 1368390144 | bytes 76331264 | solution.py:220
  864.6 5.0 multiply_reduce_fusion.4
  876.3 9.8 dynamic_update_slice.41
  890.4 5.0 multiply_reduce_fusion.4
  902.0 9.8 dynamic_update_slice.41
  917.7 3.2 copy.78
  922.9 6.6 convolution_convert_fusion.1
  930.2 12.6 %fusion.55 = f32[1024,1024]{1,0:T(8,128)} fusion(bf16[2048,1024]{1,0:T(8,128)(2,1)} %all-gather.20.cloned.1.call-done, f32[2048,1024]{1,0:T(8,128)} %fusion.63, f32[1024]{0:T(1024)S(1)} %bitcast.179), kind=kOutput, calls=%fused_computation.123 | convolution fusion | flops 4315938816 | bytes 16781312 | tf_op jit(solution)/shard_map/dot_general | solution.py:29
  942.9 10.0 fusion.66
  954.2 4.5 fusion.65
  959.0 8.4 fusion.64
  970.3 63.7 %reduce-scatter.21.cloned.1.call-done = bf16[512,1024]{1,0:T(8,128)(2,1)} async-done(((bf16[2048,1024]{1,0:T(8,128)(2,1)}), bf16[512,1024]{1,0:T(8,128)(2,1)}) %reduce-scatter.21.cloned.1.call-update) | async-done | bytes 1048592 | tf_op jit(solution)/shard_map/reduce_scatter | solution.py:231
  1038.3 40.4 %all-reduce.12 = (f32[1024]{0:T(1024)S(1)}, f32[1024]{0:T(1024)S(1)}, f32[1024]{0:T(1024)S(1)}, f32[1024]{0:T(1024)S(1)}, f32[1024]{0:T(1024)S(1)}, /*index=5*/f32[1024]{0:T(1024)S(1)}) all-reduce(f32[1024]{0:T(1024)S(1)} %get-tuple-element.342, ...), channel_id=6, replica_groups=mesh['dp'=8,'tensor'=4] {'dp','tensor'}, use_global_device_ids=true, to_apply=%region_24.25.clone | all-reduce | flops 6144 | bytes 49152
  1082.2 3.6 add_add_fusion.2
  1085.8 4.0 reduce-scatter.29.cloned.1.call-done
  1089.8 55.5 %reduce-scatter.27.cloned.1.call-done = f32[128,1024]{1,0:T(8,128)} async-done(((f32[1024,1024]{1,0:T(8,128)}), f32[128,1024]{1,0:T(8,128)}) %reduce-scatter.27.cloned.1.call-update) | async-done | bytes 524304 | tf_op jit(solution)/shard_map/reduce_scatter | solution.py:252
  1145.4 39.5 %reduce-scatter.25.cloned.1.call-done = f32[256,128]{1,0:T(8,128)} async-done(((f32[256,1024]{1,0:T(8,128)}), f32[256,128]{1,0:T(8,128)}) %reduce-scatter.25.cloned.1.call-update) | async-done | bytes 131088 | tf_op jit(solution)/shard_map/reduce_scatter | solution.py:251
  1184.9 50.2 %reduce-scatter.23.cloned.1.call-done = f32[128,768]{1,0:T(8,128)} async-done(((f32[1024,768]{1,0:T(8,128)}), f32[128,768]{1,0:T(8,128)}) %reduce-scatter.23.cloned.1.call-update) | async-done | bytes 393232 | tf_op jit(solution)/shard_map/reduce_scatter | solution.py:249
  (288 shorter events, 125.8 us)
Async XLA Ops:
  7.2 52.0 %copy-start = (f32[512,1024]{1,0:T(8,128)S(1)}, f32[512,1024]{1,0:T(8,128)}, u32[]{:S(2)}) copy-start(f32[512,1024]{1,0:T(8,128)} %param.22) | copy-start | bytes 6291460
  7.2 74.8 %all-gather.12.cloned.1.call-start = ((), (), s32[]{:S(2)}) async-start(), calls=%async_computation.11 | async-start | bytes 1769472 | tf_op jit(solution)/shard_map/all_gather | solution.py:79
  7.9 134.2 %all-gather.10.cloned.1.call-start = ((), (), s32[]{:S(2)}) async-start(), calls=%async_computation.10 | async-start | bytes 5242880 | tf_op jit(solution)/shard_map/all_gather | solution.py:101
  54.2 6.4 copy-start.15
  54.2 6.4 copy-start.34
  54.2 17.7 %copy-start.19 = (bf16[256,128]{1,0:T(8,128)(2,1)S(1)}, bf16[256,128]{1,0:T(8,128)(2,1)}, u32[]{:S(2)}) copy-start(bf16[256,128]{1,0:T(8,128)(2,1)} %param.27) | copy-start | bytes 196612
  56.0 2.5 copy-start.17
  58.0 0.6 copy-start.22
  58.5 0.6 copy-start.20
  60.5 238.6 %reduce-scatter.15.cloned.1.call-start = ((), (), s32[]{:S(2)}) async-start(), calls=%async_computation.12 | async-start | bytes 5242880 | tf_op jit(solution)/shard_map/reduce_scatter | solution.py:134
  214.5 3.9 copy-start.5
  218.4 1.0 copy-start.11
  223.6 0.7 copy-start.33
  223.6 0.7 copy-start.32
  223.6 0.7 copy-start.31
  223.6 75.5 %copy-start.1 = (f32[512,1024]{1,0:T(8,128)S(1)}, f32[512,1024]{1,0:T(8,128)}, u32[]{:S(2)}) copy-start(f32[512,1024]{1,0:T(8,128)} %param.22) | copy-start | bytes 6291460
  223.7 106.2 %all-gather.16.cloned.1.call-start = ((), (), s32[]{:S(2)}) async-start(), calls=%async_computation.14 | async-start | bytes 2359296 | tf_op jit(solution)/shard_map/all_gather | solution.py:82
  224.3 188.1 %all-gather.14.cloned.1.call-start = ((), (), s32[]{:S(2)}) async-start(), calls=%async_computation.13 | async-start | bytes 5242880 | tf_op jit(solution)/shard_map/all_gather | solution.py:143
  300.7 1.3 copy-start.3
  300.8 3.3 copy-start.10
  302.1 3.9 copy-start.35
  303.5 137.9 %all-gather.18.cloned.1.call-start = ((), (), s32[]{:S(2)}) async-start(), calls=%async_computation.15 | async-start | bytes 2359296 | tf_op jit(solution)/shard_map/all_gather | solution.py:84
  304.0 219.4 %all-gather.20.cloned.1.call-start = ((), (), s32[]{:S(2)}) async-start(), calls=%async_computation.17 | async-start | bytes 5242880 | tf_op jit(solution)/shard_map/all_gather | solution.py:157
  305.9 316.3 %reduce-scatter.19.cloned.1.call-start = ((), (), s32[]{:S(2)}) async-start(), calls=%async_computation.18 | async-start | bytes 5242880 | tf_op jit(solution)/shard_map/reduce_scatter | solution.py:164
  315.3 231.8 %copy-start.28 = (f32[1,2,4,128]{3,1,2,0:T(2,128)}, f32[1,2,4,128]{3,1,2,0:T(2,128)S(1)}, u32[]{:S(2)}) copy-start(f32[1,2,4,128]{3,1,2,0:T(2,128)S(1)} %copy.88) | copy-start | bytes 12292
  523.4 17.0 %copy-start.36 = (bf16[1024,1024]{1,0:T(8,128)(2,1)S(1)}, bf16[1024,1024]{1,0:T(8,128)(2,1)}, u32[]{:S(2)}) copy-start(bf16[1024,1024]{1,0:T(8,128)(2,1)} %all-gather.16.cloned.1.call-done) | copy-start | bytes 6291460
  538.5 1.9 copy-start.38
  546.7 1.6 copy-start.37
  546.7 155.1 %reduce-scatter.17.cloned.1.call-start = ((), (), s32[]{:S(2)}) async-start(), calls=%async_computation.16 | async-start | bytes 5242880 | tf_op jit(solution)/shard_map/reduce_scatter | solution.py:148
  559.4 0.7 copy-start.30
  559.4 62.8 %copy-start.4 = (f32[512,1024]{1,0:T(8,128)S(1)}, f32[512,1024]{1,0:T(8,128)}, u32[]{:S(2)}) copy-start(f32[512,1024]{1,0:T(8,128)} %copy-done.3) | copy-start | bytes 6291460
  559.4 230.9 %all-gather.22.cloned.1.call-start = ((), (), s32[]{:S(2)}) async-start(), calls=%async_computation.19 | async-start | bytes 5242880 | tf_op jit(solution)/shard_map/all_gather | solution.py:174
  622.2 79.6 %copy-start.8 = (bf16[512,1024]{1,0:T(8,128)(2,1)S(1)}, bf16[512,1024]{1,0:T(8,128)(2,1)}, u32[]{:S(2)}) copy-start(bf16[512,1024]{1,0:T(8,128)(2,1)} %reduce-scatter.19.cloned.1.call-done) | copy-start | bytes 3145732
  706.4 1.3 copy-start.6
  706.4 83.9 %copy-start.14 = (bf16[256,1024]{1,0:T(8,128)(2,1)S(1)}, bf16[256,1024]{1,0:T(8,128)(2,1)}, u32[]{:S(2)}) copy-start(bf16[256,1024]{1,0:T(8,128)(2,1)} %all_gather.53) | copy-start | bytes 1572868
  708.9 258.5 %reduce-scatter.33.cloned.1.call-start = ((), (), s32[]{:S(2)}) async-start(), calls=%async_computation.26 | async-start | bytes 147456
  709.8 259.2 %reduce-scatter.31.cloned.1.call-start = ((), (), s32[]{:S(2)}) async-start(), calls=%async_computation.25 | async-start | bytes 73728
  914.8 2.8 copy-start.7
  922.0 7.6 copy-start.13
  922.9 111.1 %reduce-scatter.21.cloned.1.call-start = ((), (), s32[]{:S(2)}) async-start(), calls=%async_computation.20 | async-start | bytes 5242880 | tf_op jit(solution)/shard_map/reduce_scatter | solution.py:231
  929.6 0.7 copy-start.29
  929.6 160.2 %reduce-scatter.29.cloned.1.call-start = ((), (), s32[]{:S(2)}) async-start(), calls=%async_computation.24 | async-start | bytes 4718592 | tf_op jit(solution)/shard_map/reduce_scatter | solution.py:254
  942.8 202.5 %reduce-scatter.27.cloned.1.call-start = ((), (), s32[]{:S(2)}) async-start(), calls=%async_computation.23 | async-start | bytes 4718592 | tf_op jit(solution)/shard_map/reduce_scatter | solution.py:252
  952.9 1.2 copy-start.12
  953.0 231.9 %reduce-scatter.25.cloned.1.call-start = ((), (), s32[]{:S(2)}) async-start(), calls=%async_computation.22 | async-start | bytes 1179648 | tf_op jit(solution)/shard_map/reduce_scatter | solution.py:251
  958.6 75.4 %copy-start.16 = (f32[1024]{0:T(1024)S(1)}, f32[1024]{0:T(1024)}, u32[]{:S(2)}) copy-start(f32[1024]{0:T(1024)} %copy-done.15) | copy-start | bytes 12292
  958.6 75.4 %copy-start.18 = (f32[512]{0:T(512)S(1)}, f32[512]{0:T(512)}, u32[]{:S(2)}) copy-start(f32[512]{0:T(512)} %copy-done.17) | copy-start | bytes 6148
  958.7 276.4 %reduce-scatter.23.cloned.1.call-start = ((), (), s32[]{:S(2)}) async-start(), calls=%async_computation.21 | async-start | bytes 3538944 | tf_op jit(solution)/shard_map/reduce_scatter | solution.py:249
  967.4 66.6 %copy-start.2 = (f32[512,1024]{1,0:T(8,128)S(1)}, f32[512,1024]{1,0:T(8,128)}, u32[]{:S(2)}) copy-start(f32[512,1024]{1,0:T(8,128)} %param.22) | copy-start | bytes 6291460
  967.4 68.6 %copy-start.23 = (f32[512]{0:T(512)S(1)}, f32[512]{0:T(512)}, u32[]{:S(2)}) copy-start(f32[512]{0:T(512)} %copy-done.22) | copy-start | bytes 6148
  967.4 68.6 %copy-start.21 = (f32[512]{0:T(512)S(1)}, f32[512]{0:T(512)}, u32[]{:S(2)}) copy-start(f32[512]{0:T(512)} %copy-done.20) | copy-start | bytes 6148
  967.4 70.9 %copy-start.24 = (f32[1024]{0:T(1024)S(1)}, f32[1024]{0:T(1024)}, u32[]{:S(2)}) copy-start(f32[1024]{0:T(1024)} %get-tuple-element.447) | copy-start | bytes 12292
  967.4 70.9 %copy-start.25 = (f32[1024]{0:T(1024)S(1)}, f32[1024]{0:T(1024)}, u32[]{:S(2)}) copy-start(f32[1024]{0:T(1024)} %get-tuple-element.344) | copy-start | bytes 12292
  967.4 70.9 %copy-start.26 = (f32[1024]{0:T(1024)S(1)}, f32[1024]{0:T(1024)}, u32[]{:S(2)}) copy-start(f32[1024]{0:T(1024)} %get-tuple-element.340) | copy-start | bytes 12292
  967.4 70.9 %copy-start.27 = (f32[1024]{0:T(1024)S(1)}, f32[1024]{0:T(1024)}, u32[]{:S(2)}) copy-start(f32[1024]{0:T(1024)} %get-tuple-element.430) | copy-start | bytes 12292
  1034.0 48.2 %copy-start.9 = (bf16[512,1024]{1,0:T(8,128)(2,1)S(1)}, bf16[512,1024]{1,0:T(8,128)(2,1)}, u32[]{:S(2)}) copy-start(bf16[512,1024]{1,0:T(8,128)(2,1)} %reduce-scatter.21.cloned.1.call-done) | copy-start | bytes 3145732
Sparse Core Ops, SparseCore 0:
  9.9 28.4 all-gather.11
  60.7 81.4 all-gather.9
  223.8 75.3 reduce-scatter.14
  301.1 28.7 all-gather.15
  332.0 80.3 all-gather.13
  414.2 27.1 all-gather.17
  443.0 80.3 all-gather.19
  546.8 75.2 reduce-scatter.18
  624.5 77.2 reduce-scatter.16
  709.0 81.2 all-gather.21
  793.6 31.3 reduce-scatter.32
  923.0 31.2 reduce-scatter.30
  956.7 77.2 reduce-scatter.20
  1037.8 51.9 reduce-scatter.28
  1094.0 51.3 reduce-scatter.26
  1149.0 35.8 reduce-scatter.24
  1188.7 46.3 reduce-scatter.22
where the time goes:
time: 1250 us; the launch traced here: 1240 us
  waiting for transfers between devices  764 us (61%)
  matrix products  175 us (14%)
  local copies, waits for them, and re-layouts  113 us (9%)
  blocking collectives  112 us (9%)
  other arithmetic  55.1 us (4%)
  between operations  14.9 us (1%)
    all_gather x1, waiting for transfers between devices, local(): lax.all_gather(normed_two.astype(jnp.bfloat16), 'tensor', axis=0, tiled=T...  82.4 us
    all_gather x1, waiting for transfers between devices, local(): lax.all_gather(cotangent.astype(jnp.bfloat16), 'tensor', axis=0, tiled=True)  82 us
    unnamed x2, blocking collectives  81.5 us
    all_gather x1, waiting for transfers between devices, local(): lax.all_gather(grad_mid.astype(jnp.bfloat16), 'tensor', axis=0, tiled=True)  80.3 us
    reduce_scatter x1, waiting for transfers between devices, local(): lax.psum_scatter(jnp.dot(context, w_out, preferred_element_type=jnp.float...  74.8 us
    reduce_scatter x1, waiting for transfers between devices, local(): lax.psum_scatter(jnp.dot(active, w_down, preferred_element_type=jnp.float...  74.1 us
    reduce_scatter x1, waiting for transfers between devices, local(): lax.psum_scatter(contract_cols(grad_qkv, w_qkv).astype(jnp.bfloat16), 'te...  63.7 us
    reduce_scatter x1, waiting for transfers between devices, local(): lax.psum_scatter(contract_cols(grad_pre, w_up).astype(jnp.bfloat16), 'ten...  62.1 us
  transfers between devices with their start and end apart: 17, of which 14 were waited for; matrix products, arithmetic and copies ran while one was open for 18% of the time, Pallas kernels for 0%

commit v1 on v0

v1 whole, which is shorter than its diff:
```python
import functools

import jax
import jax.numpy as jnp
from jax import lax
from jax.experimental import pallas as pl
from jax.experimental.pallas import tpu as pltpu
from jax.sharding import PartitionSpec as P

H = 16
HD = 64
FF = 4096
SEQ_LEN = 1024
EPSILON = 1e-05
MASKED = -1e30
BF = jnp.bfloat16
F32 = jnp.float32


def gelu_tanh(values):
    inner = 0.7978845608028654 * (values + 0.044715 * values * values * values)
    return 0.5 * values * (1.0 + jnp.tanh(inner))


def dot_nn(left, right):
    return lax.dot_general(left, right, (((1,), (0,)), ((), ())), preferred_element_type=F32)


def dot_tn(left, right):
    return lax.dot_general(left, right, (((0,), (0,)), ((), ())), preferred_element_type=F32)


def dot_nt(left, right):
    return lax.dot_general(left, right, (((1,), (1,)), ((), ())), preferred_element_type=F32)


def swap_bit(values, bit):
    size = lax.axis_size("dp")
    return lax.ppermute(values, "dp", [(i, i ^ (1 << bit)) for i in range(size)])


def swap_core(values):
    return swap_bit(values, 0)


def from_tensor(values, step):
    size = lax.axis_size("tensor")
    return lax.ppermute(values, "tensor", [(i, (i - step) % size) for i in range(size)])


def swap_pair(values):
    dp, tensor = lax.axis_size("dp"), lax.axis_size("tensor")
    pairs = []
    for d in range(dp):
        for t in range(tensor):
            if d % 2 != t % 2:
                pairs.append((d * tensor + t, (d ^ 1) * tensor + (t ^ 1)))
    return lax.ppermute(values, ("dp", "tensor"), pairs)


def chip_bits():
    return (lax.axis_size("dp") // 2).bit_length() - 1


def gather_chips(line, split):
    bits = chip_bits()
    if bits == 2:
        along = swap_bit(line, 1)
        across = swap_bit(line, 2)
        far_top = swap_bit(along[:split], 2)
        far_low = swap_bit(across[split:], 1)
        return [
            [line[:split], line[split:]],
            [along[:split], along[split:]],
            [across[:split], across[split:]],
            [far_top, far_low],
        ]
    held = line[None]
    for bit in range(bits):
        held = jnp.concatenate([held, swap_bit(held, bit + 1)], axis=0)
    return [[held[r, :split], held[r, split:]] for r in range(1 << bits)]


def scatter_chips(grad, rows, split):
    bits = chip_bits()
    if bits == 2:
        block = [grad[r * rows : (r + 1) * rows] for r in range(4)]
        far_top = swap_bit(block[3][:split], 2)
        far_low = swap_bit(block[3][split:], 1)
        top = (block[1][:split].astype(F32) + far_top.astype(F32)).astype(BF)
        low = (block[2][split:].astype(F32) + far_low.astype(F32)).astype(BF)
        along = swap_bit(jnp.concatenate([top, block[1][split:]], axis=0), 1)
        across = swap_bit(jnp.concatenate([block[2][:split], low], axis=0), 2)
        return block[0].astype(F32) + along.astype(F32) + across.astype(F32)
    held = grad.reshape(-1, rows, grad.shape[1])
    for bit in range(bits)[::-1]:
        half = held.shape[0] // 2
        got = swap_bit(held[half:], bit + 1)
        held = (held[:half].astype(F32) + got.astype(F32)).astype(BF)
    return held[0].astype(F32)


def gather_weights(piece, widths, extra=None):
    size = lax.axis_size("tensor")
    rows = piece.shape[0]
    mine = piece if extra is None else jnp.concatenate([piece, extra], axis=0)
    turned = [mine] + [from_tensor(mine, k) for k in range(1, size)]
    cols, at = [], 0
    for width in widths:
        cols += [t[:rows, at : at + width] for t in turned]
        at += width
    line = jnp.concatenate(cols, axis=1)
    if extra is not None:
        added = functools.reduce(jnp.add, [t[rows:] for t in turned])
        added = jnp.pad(added, ((0, 0), (0, line.shape[1] - added.shape[1])))
        line = jnp.concatenate([line, added], axis=0)
    got = gather_chips(line, rows // 2)
    out, at = [], 0
    for width in widths:
        cut = slice(at, at + size * width)
        out.append(jnp.concatenate([part for top, low in got for part in (top[:, cut], low[: rows - rows // 2, cut])]))
        at += size * width
    table = None
    if extra is not None:
        table = jnp.stack([low[rows - rows // 2 :, : extra.shape[1]] for _, low in got])
    return out, table


def scatter_grads(grad, core):
    size = lax.axis_size("tensor")
    rows = grad.shape[0] // (lax.axis_size("dp") // 2)
    width = grad.shape[1] // size
    line = scatter_chips(grad, rows, rows // 2)
    total = line[:, :width]
    for k in range(1, size):
        part = line[:, k * width : (k + 1) * width].astype(BF)
        total = total + from_tensor(part, size - k).astype(F32)
    half = rows // 2
    keep = lax.dynamic_slice_in_dim(total, core * half, half, 0)
    give = lax.dynamic_slice_in_dim(total, (1 - core) * half, half, 0)
    got = swap_core(give)
    return jnp.where(core == 0, jnp.stack([keep, got], 1), jnp.stack([got, keep], 1))


def both_halves(mine, other, core):
    return jnp.concatenate([jnp.where(core == 0, mine, other), jnp.where(core == 0, other, mine)], axis=0)


def to_sequence(mine, core, keeps):
    here = jnp.where(keeps, mine, swap_pair(mine))
    return both_halves(here, swap_core(here), core)


def from_sequence(left, weight, core):
    half = left.shape[0] // 2
    give = lax.dynamic_slice_in_dim(left, (1 - core) * half, half, 0)
    got = swap_core(dot_nt(give, weight).astype(BF))
    own = dot_nt(lax.dynamic_slice_in_dim(left, core * half, half, 0), weight)
    here = (own + got.astype(F32)).astype(BF)
    return here, swap_pair(here)


BLOCK_Q = 256


def biased_pair(q, k, slope_ref, group, head):
    seq = k.shape[0]
    lane = lax.broadcasted_iota(jnp.int32, (1, 2 * HD), 1)
    mine = (lane >= head * HD) & (lane < (head + 1) * HD)
    slot = lane & (HD - 1)
    bias = slope_ref[group, head] * lax.broadcasted_iota(jnp.int32, (seq, 2 * HD), 0).astype(F32)
    high = bias.astype(BF)
    rest = bias - high.astype(F32)
    middle = rest.astype(BF)
    low = (rest - middle.astype(F32)).astype(BF)
    zero = jnp.zeros_like(k)
    extra = jnp.where(slot == 0, high, jnp.where(slot == 1, middle, jnp.where(slot == 2, low, zero)))
    ones = jnp.where(slot < 3, 1.0, 0.0).astype(BF)
    return jnp.where(mine, q, jnp.broadcast_to(ones, q.shape)), jnp.where(mine, k, extra), mine


def below_diagonal(size):
    keys = lax.broadcasted_iota(jnp.int32, (size, size), 0)
    return keys <= lax.broadcasted_iota(jnp.int32, (size, size), 1)


def attend_kernel(slope_ref, qkv_ref, ctx_ref, lse_ref):
    group = pl.program_id(0)
    wide = 2 * HD
    seq = qkv_ref.shape[0]
    size = min(BLOCK_Q, seq)
    q = qkv_ref[:, :wide] * BF(HD**-0.5)
    k = qkv_ref[:, wide : 2 * wide]
    v_t = qkv_ref[:, 2 * wide :].T
    heads = [biased_pair(q, k, slope_ref, group, h) for h in range(2)]
    seen = below_diagonal(size)
    for i in range(seq // size):
        lo, hi = i * size, (i + 1) * size
        outs = []
        for h, (qh, kh, _) in enumerate(heads):
            s = dot_nt(kh[:hi], qh[lo:hi])
            last = jnp.where(seen, s[lo:], MASKED)
            top = jnp.max(last, axis=0, keepdims=True)
            if i:
                top = jnp.maximum(top, jnp.max(s[:lo], axis=0, keepdims=True))
            e = jnp.exp(last - top)
            total = jnp.sum(e, axis=0, keepdims=True)
            e = e.astype(BF)
            if i:
                e0 = jnp.exp(s[:lo] - top)
                total = total + jnp.sum(e0, axis=0, keepdims=True)
                e = jnp.concatenate([e0.astype(BF), e], axis=0)
            o_t = dot_nn(v_t[h * HD : (h + 1) * HD, :hi], e)
            outs.append(o_t * (1.0 / total))
            lse_ref[0, h : h + 1, lo:hi] = top + jnp.log(total)
        ctx_ref[lo:hi, :] = jnp.concatenate(outs, axis=0).T.astype(BF)


def attend(qkv, slopes):
    seq, groups = qkv.shape[0], slopes.shape[0]
    wide = 2 * HD
    return pl.pallas_call(
        attend_kernel,
        grid=(groups,),
        in_specs=[
            pl.BlockSpec(memory_space=pltpu.SMEM),
            pl.BlockSpec((seq, 3 * wide), lambda g: (0, g)),
        ],
        out_specs=[
            pl.BlockSpec((seq, wide), lambda g: (0, g)),
            pl.BlockSpec((1, 2, seq), lambda g: (g, 0, 0)),
        ],
        out_shape=[
            jax.ShapeDtypeStruct((seq, groups * wide), BF),
            jax.ShapeDtypeStruct((groups, 2, seq), F32),
        ],
        compiler_params=pltpu.CompilerParams(vmem_limit_bytes=48 * 1024 * 1024),
        cost_estimate=pl.CostEstimate(
            flops=groups * 2 * seq * seq * HD * 4, bytes_accessed=qkv.size * 2 * 2, transcendentals=groups * seq * seq
        ),
        name="attend",
    )(slopes, qkv)


def attend_back_kernel(slope_ref, qkv_ref, grad_ref, lse_ref, out_ref, bias_ref, dk_ref, dv_ref):
    group = pl.program_id(0)
    wide = 2 * HD
    seq = qkv_ref.shape[0]
    size = min(BLOCK_Q, seq)
    q = qkv_ref[:, :wide] * BF(HD**-0.5)
    k = qkv_ref[:, wide : 2 * wide]
    v = qkv_ref[:, 2 * wide :]
    k_t = k.T
    zero = jnp.zeros_like(q)
    heads = [biased_pair(q, k, slope_ref, group, h) for h in range(2)]
    clean = [jnp.where(mine, q, zero) for _, _, mine in heads]
    grads = [jnp.where(mine, grad_ref[...], zero) for _, _, mine in heads]
    seen = below_diagonal(size)
    dk_ref[...] = jnp.zeros_like(dk_ref)
    dv_ref[...] = jnp.zeros_like(dv_ref)
    bias_q = jnp.zeros((1, wide), F32)
    for i in range(seq // size):
        lo, hi = i * size, (i + 1) * size
        outs = []
        for h, (qh, kh, _) in enumerate(heads):
            s = dot_nt(kh[:hi], qh[lo:hi])
            lse = lse_ref[0, h : h + 1, lo:hi]
            p = jnp.exp(jnp.where(seen, s[lo:], MASKED) - lse)
            if i:
                p = jnp.concatenate([jnp.exp(s[:lo] - lse), p], axis=0)
            dp = dot_nt(v[:hi], grads[h][lo:hi])
            inner = jnp.sum(p * dp, axis=0, keepdims=True)
            ds = (p * (dp - inner)).astype(BF)
            dk_ref[:hi, :] += dot_nn(ds, clean[h][lo:hi])
            dv_ref[:hi, :] += dot_nn(p.astype(BF), grads[h][lo:hi])
            outs.append(dot_nn(k_t[h * HD : (h + 1) * HD, :hi], ds))
        dq = (jnp.concatenate(outs, axis=0).T * HD**-0.5).astype(BF)
        bias_q = bias_q + jnp.sum(dq.astype(F32), axis=0, keepdims=True)
        out_ref[lo:hi, :wide] = dq
    dk = dk_ref[...].astype(BF)
    out_ref[:, wide : 2 * wide] = dk
    dv = dv_ref[...].astype(BF)
    out_ref[:, 2 * wide :] = dv
    bias_ref[0, :, :wide] = bias_q
    bias_ref[0, :, wide : 2 * wide] = jnp.sum(dk.astype(F32), axis=0, keepdims=True)
    bias_ref[0, :, 2 * wide :] = jnp.sum(dv.astype(F32), axis=0, keepdims=True)


def attend_back(qkv, slopes, lse, grad_ctx):
    seq, groups = qkv.shape[0], slopes.shape[0]
    wide = 2 * HD
    return pl.pallas_call(
        attend_back_kernel,
        grid=(groups,),
        in_specs=[
            pl.BlockSpec(memory_space=pltpu.SMEM),
            pl.BlockSpec((seq, 3 * wide), lambda g: (0, g)),
            pl.BlockSpec((seq, wide), lambda g: (0, g)),
            pl.BlockSpec((1, 2, seq), lambda g: (g, 0, 0)),
        ],
        out_specs=[
            pl.BlockSpec((seq, 3 * wide), lambda g: (0, g)),
            pl.BlockSpec((1, 1, 3 * wide), lambda g: (g, 0, 0)),
        ],
        out_shape=[
            jax.ShapeDtypeStruct(qkv.shape, BF),
            jax.ShapeDtypeStruct((groups, 1, 3 * wide), F32),
        ],
        scratch_shapes=[pltpu.VMEM((seq, wide), F32), pltpu.VMEM((seq, wide), F32)],
        compiler_params=pltpu.CompilerParams(vmem_limit_bytes=48 * 1024 * 1024),
        cost_estimate=pl.CostEstimate(
            flops=groups * 2 * seq * seq * HD * 10, bytes_accessed=qkv.size * 2 * 3, transcendentals=groups * seq * seq
        ),
        name="attend_back",
    )(slopes, qkv, grad_ctx, lse)


VMEM_LIMIT = 48 * 1024 * 1024


def read_mixed(ref, ids_ref, chips, mixed):
    if not mixed:
        return ref[...]
    block = ref.shape[1] // chips
    parts = [ref[:, pl.ds(pl.multiple_of((ids_ref[0] ^ r) * block, block), block)] for r in range(chips)]
    return jnp.concatenate(parts, axis=1)


def write_mixed(ref, values, ids_ref, chips, mixed):
    if not mixed:
        ref[...] = values
        return
    block = ref.shape[1] // chips
    for r in range(chips):
        ref[:, pl.ds(pl.multiple_of((ids_ref[0] ^ r) * block, block), block)] = values[:, r * block : (r + 1) * block]


def centre(x):
    mean_row = jnp.mean(x, axis=1, keepdims=True)
    centred = x - mean_row
    inv = lax.rsqrt(jnp.mean(centred * centred, axis=1, keepdims=True) + EPSILON)
    return centred * inv, inv


def norm_back(grad, gain, z, inv):
    g = grad * gain
    mean_g = jnp.mean(g, axis=1, keepdims=True)
    mean_gz = jnp.mean(g * z, axis=1, keepdims=True)
    return inv * (g - mean_g - z * mean_gz)


def add_sums(ref, rows):
    @pl.when(pl.program_id(0) == 0)
    def _():
        ref[...] = jnp.zeros_like(ref)

    for i, row in enumerate(rows):
        ref[i : i + 1, :] += jnp.sum(row, axis=0, keepdims=True)


def row_call(body, name, ids, rows, wholes, outs, sums):
    tokens, width = rows[0].shape
    step = min(128, tokens)
    tile = pl.BlockSpec((step, width), lambda i: (i, 0))
    one = pl.BlockSpec((8, width), lambda i: (0, 0))
    shapes = [jax.ShapeDtypeStruct((tokens, width), t) for t in outs]
    if sums:
        shapes.append(jax.ShapeDtypeStruct((8, width), F32))
    moved = sum(r.size * r.dtype.itemsize for r in rows) + sum(tokens * width * jnp.dtype(t).itemsize for t in outs)
    return pl.pallas_call(
        body,
        grid=(tokens // step,),
        in_specs=[pl.BlockSpec(memory_space=pltpu.SMEM)] + [tile] * len(rows) + [one] * len(wholes),
        out_specs=[tile] * len(outs) + ([one] if sums else []),
        out_shape=shapes,
        compiler_params=pltpu.CompilerParams(vmem_limit_bytes=VMEM_LIMIT),
        cost_estimate=pl.CostEstimate(flops=tokens * width * 10, bytes_accessed=moved, transcendentals=0),
        name=name,
    )(ids, *rows, *wholes)


def rows_first(chips, mixed, ids, hidden):
    def body(ids_ref, x_ref, z_ref):
        z_ref[...] = centre(read_mixed(x_ref, ids_ref, chips, mixed))[0].astype(BF)

    return row_call(body, "rows_first", ids, [hidden], [], [BF], False)[0]


def rows_cot(chips, mixed, ids, cot):
    def body(ids_ref, x_ref, low_ref, sum_ref):
        x = read_mixed(x_ref, ids_ref, chips, mixed)
        low_ref[...] = x.astype(BF)
        add_sums(sum_ref, [x])

    return row_call(body, "rows_cot", ids, [cot], [], [BF], True)


def rows_mid(chips, mixed, ids, hidden, here, swapped, vec):
    def body(ids_ref, x_ref, here_ref, swapped_ref, vec_ref, res_ref, norm_ref):
        added = jnp.where(ids_ref[3] == 1, here_ref[...].astype(F32), swapped_ref[...].astype(F32))
        res = read_mixed(x_ref, ids_ref, chips, mixed) + added + vec_ref[2:3, :]
        res_ref[...] = res
        norm_ref[...] = (centre(res)[0] * vec_ref[3:4, :] + vec_ref[4:5, :]).astype(BF)

    return row_call(body, "rows_mid", ids, [hidden, here, swapped], [vec], [F32, BF], False)


def rows_out(chips, mixed, ids, residual, own, got, vec):
    def body(ids_ref, res_ref, own_ref, got_ref, vec_ref, out_ref):
        out = res_ref[...] + (own_ref[...] + got_ref[...].astype(F32)) + vec_ref[5:6, :]
        write_mixed(out_ref, out, ids_ref, chips, mixed)

    return row_call(body, "rows_out", ids, [residual, own, got], [vec], [F32], False)[0]


def rows_mid_back(chips, mixed, ids, cot, residual, own, got, vec):
    def body(ids_ref, cot_ref, res_ref, own_ref, got_ref, vec_ref, grad_ref, low_ref, sum_ref):
        z, inv = centre(res_ref[...])
        grad = own_ref[...] + got_ref[...].astype(F32)
        mid = read_mixed(cot_ref, ids_ref, chips, mixed) + norm_back(grad, vec_ref[3:4, :], z, inv)
        grad_ref[...] = mid
        low_ref[...] = mid.astype(BF)
        add_sums(sum_ref, [grad * z, grad, mid])

    return row_call(body, "rows_mid_back", ids, [cot, residual, own, got], [vec], [F32, BF], True)


def rows_first_back(chips, mixed, ids, hidden, grad_mid, here, swapped, vec):
    def body(ids_ref, x_ref, mid_ref, here_ref, swapped_ref, vec_ref, out_ref):
        z, inv = centre(read_mixed(x_ref, ids_ref, chips, mixed))
        grad = jnp.where(ids_ref[3] == 1, here_ref[...].astype(F32), swapped_ref[...].astype(F32))
        out = mid_ref[...] + norm_back(grad, vec_ref[0:1, :], z, inv)
        write_mixed(out_ref, out, ids_ref, chips, mixed)

    return row_call(body, "rows_first_back", ids, [hidden, grad_mid, here, swapped], [vec], [F32], False)[0]


class Plan:
    def __init__(self, dp, size, small, d_model, heads, qb, ups, ub):
        self.dp, self.size, self.small, self.d_model = dp, size, small, d_model
        self.heads, self.qb, self.ups, self.ub = heads, qb, ups, ub
        self.chips = dp // 2
        self.pair = heads // 2
        self.n_q = size * 3 * self.pair * HD
        self.n_u = size * (ups // 2) * ub * dp
        self.used = 6 * small + heads * qb + ups * ub

    def vector(self, which, n):
        owner = n // self.small
        t = owner % self.size
        c = (owner // self.size) % 2
        r = owner // (2 * self.size)
        return r, c, t, which * self.small + n % self.small

    def query(self, n, chip, core, tensor):
        per = 3 * self.pair * HD
        part = (n % per) // (self.pair * HD)
        head = (n % (self.pair * HD)) // HD
        b = n % HD + jnp.where(part == 2, HD, 0)
        d = b // self.qb
        place = 6 * self.small + (core * self.pair + head) * self.qb + b % self.qb
        place = jnp.where(part == 1, -1, place)
        return chip ^ (d // 2), d % 2, (tensor + n // per) % self.size, place

    def up(self, n, chip, core, tensor):
        row_len = self.ub * self.dp
        per = (self.ups // 2) * row_len
        row = (n % per) // row_len
        d = (n % row_len) // self.ub
        place = 6 * self.small + self.heads * self.qb + (core * (self.ups // 2) + row) * self.ub + n % self.ub
        return chip ^ (d // 2), d % 2, (tensor + n // per) % self.size, place


def spread_small(plan, ids, table):
    count, pack = table.shape

    def body(ids_ref, table_ref, vec_ref, bq_ref, bu_ref):
        chip, core, tensor = ids_ref[0], ids_ref[1], ids_ref[2]

        def pick(where_, n):
            col = lax.broadcasted_iota(jnp.int32, (1, n), 1)
            r, c, t, place = where_(col)
            hot = lax.broadcasted_iota(jnp.int32, (pack, n), 0) == place
            got = dot_nn(table_ref[...], jnp.where(hot, 1.0, 0.0).astype(BF))
            row = (r * 2 + c) * plan.size + t
            return jnp.sum(
                jnp.where(lax.broadcasted_iota(jnp.int32, (count, n), 0) == row, got, 0.0), axis=0, keepdims=True
            )

        for v in range(6):
            vec_ref[v : v + 1, :] = pick(functools.partial(plan.vector, v), plan.d_model)
        vec_ref[6:8, :] = jnp.zeros((2, plan.d_model), F32)
        bq_ref[...] = pick(lambda n: plan.query(n, chip, core, tensor), plan.n_q)
        bu_ref[...] = pick(lambda n: plan.up(n, chip, core, tensor), plan.n_u)

    return pl.pallas_call(
        body,
        in_specs=[pl.BlockSpec(memory_space=pltpu.SMEM), pl.BlockSpec(memory_space=pltpu.VMEM)],
        out_shape=[
            jax.ShapeDtypeStruct((8, plan.d_model), F32),
            jax.ShapeDtypeStruct((1, plan.n_q), F32),
            jax.ShapeDtypeStruct((1, plan.n_u), F32),
        ],
        compiler_params=pltpu.CompilerParams(vmem_limit_bytes=VMEM_LIMIT),
        cost_estimate=pl.CostEstimate(flops=10**8, bytes_accessed=10**5, transcendentals=0),
        name="spread_small",
    )(ids, table)


def pack_small(plan, ids, mid_sums, cot_sums, bias_q, bias_u):
    size = plan.size
    width = plan.d_model
    per_q, per_u = plan.n_q // size, plan.n_u // size

    def body(ids_ref, mid_ref, cot_ref, bq_ref, bu_ref, out_ref):
        core, tensor = ids_ref[1], ids_ref[2]
        out_ref[...] = jnp.zeros_like(out_ref)
        out_ref[0:2, :] = mid_ref[3:5, :]
        out_ref[2:3, :] = mid_ref[2:3, :]
        out_ref[3:5, :] = mid_ref[0:2, :]
        out_ref[5:6, :] = cot_ref[0:1, :]
        at = 8
        for ref, per in ((bq_ref, per_q), (bu_ref, per_u)):
            x = ref[...]
            turned = x
            for t in range(1, size):
                moved = jnp.concatenate([x[:, (size - t) * per :], x[:, : (size - t) * per]], axis=1)
                turned = jnp.where(tensor == t, moved, turned)
            for c in range(2):
                put = jnp.where(core == c, turned, 0.0)
                for lo in range(0, put.shape[1], width):
                    part = put[:, lo : lo + width]
                    out_ref[at : at + 1, : part.shape[1]] = part
                    at += 1

    lines = 8 + 2 * (-(-plan.n_q // width) - (-plan.n_u // width))
    return pl.pallas_call(
        body,
        in_specs=[pl.BlockSpec(memory_space=pltpu.SMEM)] + [pl.BlockSpec(memory_space=pltpu.VMEM)] * 4,
        out_shape=jax.ShapeDtypeStruct((-(-lines // 8) * 8, width), F32),
        compiler_params=pltpu.CompilerParams(vmem_limit_bytes=VMEM_LIMIT),
        cost_estimate=pl.CostEstimate(flops=10**6, bytes_accessed=10**5, transcendentals=0),
        name="pack_small",
    )(ids, mid_sums, cot_sums, bias_q, bias_u)


def own_small(plan, total, index, tensor):
    size, width = plan.size, plan.d_model
    n_q, n_u = -(-plan.n_q // width), -(-plan.n_u // width)
    vectors = lax.dynamic_slice_in_dim(total[:6], (index % 2 * size + tensor) * plan.small, plan.small, 1)
    q = total[8 : 8 + 2 * n_q].reshape(2, -1)[:, : plan.n_q].reshape(2, size, 3, plan.pair, HD)
    q = lax.dynamic_index_in_dim(q, tensor, 1, keepdims=False)
    q = jnp.stack([q[:, 0], q[:, 2]], axis=2).reshape(plan.heads, 2 * HD)
    q = lax.dynamic_slice_in_dim(q, index * plan.qb, plan.qb, 1)
    u = total[8 + 2 * n_q : 8 + 2 * (n_q + n_u)].reshape(2, -1)[:, : plan.n_u].reshape(2, size, plan.ups // 2, -1)
    u = lax.dynamic_index_in_dim(u, tensor, 1, keepdims=False).reshape(plan.ups, -1)
    u = lax.dynamic_slice_in_dim(u, index * plan.ub, plan.ub, 1)
    return [vectors[i] for i in range(6)], q, u


def qkv_grads(seq_one, grad_qkv, w_qkv, colsum, vec_t):
    seq, d_model = seq_one.shape
    width = grad_qkv.shape[1]
    step = min(256, d_model)

    def body(z_ref, grad_ref, w_ref, col_ref, vec_ref, out_ref, sum_ref):
        g = lax.dot_general(z_ref[...], grad_ref[...], (((0,), (0,)), ((), ())), preferred_element_type=F32)
        w = w_ref[...].astype(F32)
        col = col_ref[...]
        out_ref[...] = (g * vec_ref[:, 0:1] + vec_ref[:, 1:2] * col).astype(BF)
        gain = jnp.sum(g * w, axis=1, keepdims=True)
        shift = jnp.sum(w * col, axis=1, keepdims=True)
        lane = lax.broadcasted_iota(jnp.int32, (step, 128), 1)
        sum_ref[...] = jnp.where(lane == 0, gain, jnp.where(lane == 1, shift, 0.0)).T[:8]

    return pl.pallas_call(
        body,
        grid=(d_model // step,),
        in_specs=[
            pl.BlockSpec((seq, step), lambda i: (0, i)),
            pl.BlockSpec((seq, width), lambda i: (0, 0)),
            pl.BlockSpec((step, width), lambda i: (i, 0)),
            pl.BlockSpec((1, width), lambda i: (0, 0)),
            pl.BlockSpec((step, 128), lambda i: (i, 0)),
        ],
        out_specs=[pl.BlockSpec((step, width), lambda i: (i, 0)), pl.BlockSpec((8, step), lambda i: (0, i))],
        out_shape=[jax.ShapeDtypeStruct((d_model, width), BF), jax.ShapeDtypeStruct((8, d_model), F32)],
        compiler_params=pltpu.CompilerParams(vmem_limit_bytes=VMEM_LIMIT),
        cost_estimate=pl.CostEstimate(
            flops=2 * seq * d_model * width, bytes_accessed=2 * (seq + 2 * d_model) * width, transcendentals=0
        ),
        name="qkv_grads",
    )(seq_one, grad_qkv, w_qkv, colsum, vec_t)


def split_weights(ids, w_qkv, w_out, w_up, w_down):
    rows = w_qkv.shape[0]
    n_q, n_o, n_u = w_qkv.shape[1] // 2, w_out.shape[0] // 2, w_up.shape[1] // 2
    pair = n_q // (3 * HD)
    width = n_q + n_o + 2 * n_u

    def body(ids_ref, q_ref, o_ref, u_ref, d_ref, mine_ref, give_ref):
        core = ids_ref[1]
        for half, ref in ((core, mine_ref), (1 - core, give_ref)):
            x = q_ref[:, pl.ds(pl.multiple_of(half * n_q, n_q), n_q)]
            parts = [
                x[:, (h * 3 + p) * HD : (h * 3 + p + 1) * HD] for p in range(3) for h in range(pair)
            ]
            ref[:, :n_q] = jnp.concatenate(parts, axis=1)
            ref[:, n_q : n_q + n_o] = o_ref[pl.ds(pl.multiple_of(half * n_o, n_o), n_o), :].T
            ref[:, n_q + n_o : n_q + n_o + n_u] = u_ref[:, pl.ds(pl.multiple_of(half * n_u, n_u), n_u)]
            ref[:, n_q + n_o + n_u :] = d_ref[pl.ds(pl.multiple_of(half * n_u, n_u), n_u), :].T

    return pl.pallas_call(
        body,
        in_specs=[pl.BlockSpec(memory_space=pltpu.SMEM)] + [pl.BlockSpec(memory_space=pltpu.VMEM)] * 4,
        out_shape=[jax.ShapeDtypeStruct((rows, width), BF)] * 2,
        compiler_params=pltpu.CompilerParams(vmem_limit_bytes=VMEM_LIMIT),
        cost_estimate=pl.CostEstimate(flops=0, bytes_accessed=rows * width * 8, transcendentals=0),
        name="split_weights",
    )(ids, w_qkv, w_out, w_up, w_down)


def swap_blocks(values, bit, block):
    count = values.shape[1] // block
    return jnp.concatenate([values[:, (r ^ (1 << bit)) * block : ((r ^ (1 << bit)) + 1) * block] for r in range(count)], axis=1)


def local(
    hidden_in,
    ln1_gain,
    ln1_bias,
    qkv_weight,
    qkv_bias,
    out_weight,
    out_bias,
    ln2_gain,
    ln2_bias,
    up_weight,
    up_bias,
    down_weight,
    down_bias,
    cotangent,
):
    dp = lax.axis_size("dp")
    size = lax.axis_size("tensor")
    index = lax.axis_index("dp")
    core = index % 2
    chip = index // 2
    tensor = lax.axis_index("tensor")
    keeps = core == tensor % 2
    chips = dp // 2
    tokens, d_model = hidden_in.shape
    block = d_model // chips
    heads_here = qkv_weight.shape[1] // (3 * HD)
    pair = heads_here // 2
    rows = qkv_weight.shape[0]
    mixed = block % 128 == 0
    ids = jnp.stack([chip, core, tensor, keeps.astype(jnp.int32)]).astype(jnp.int32)
    small = ln1_gain.shape[0]
    plan = Plan(dp, size, small, d_model, heads_here, qkv_bias.shape[1], up_bias.shape[0], up_bias.shape[1])

    def relative(values):
        if mixed:
            return values
        return jnp.concatenate(
            [lax.dynamic_slice_in_dim(values, (chip ^ r) * block, block, 1) for r in range(chips)], axis=1
        )

    wide = [qkv_weight.shape[1] // 2, out_weight.shape[0] // 2, up_weight.shape[1] // 2, down_weight.shape[0] // 2]
    packed = jnp.concatenate(
        [v.reshape(-1) for v in (ln1_gain, ln1_bias, out_bias, ln2_gain, ln2_bias, down_bias, qkv_bias, up_bias)]
    )
    pack = wide[0]
    packed = jnp.pad(packed, (0, pack - packed.shape[0])).reshape(1, pack)
    if mixed:
        own, give = split_weights(ids, qkv_weight, out_weight, up_weight, down_weight)
    else:
        w_q = qkv_weight.reshape(rows, 2, pair, 3, HD).transpose(0, 1, 3, 2, 4).reshape(rows, 2, 3 * pair * HD)
        parts = [w_q] + [w.reshape(rows, 2, -1) for w in (out_weight.T, up_weight, down_weight.T)]
        loc = jnp.concatenate(parts, axis=2).transpose(1, 0, 2)
        own = lax.dynamic_index_in_dim(loc, core, 0, keepdims=False)
        give = lax.dynamic_index_in_dim(loc, 1 - core, 0, keepdims=False)
    other_pack = swap_core(packed)
    piece = both_halves(own, swap_core(give), core)
    slot = jnp.arange(16)[:, None]
    extra = jnp.where(slot == core * size + tensor, packed, jnp.zeros_like(packed))
    extra = jnp.where(slot == (1 - core) * size + tensor, other_pack, extra)

    hidden = relative(hidden_in)
    z_one = rows_first(chips, mixed, ids, hidden)
    seq_one = to_sequence(z_one, core, keeps)
    (w_qkv,), table = gather_weights(piece[:, : wide[0]], wide[:1], extra)
    table = table.reshape(chips, 16, pack)[:, : 2 * size].reshape(chips * 2 * size, pack)
    vec, b_qkv, b_up = spread_small(plan, ids, table)
    (w_out_t, w_up), _ = gather_weights(piece[:, wide[0] : wide[0] + wide[1] + wide[2]], wide[1:3])
    (w_down_t,), _ = gather_weights(piece[:, wide[0] + wide[1] + wide[2] :], wide[3:])
    cot = relative(cotangent)
    cot_low, cot_sums = rows_cot(chips, mixed, ids, cot)
    cot_rows = jnp.concatenate([cot_low, swap_core(cot_low)], axis=0)

    head_ids = ((tensor + jnp.arange(size)) % size)[:, None] * heads_here + core * pair + jnp.arange(pair)[None]
    slopes = jnp.exp2(-8.0 * (head_ids + 1).astype(F32) / H)

    rows_one = (seq_one.astype(F32) * vec[0:1] + vec[1:2]).astype(BF)
    qkv = (dot_nn(rows_one, w_qkv) + b_qkv).astype(BF)
    context, lse = attend(qkv, slopes)
    here, swapped = from_sequence(context, w_out_t, core)
    residual, norm_two = rows_mid(chips, mixed, ids, hidden, here, swapped, vec)

    rows_two = jnp.concatenate([norm_two, swap_core(norm_two)], axis=0)
    up_pre = dot_nn(rows_two, w_up) + b_up
    active = gelu_tanh(up_pre).astype(BF)
    got_down = swap_core(dot_nt(active[tokens:], w_down_t).astype(BF))
    own_down = dot_nt(active[:tokens], w_down_t)
    output = rows_out(chips, mixed, ids, residual, own_down, got_down, vec)

    grad_active = dot_nn(cot_rows, w_down_t)
    _, gelu_back = jax.vjp(gelu_tanh, up_pre)
    grad_pre = gelu_back(grad_active)[0].astype(BF)
    got_two = swap_core(dot_nt(grad_pre[tokens:], w_up).astype(BF))
    own_two = dot_nt(grad_pre[:tokens], w_up)
    g_down_t = dot_tn(cot_rows, active).astype(BF)
    sum_down = scatter_grads(g_down_t, core)
    g_up = dot_tn(rows_two, grad_pre).astype(BF)
    sum_up = scatter_grads(g_up, core)
    grad_b_up = jnp.sum(grad_pre.astype(F32), axis=0, keepdims=True)
    grad_mid, mid_low, mid_sums = rows_mid_back(chips, mixed, ids, cot, residual, own_two, got_two, vec)

    mid_rows = to_sequence(mid_low, core, keeps)
    grad_context = dot_nn(mid_rows, w_out_t).astype(BF)
    g_out_t = dot_tn(mid_rows, context).astype(BF)
    grad_qkv, grad_b_qkv = attend_back(qkv, slopes, lse, grad_context)
    grad_b_qkv = grad_b_qkv.reshape(1, -1)
    vec_t = jnp.pad(vec[:8].T, ((0, 0), (0, 120)))
    g_qkv, one_sums = qkv_grads(seq_one, grad_qkv, w_qkv, grad_b_qkv, vec_t)
    sum_out = scatter_grads(g_out_t, core)
    sum_qkv = scatter_grads(g_qkv, core)
    here, swapped = from_sequence(grad_qkv, w_qkv, core)
    grad_in = rows_first_back(chips, mixed, ids, hidden, grad_mid, here, swapped, vec)

    mid_sums = jnp.concatenate([mid_sums[:3], one_sums[:2], mid_sums[5:]], axis=0)
    total = pack_small(plan, ids, mid_sums, cot_sums, grad_b_qkv, grad_b_up)
    total = total + swap_core(total)
    for bit in range(chip_bits()):
        got = swap_bit(total, bit + 1)
        total = total + jnp.concatenate([swap_blocks(got[:8], bit, block), got[8:]], axis=0)
    for bit in range((size - 1).bit_length()):
        total = total + lax.ppermute(total, "tensor", [(i, i ^ (1 << bit)) for i in range(size)])
    vector_sums, sum_b_qkv, sum_b_up = own_small(plan, total, index, tensor)

    sum_w_qkv = sum_qkv.reshape(rows, 2, 3, pair, HD).transpose(0, 1, 3, 2, 4).reshape(rows, -1)
    return (
        relative(output),
        relative(grad_in),
        vector_sums[0],
        vector_sums[1],
        sum_w_qkv,
        sum_b_qkv,
        sum_out.reshape(rows, -1).T,
        vector_sums[2],
        vector_sums[3],
        vector_sums[4],
        sum_up.reshape(rows, -1),
        sum_b_up,
        sum_down.reshape(rows, -1).T,
        vector_sums[5],
    )


def solution(mesh):
    both = P(("dp", "tensor"))
    wide = P(("dp", "tensor"), None)
    split, turned = P("dp", "tensor"), P("tensor", "dp")
    return jax.shard_map(
        local,
        mesh=mesh,
        in_specs=(wide, both, both, split, turned, turned, both, both, both, split, turned, turned, both, wide),
        out_specs=(wide, wide, both, both, split, turned, turned, both, both, both, split, turned, turned, both),
        check_vma=False,
    )
```

time: 1250 us -> 504 us (0.40)
  waiting for transfers between devices: 764 us -> 190 us
  blocking collectives: 112 us -> 0 us
  matrix products: 175 us -> 64.4 us
  starting transfers between devices: 2.03 us -> 94.3 us
  Pallas kernels: 0 us -> 67.9 us
  local copies, waits for them, and re-layouts: 113 us -> 54.1 us
  other arithmetic: 55.1 us -> 26.4 us
  between operations: 14.9 us -> 2.22 us
    reduce_scatter x8 -> x0, waiting for transfers between devices: 424 us -> none  [the longest x1 74.8 us: local(): lax.psum_scatter(jnp.dot(context, w_out, preferred_element_type=jnp.float...]
    all_gather x7 -> x0, waiting for transfers between devices: 338 us -> none  [the longest x1 82.4 us: local(): lax.all_gather(normed_two.astype(jnp.bfloat16), 'tensor', axis=0, tiled=T...]
    ppermute x0 -> x72, waiting for transfers between devices: none -> 190 us  [the longest x45 95.5 us: swap_bit(): return lax.ppermute(values, 'dp', [(i, i ^ 1 << bit) for i in range(size)])]
    dot_general x40 -> x15, matrix products: 175 us -> 64.4 us  [the longest x4 29.1 us: dot_nn(): lax.dot_general(left, right, (((1,), (0,)), ((), ())), preferred_element_...]
    ppermute x0 -> x72, starting transfers between devices: none -> 94.3 us  [the longest x45 41 us: swap_bit(): return lax.ppermute(values, 'dp', [(i, i ^ 1 << bit) for i in range(size)])]
    unnamed x2 -> x0, blocking collectives: 81.5 us -> none
    pallas_call x0 -> x12, Pallas kernels: none -> 67.9 us  [the longest x1 21.7 us: attend_back(): pl.pallas_call(attend_back_kernel, grid=(groups,), in_specs=[pl.BlockSpec...]
    dynamic_update_slice x12 -> x0, local copies, waits for them, and re-layouts: 43.5 us -> none  [the longest x8 40.8 us: forward_sequence(): attended, log_sums = lax.map(forward_block, jnp.arange(block_count))]
  transfers between devices with their start and end apart: 17 -> 72, of which waited for: 14 -> 28; matrix products, arithmetic and copies ran while one was open for 18% -> 17% of each run, Pallas kernels for 0% -> 7%
where the time goes in v1:
time: 504 us; the launch traced here: 499 us
  waiting for transfers between devices  190 us (38%)
  starting transfers between devices  94.3 us (19%)
  Pallas kernels  67.9 us (13%)
  matrix products  64.4 us (13%)
  local copies, waits for them, and re-layouts  54.1 us (11%)
  other arithmetic  26.4 us (5%)
    ppermute x45, waiting for transfers between devices, swap_bit(): return lax.ppermute(values, 'dp', [(i, i ^ 1 << bit) for i in range(size)])  95.5 us
    ppermute x21, waiting for transfers between devices, from_tensor(): lax.ppermute(values, 'tensor', [(i, (i - step) % size) for i in range(siz...  81.7 us
    ppermute x45, starting transfers between devices, swap_bit(): return lax.ppermute(values, 'dp', [(i, i ^ 1 << bit) for i in range(size)])  41 us
    ppermute x21, starting transfers between devices, from_tensor(): lax.ppermute(values, 'tensor', [(i, (i - step) % size) for i in range(siz...  30.7 us
    dot_general x4, matrix products, dot_nn(): lax.dot_general(left, right, (((1,), (0,)), ((), ())), preferred_element_...  29.1 us
    unnamed x113, local copies, waits for them, and re-layouts  27.4 us
    dot_general x8, matrix products, dot_nt(): lax.dot_general(left, right, (((1,), (1,)), ((), ())), preferred_element_...  22.5 us
    ppermute x4, starting transfers between devices, swap_pair(): return lax.ppermute(values, ('dp', 'tensor'), pairs)  21.9 us
  transfers between devices with their start and end apart: 72, of which 28 were waited for; matrix products, arithmetic and copies ran while one was open for 17% of the time, Pallas kernels for 7%

profile of v1, /device:TPU:1, one launch (start us, length us, event | category | flops | bytes accessed | tf_op | source)
XLA Modules:
  0.0 499.3 jit_solution(3188946737923321981)
XLA Ops:
  7.5 4.1 concatenate.97
  15.8 4.6 collective-permute-start
  26.5 2.4 collective-permute-start.5
  28.9 2.3 collective-permute-start.4
  31.9 9.1 %collective-permute-done.6 = bf16[272,384]{1,0:T(8,128)(2,1)S(1)} collective-permute-done((bf16[272,384]{1,0:T(8,128)(2,1)S(1)}, bf16[272,384]{1,0:T(8,128)(2,1)S(1)}, u32[]{:S(2)}, u32[]{:S(2)}) %collective-permute-start.6) | collective-permute-done | bytes 208928 | tf_op jit(solution)/shard_map/ppermute | solution.py:48
  41.0 7.3 %collective-permute-start.12 = (bf16[256,640]{1,0:T(8,128)(2,1)S(1)}, bf16[256,640]{1,0:T(8,128)(2,1)S(1)}, u32[]{:S(2)}, u32[]{:S(2)}) collective-permute-start(bf16[256,640]{1,0:T(8,128)(2,1)S(1)} %fusion.44), channel_id=1, source_target_pairs={{0,2},{1,3},{2,0},{3,1},{4,6},{5,7},{6,4},{7,5},{8,10},{9,11},{10,... | collective-permute-start | bytes 983048 | tf_op jit(solution)/shard_map/ppermute | solution.py:48
  48.3 4.8 collective-permute-start.13
  54.8 2.2 collective-permute-done.11
  58.8 16.7 %collective-permute-done.12 = bf16[256,640]{1,0:T(8,128)(2,1)S(1)} collective-permute-done((bf16[256,640]{1,0:T(8,128)(2,1)S(1)}, bf16[256,640]{1,0:T(8,128)(2,1)S(1)}, u32[]{:S(2)}, u32[]{:S(2)}) %collective-permute-start.12) | collective-permute-done | bytes 327712 | tf_op jit(solution)/shard_map/ppermute | solution.py:48
  80.4 5.7 %collective-permute-done.23 = bf16[256,512]{1,0:T(8,128)(2,1)S(1)} collective-permute-done((bf16[256,512]{1,0:T(8,128)(2,1)S(1)}, bf16[256,512]{1,0:T(8,128)(2,1)S(1)}, u32[]{:S(2)}, u32[]{:S(2)}) %collective-permute-start.23) | collective-permute-done | bytes 262176 | tf_op jit(solution)/shard_map/ppermute | solution.py:48
  88.1 8.8 %collective-permute-done.22 = bf16[256,512]{1,0:T(8,128)(2,1)S(1)} collective-permute-done((bf16[256,512]{1,0:T(8,128)(2,1)S(1)}, bf16[256,512]{1,0:T(8,128)(2,1)S(1)}, u32[]{:S(2)}, u32[]{:S(2)}) %collective-permute-start.22) | collective-permute-done | bytes 262176 | tf_op jit(solution)/shard_map/ppermute | solution.py:48
  96.9 2.5 collective-permute-start.29
  105.7 32.7 %collective-permute-done.10 = bf16[128,1536]{1,0:T(8,128)(2,1)S(1)} collective-permute-done((bf16[128,1536]{1,0:T(8,128)(2,1)S(1)}, bf16[128,1536]{1,0:T(8,128)(2,1)S(1)}, u32[]{:S(2)}, u32[]{:S(2)}) %collective-permute-start.10) | collective-permute-done | bytes 393248 | tf_op jit(solution)/shard_map/ppermute | solution.py:39
  138.8 4.0 collective-permute-start.1
  143.5 1.9 spread_small.1
  145.4 1.8 slice_dynamic-update-slice_fusion.6.w_ref
  157.0 4.5 add_convert_fusion.qkv_ref
  161.5 17.0 %attend.1 = (bf16[1024,512]{1,0:T(8,128)(2,1)S(1)}, f32[4,2,1024]{2,1,0:T(2,128)S(1)}) custom-call(f32[4,2]{1,0:T(4,128)S(1)} %multiply_exponential_fusion.slope_ref, bf16[1024,1536]{1,0:T(8,128)(2,1)S(1)} %add_convert_fusion.qkv_ref), custom_call_target="tpu_custom_call" | custom-call | flops 2147483648 | bytes 6291456 | tf_op jit(solution)/shard_map/attend/pallas_call | solution.py:222
  178.5 6.7 %collective-permute-done.16 = bf16[128,2560]{1,0:T(8,128)(2,1)S(1)} collective-permute-done((bf16[128,2560]{1,0:T(8,128)(2,1)S(1)}, bf16[128,2560]{1,0:T(8,128)(2,1)S(1)}, u32[]{:S(2)}, u32[]{:S(2)}) %collective-permute-start.16) | collective-permute-done | bytes 655392 | tf_op jit(solution)/shard_map/ppermute | solution.py:39
  185.3 1.8 convolution_convert_fusion.4
  187.1 1.8 collective-permute-start.18
  188.9 2.3 constant_dynamic-update-slice_fusion.16
  197.0 2.3 slice_dynamic-update-slice_fusion.1
  199.3 2.5 slice_dynamic-update-slice_fusion
  201.8 2.0 add_convert_fusion.4.here_ref
  203.8 5.2 %collective-permute-start.19 = (bf16[512,1024]{1,0:T(8,128)(2,1)S(1)}, bf16[512,1024]{1,0:T(8,128)(2,1)S(1)}, u32[]{:S(2)}, u32[]{:S(2)}) collective-permute-start(bf16[512,1024]{1,0:T(8,128)(2,1)S(1)} %add_convert_fusion.4.here_ref), channel_id=1, source_target_pairs={{1,4},{3,6},{4,1},{6,3},{9,12},{11,14},{12,9},{14,11},{17,20},{19,... | collective-permute-start | bytes 3145736 | tf_op jit(solution)/shard_map/ppermute | solution.py:58
  213.5 7.6 %collective-permute-done.19.swapped_ref = bf16[512,1024]{1,0:T(8,128)(2,1)S(1)} collective-permute-done((bf16[512,1024]{1,0:T(8,128)(2,1)S(1)}, bf16[512,1024]{1,0:T(8,128)(2,1)S(1)}, u32[]{:S(2)}, u32[]{:S(2)}) %collective-permute-start.19) | collective-permute-done | bytes 1048608 | tf_op jit(solution)/shard_map/ppermute | solution.py:58
  221.0 3.1 rows_mid.1
  226.9 9.0 %fusion.84 = f32[1024,2048]{1,0:T(8,128)} fusion(bf16[1024,1024]{1,0:T(8,128)(2,1)S(1)} %constant_dynamic-update-slice_fusion.9, bf16[1024,2048]{1,0:T(8,128)(2,1)} %slice_dynamic-update-slice_fusion.4), kind=kOutput, calls=%fused_computation.210 | convolution fusion | flops 4294967296 | bytes 14680064 | tf_op jit(solution)/shard_map/dot_general | solution.py:26
  235.9 14.3 %convert_reduce_fusion = (f32[2048]{0:T(1024)S(1)}, bf16[1024,2048]{1,0:T(8,128)(2,1)S(1)}, bf16[1024,2048]{1,0:T(8,128)(2,1)S(1)}) fusion(f32[1024,2048]{1,0:T(8,128)} %fusion.84, f32[2048]{0:T(1024)S(1)} %bitcast.80, bf16[1024,1024]{1,0:T(8,128)(2,1)} %constant_dynamic-update-slice_fusion.16, bf16[1024,2048]{1,0:T(8,128)(2,1)S(1)} %constant_dynamic-update-slice_fusion.11), kind=kOutput, calls=%fused_computation.10 | convolution fusion | flops 4355782656 | bytes 23085056 | tf_op jit(solution)/shard_map/dot_general | solution.py:26
  250.2 2.4 fusion.29
  252.6 4.9 convolution_convert_fusion.1
  257.6 3.4 fusion.26
  261.0 6.6 %convolution_convert_fusion = bf16[1024,2048]{1,0:T(8,128)(2,1)S(1)} fusion(bf16[1024,1024]{1,0:T(8,128)(2,1)} %constant_dynamic-update-slice_fusion.16, bf16[1024,2048]{1,0:T(8,128)(2,1)S(1)} %get-tuple-element.78), kind=kOutput, calls=%fused_computation.15 | convolution fusion | flops 4297064448 | bytes 10485760 | tf_op jit(solution)/shard_map/dot_general | solution.py:30
  271.3 2.4 fusion.14.own_ref
  273.6 8.2 %collective-permute-done.56 = bf16[128,2048]{1,0:T(8,128)(2,1)S(1)} collective-permute-done((bf16[128,2048]{1,0:T(8,128)(2,1)S(1)}, bf16[128,2048]{1,0:T(8,128)(2,1)S(1)}, u32[]{:S(2)}, u32[]{:S(2)}) %collective-permute-start.56) | collective-permute-done | bytes 524320 | tf_op jit(solution)/shard_map/ppermute | solution.py:39
  283.6 9.4 %collective-permute-done.64 = bf16[128,2048]{1,0:T(8,128)(2,1)S(1)} collective-permute-done((bf16[128,2048]{1,0:T(8,128)(2,1)S(1)}, bf16[128,2048]{1,0:T(8,128)(2,1)S(1)}, u32[]{:S(2)}, u32[]{:S(2)}) %collective-permute-start.64) | collective-permute-done | bytes 524320 | tf_op jit(solution)/shard_map/ppermute | solution.py:39
  296.4 3.7 fusion.10.own_ref
  300.1 4.7 rows_mid_back.1
  306.2 5.4 %collective-permute-start.31 = (bf16[512,1024]{1,0:T(8,128)(2,1)S(1)}, bf16[512,1024]{1,0:T(8,128)(2,1)S(1)}, u32[]{:S(2)}, u32[]{:S(2)}) collective-permute-start(bf16[512,1024]{1,0:T(8,128)(2,1)S(1)} %get-tuple-element.42), channel_id=1, source_target_pairs={{1,4},{3,6},{4,1},{6,3},{9,12},{11,14},{12,9},{14,11},{17,20},{19,... | collective-permute-start | bytes 3145736 | tf_op jit(solution)/shard_map/ppermute | solution.py:58
  311.7 2.6 rows_out.1
  316.3 2.4 fusion.61
  318.8 3.6 collective-permute-start.62
  322.4 15.7 %collective-permute-done.67 = bf16[256,2048]{1,0:T(8,128)(2,1)} collective-permute-done((bf16[256,2048]{1,0:T(8,128)(2,1)S(1)}, bf16[256,2048]{1,0:T(8,128)(2,1)}, u32[]{:S(2)}, u32[]{:S(2)}) %collective-permute-start.67) | collective-permute-done | bytes 1048608 | tf_op jit(solution)/shard_map/ppermute | solution.py:39
  339.4 2.4 fusion.60
  341.9 3.0 collective-permute-start.70
  346.6 2.7 collective-permute-start.32
  351.1 3.4 collective-permute-done.70
  354.5 16.6 %collective-permute-done.69 = bf16[256,512]{1,0:T(8,128)(2,1)S(1)} collective-permute-done((bf16[256,512]{1,0:T(8,128)(2,1)S(1)}, bf16[256,512]{1,0:T(8,128)(2,1)S(1)}, u32[]{:S(2)}, u32[]{:S(2)}) %collective-permute-start.69) | collective-permute-done | bytes 262176 | tf_op jit(solution)/shard_map/ppermute | solution.py:48
  381.0 21.7 %attend_back.1 = (bf16[1024,1536]{1,0:T(8,128)(2,1)S(1)}, f32[4,1,384]{2,1,0:T(1,128)S(1)}) custom-call(f32[4,2]{1,0:T(4,128)S(1)} %multiply_exponential_fusion.slope_ref, bf16[1024,1536]{1,0:T(8,128)(2,1)} %copy-done.18, bf16[1024,512]{1,0:T(8,128)(2,1)S(1)} %convolution_convert_fusion.3.grad_ref, f32[4,2,1024]{2,1,0:T(2,128)S(1)} %get-tuple-element.43.lse_ref), custom_call_target="tpu_custom_call" | custom-call | flops 5368709120 | bytes 9437184 | tf_op jit(solution)/shard_map/attend_back/pallas_call | solution.py:292
  402.7 2.8 fusion.23
  405.6 7.4 %qkv_grads.1 = (bf16[1024,1536]{1,0:T(8,128)(2,1)S(1)}, f32[8,1024]{1,0:T(8,128)S(1)}) custom-call(bf16[1024,1024]{1,0:T(8,128)(2,1)S(1)} %copy-done.5, bf16[1024,1536]{1,0:T(8,128)(2,1)} %copy-done.16, bf16[1024,1536]{1,0:T(8,128)(2,1)} %slice_dynamic-update-slice_fusion.6.w_ref, f32[1,1536]{1,0:T(1,128)S(1)} %bitcast.78, f32[1024,128]{1,0:T(8,128)S(1)} %copy-done.9), custom_call_target="tpu_custom_call" | custom-call | flops 3221225472 | bytes 9437184 | tf_op jit(solution)/shard_map/qkv_grads/pallas_call | solution.py:576
  418.5 9.1 %collective-permute-done.36 = f32[16,1024]{1,0:T(8,128)S(1)} collective-permute-done((f32[16,1024]{1,0:T(8,128)S(1)}, f32[16,1024]{1,0:T(8,128)S(1)}, u32[]{:S(2)}, u32[]{:S(2)}) %collective-permute-start.36) | collective-permute-done | bytes 65568 | tf_op jit(solution)/shard_map/ppermute | solution.py:39
  429.2 2.2 collective-permute-done.50
  433.5 2.0 collective-permute-done.38
  436.9 3.2 collective-permute-done.39
  448.4 4.0 add_convert_fusion.3.here_ref
  452.5 6.0 %collective-permute-done.43 = bf16[256,1536]{1,0:T(8,128)(2,1)S(1)} collective-permute-done((bf16[256,1536]{1,0:T(8,128)(2,1)S(1)}, bf16[256,1536]{1,0:T(8,128)(2,1)S(1)}, u32[]{:S(2)}, u32[]{:S(2)}) %collective-permute-start.43) | collective-permute-done | bytes 786464 | tf_op jit(solution)/shard_map/ppermute | solution.py:39
  458.5 6.7 %collective-permute-start.34 = (bf16[512,1024]{1,0:T(8,128)(2,1)}, bf16[512,1024]{1,0:T(8,128)(2,1)}, u32[]{:S(2)}, u32[]{:S(2)}) collective-permute-start(bf16[512,1024]{1,0:T(8,128)(2,1)} %add_convert_fusion.3.here_ref), channel_id=1, source_target_pairs={{1,4},{3,6},{4,1},{6,3},{9,12},{11,14},{12,9},{14,11},{17,20},{19,... | collective-permute-start | bytes 3145736 | tf_op jit(solution)/shard_map/ppermute | solution.py:58
  467.6 2.9 collective-permute-start.55
  470.5 15.0 %collective-permute-done.46 = bf16[256,384]{1,0:T(8,128)(2,1)S(1)} collective-permute-done((bf16[256,384]{1,0:T(8,128)(2,1)S(1)}, bf16[256,384]{1,0:T(8,128)(2,1)S(1)}, u32[]{:S(2)}, u32[]{:S(2)}) %collective-permute-start.46) | collective-permute-done | bytes 196640 | tf_op jit(solution)/shard_map/ppermute | solution.py:48
  485.5 2.1 collective-permute-done.45
  487.6 2.1 collective-permute-done.44
  494.2 4.9 rows_first_back.1
  (342 shorter events, 110.4 us)
Async XLA Ops:
  5.9 19.4 %collective-permute-start.3 = (bf16[128,1536]{1,0:T(8,128)(2,1)}, bf16[128,1536]{1,0:T(8,128)(2,1)}, u32[]{:S(2)}, u32[]{:S(2)}) collective-permute-start(bf16[128,1536]{1,0:T(8,128)(2,1)} %get-tuple-element.33), channel_id=1, source_target_pairs={{0,4},{4,0},{8,12},{12,8},{16,20},{20,16},{24,28},{28,24},{1,5},{5... | collective-permute-start | bytes 1179656 | tf_op jit(solution)/shard_map/ppermute | solution.py:39
  12.2 12.5 %collective-permute-start.2 = (bf16[1,384]{1,0:T(2,128)(2,1)}, bf16[1,384]{1,0:T(2,128)(2,1)}, u32[]{:S(2)}, u32[]{:S(2)}) collective-permute-start(bf16[1,384]{1,0:T(2,128)(2,1)} %reshape.115), channel_id=1, source_target_pairs={{0,4},{4,0},{8,12},{12,8},{16,20},{20,16},{24,28},{28,24},{1,5},{5... | collective-permute-start | bytes 2312 | tf_op jit(solution)/shard_map/ppermute | solution.py:39
  15.8 86.4 %collective-permute-start = (bf16[512,1024]{1,0:T(8,128)(2,1)S(1)}, bf16[512,1024]{1,0:T(8,128)(2,1)}, u32[]{:S(2)}, u32[]{:S(2)}) collective-permute-start(bf16[512,1024]{1,0:T(8,128)(2,1)S(1)} %rows_first.1), channel_id=1, source_target_pairs={{1,4},{3,6},{4,1},{6,3},{9,12},{11,14},{12,9},{14,11},{17,20},{19,... | collective-permute-start | bytes 3145736 | tf_op jit(solution)/shard_map/ppermute | solution.py:58
  26.5 14.6 %collective-permute-start.6 = (bf16[272,384]{1,0:T(8,128)(2,1)S(1)}, bf16[272,384]{1,0:T(8,128)(2,1)S(1)}, u32[]{:S(2)}, u32[]{:S(2)}) collective-permute-start(bf16[272,384]{1,0:T(8,128)(2,1)S(1)} %pad_maximum_fusion.14), channel_id=1, source_target_pairs={{0,1},{1,2},{2,3},{3,0},{4,5},{5,6},{6,7},{7,4},{8,9},{9,10},{10,1... | collective-permute-start | bytes 626696 | tf_op jit(solution)/shard_map/ppermute | solution.py:48
  26.5 21.8 %collective-permute-start.5 = (bf16[272,384]{1,0:T(8,128)(2,1)S(1)}, bf16[272,384]{1,0:T(8,128)(2,1)S(1)}, u32[]{:S(2)}, u32[]{:S(2)}) collective-permute-start(bf16[272,384]{1,0:T(8,128)(2,1)S(1)} %pad_maximum_fusion.14), channel_id=1, source_target_pairs={{0,2},{1,3},{2,0},{3,1},{4,6},{5,7},{6,4},{7,5},{8,10},{9,11},{10,... | collective-permute-start | bytes 626696 | tf_op jit(solution)/shard_map/ppermute | solution.py:48
  28.9 24.3 %collective-permute-start.4 = (bf16[272,384]{1,0:T(8,128)(2,1)S(1)}, bf16[272,384]{1,0:T(8,128)(2,1)S(1)}, u32[]{:S(2)}, u32[]{:S(2)}) collective-permute-start(bf16[272,384]{1,0:T(8,128)(2,1)S(1)} %pad_maximum_fusion.14), channel_id=1, source_target_pairs={{0,3},{1,0},{2,1},{3,2},{4,7},{5,4},{6,5},{7,6},{8,11},{9,8},{10,9... | collective-permute-start | bytes 626696 | tf_op jit(solution)/shard_map/ppermute | solution.py:48
  31.2 25.8 %collective-permute-start.11 = (bf16[256,640]{1,0:T(8,128)(2,1)S(1)}, bf16[256,640]{1,0:T(8,128)(2,1)S(1)}, u32[]{:S(2)}, u32[]{:S(2)}) collective-permute-start(bf16[256,640]{1,0:T(8,128)(2,1)S(1)} %fusion.44), channel_id=1, source_target_pairs={{0,3},{1,0},{2,1},{3,2},{4,7},{5,4},{6,5},{7,6},{8,11},{9,8},{10,9... | collective-permute-start | bytes 983048 | tf_op jit(solution)/shard_map/ppermute | solution.py:48
  41.0 34.5 %collective-permute-start.12 = (bf16[256,640]{1,0:T(8,128)(2,1)S(1)}, bf16[256,640]{1,0:T(8,128)(2,1)S(1)}, u32[]{:S(2)}, u32[]{:S(2)}) collective-permute-start(bf16[256,640]{1,0:T(8,128)(2,1)S(1)} %fusion.44), channel_id=1, source_target_pairs={{0,2},{1,3},{2,0},{3,1},{4,6},{5,7},{6,4},{7,5},{8,10},{9,11},{10,... | collective-permute-start | bytes 983048 | tf_op jit(solution)/shard_map/ppermute | solution.py:48
  48.3 27.8 %collective-permute-start.13 = (bf16[256,640]{1,0:T(8,128)(2,1)S(1)}, bf16[256,640]{1,0:T(8,128)(2,1)S(1)}, u32[]{:S(2)}, u32[]{:S(2)}) collective-permute-start(bf16[256,640]{1,0:T(8,128)(2,1)S(1)} %fusion.44), channel_id=1, source_target_pairs={{0,1},{1,2},{2,3},{3,0},{4,5},{5,6},{6,7},{7,4},{8,9},{9,10},{10,1... | collective-permute-start | bytes 983048 | tf_op jit(solution)/shard_map/ppermute | solution.py:48
  53.5 51.3 %collective-permute-start.7 = (bf16[272,1536]{1,0:T(8,128)(2,1)S(1)}, bf16[272,1536]{1,0:T(8,128)(2,1)S(1)}, u32[]{:S(2)}, u32[]{:S(2)}) collective-permute-start(bf16[272,1536]{1,0:T(8,128)(2,1)S(1)} %fusion.34), channel_id=1, source_target_pairs={{0,8},{4,12},{8,0},{12,4},{16,24},{20,28},{24,16},{28,20},{1,9},{5... | collective-permute-start | bytes 2506760 | tf_op jit(solution)/shard_map/ppermute | solution.py:39
  57.0 48.1 %collective-permute-start.8 = (bf16[272,1536]{1,0:T(8,128)(2,1)S(1)}, bf16[272,1536]{1,0:T(8,128)(2,1)S(1)}, u32[]{:S(2)}, u32[]{:S(2)}) collective-permute-start(bf16[272,1536]{1,0:T(8,128)(2,1)S(1)} %fusion.34), channel_id=1, source_target_pairs={{0,16},{4,20},{8,24},{12,28},{16,0},{20,4},{24,8},{28,12},{1,17},{... | collective-permute-start | bytes 2506760 | tf_op jit(solution)/shard_map/ppermute | solution.py:39
  77.5 8.5 %collective-permute-start.23 = (bf16[256,512]{1,0:T(8,128)(2,1)S(1)}, bf16[256,512]{1,0:T(8,128)(2,1)S(1)}, u32[]{:S(2)}, u32[]{:S(2)}) collective-permute-start(bf16[256,512]{1,0:T(8,128)(2,1)S(1)} %get-tuple-element.118), channel_id=1, source_target_pairs={{0,1},{1,2},{2,3},{3,0},{4,5},{5,6},{6,7},{7,4},{8,9},{9,10},{10,1... | collective-permute-start | bytes 786440 | tf_op jit(solution)/shard_map/ppermute | solution.py:48
  77.5 19.4 %collective-permute-start.22 = (bf16[256,512]{1,0:T(8,128)(2,1)S(1)}, bf16[256,512]{1,0:T(8,128)(2,1)S(1)}, u32[]{:S(2)}, u32[]{:S(2)}) collective-permute-start(bf16[256,512]{1,0:T(8,128)(2,1)S(1)} %get-tuple-element.118), channel_id=1, source_target_pairs={{0,2},{1,3},{2,0},{3,1},{4,6},{5,7},{6,4},{7,5},{8,10},{9,11},{10,... | collective-permute-start | bytes 786440 | tf_op jit(solution)/shard_map/ppermute | solution.py:48
  86.1 13.4 %collective-permute-start.21 = (bf16[256,512]{1,0:T(8,128)(2,1)S(1)}, bf16[256,512]{1,0:T(8,128)(2,1)S(1)}, u32[]{:S(2)}, u32[]{:S(2)}) collective-permute-start(bf16[256,512]{1,0:T(8,128)(2,1)S(1)} %get-tuple-element.118), channel_id=1, source_target_pairs={{0,3},{1,0},{2,1},{3,2},{4,7},{5,4},{6,5},{7,6},{8,11},{9,8},{10,9... | collective-permute-start | bytes 786440 | tf_op jit(solution)/shard_map/ppermute | solution.py:48
  96.9 92.0 %collective-permute-start.29 = (bf16[512,1024]{1,0:T(8,128)(2,1)S(1)}, bf16[512,1024]{1,0:T(8,128)(2,1)}, u32[]{:S(2)}, u32[]{:S(2)}) collective-permute-start(bf16[512,1024]{1,0:T(8,128)(2,1)S(1)} %copy-done.8), channel_id=1, source_target_pairs={{0,4},{4,0},{8,12},{12,8},{16,20},{20,16},{24,28},{28,24},{1,5},{5... | collective-permute-start | bytes 3145736 | tf_op jit(solution)/shard_map/ppermute | solution.py:39
  99.5 47.8 %collective-permute-start.14 = (bf16[256,2560]{1,0:T(8,128)(2,1)}, bf16[256,2560]{1,0:T(8,128)(2,1)}, u32[]{:S(2)}, u32[]{:S(2)}) collective-permute-start(bf16[256,2560]{1,0:T(8,128)(2,1)} %get-tuple-element.132), channel_id=1, source_target_pairs={{0,8},{4,12},{8,0},{12,4},{16,24},{20,28},{24,16},{28,20},{1,9},{5... | collective-permute-start | bytes 3932168 | tf_op jit(solution)/shard_map/ppermute | solution.py:39
  102.2 47.3 %collective-permute-start.15 = (bf16[256,2560]{1,0:T(8,128)(2,1)}, bf16[256,2560]{1,0:T(8,128)(2,1)}, u32[]{:S(2)}, u32[]{:S(2)}) collective-permute-start(bf16[256,2560]{1,0:T(8,128)(2,1)} %get-tuple-element.132), channel_id=1, source_target_pairs={{0,16},{4,20},{8,24},{12,28},{16,0},{20,4},{24,8},{28,12},{1,17},{... | collective-permute-start | bytes 3932168 | tf_op jit(solution)/shard_map/ppermute | solution.py:39
  104.8 33.5 %collective-permute-start.10 = (bf16[128,1536]{1,0:T(8,128)(2,1)S(1)}, bf16[128,1536]{1,0:T(8,128)(2,1)S(1)}, u32[]{:S(2)}, u32[]{:S(2)}) collective-permute-start(bf16[128,1536]{1,0:T(8,128)(2,1)S(1)} %slice.584), channel_id=1, source_target_pairs={{0,16},{4,20},{8,24},{12,28},{16,0},{20,4},{24,8},{28,12},{1,17},{... | collective-permute-start | bytes 1179656 | tf_op jit(solution)/shard_map/ppermute | solution.py:39
  105.2 33.6 %collective-permute-start.9 = (bf16[144,1536]{1,0:T(8,128)(2,1)S(1)}, bf16[144,1536]{1,0:T(8,128)(2,1)}, u32[]{:S(2)}, u32[]{:S(2)}) collective-permute-start(bf16[144,1536]{1,0:T(8,128)(2,1)S(1)} %slice.580), channel_id=1, source_target_pairs={{0,8},{4,12},{8,0},{12,4},{16,24},{20,28},{24,16},{28,20},{1,9},{5... | collective-permute-start | bytes 1327112 | tf_op jit(solution)/shard_map/ppermute | solution.py:39
  138.4 53.8 %collective-permute-start.24 = (bf16[256,2048]{1,0:T(8,128)(2,1)}, bf16[256,2048]{1,0:T(8,128)(2,1)}, u32[]{:S(2)}, u32[]{:S(2)}) collective-permute-start(bf16[256,2048]{1,0:T(8,128)(2,1)} %get-tuple-element.113), channel_id=1, source_target_pairs={{0,8},{4,12},{8,0},{12,4},{16,24},{20,28},{24,16},{28,20},{1,9},{5... | collective-permute-start | bytes 3145736 | tf_op jit(solution)/shard_map/ppermute | solution.py:39
  138.8 15.6 %collective-permute-start.1 = (bf16[512,1024]{1,0:T(8,128)(2,1)S(1)}, bf16[512,1024]{1,0:T(8,128)(2,1)}, u32[]{:S(2)}, u32[]{:S(2)}) collective-permute-start(bf16[512,1024]{1,0:T(8,128)(2,1)S(1)} %broadcast_select_fusion.1), channel_id=1, source_target_pairs={{0,4},{4,0},{8,12},{12,8},{16,20},{20,16},{24,28},{28,24},{1,5},{5... | collective-permute-start | bytes 3145736 | tf_op jit(solution)/shard_map/ppermute | solution.py:39
  147.2 47.4 %collective-permute-start.25 = (bf16[256,2048]{1,0:T(8,128)(2,1)}, bf16[256,2048]{1,0:T(8,128)(2,1)}, u32[]{:S(2)}, u32[]{:S(2)}) collective-permute-start(bf16[256,2048]{1,0:T(8,128)(2,1)} %get-tuple-element.113), channel_id=1, source_target_pairs={{0,16},{4,20},{8,24},{12,28},{16,0},{20,4},{24,8},{28,12},{1,17},{... | collective-permute-start | bytes 3145736 | tf_op jit(solution)/shard_map/ppermute | solution.py:39
  149.6 35.7 %collective-permute-start.16 = (bf16[128,2560]{1,0:T(8,128)(2,1)S(1)}, bf16[128,2560]{1,0:T(8,128)(2,1)S(1)}, u32[]{:S(2)}, u32[]{:S(2)}) collective-permute-start(bf16[128,2560]{1,0:T(8,128)(2,1)S(1)} %slice.600), channel_id=1, source_target_pairs={{0,16},{4,20},{8,24},{12,28},{16,0},{20,4},{24,8},{28,12},{1,17},{... | collective-permute-start | bytes 1966088 | tf_op jit(solution)/shard_map/ppermute | solution.py:39
  154.4 30.9 %collective-permute-start.17 = (bf16[128,2560]{1,0:T(8,128)(2,1)S(1)}, bf16[128,2560]{1,0:T(8,128)(2,1)S(1)}, u32[]{:S(2)}, u32[]{:S(2)}) collective-permute-start(bf16[128,2560]{1,0:T(8,128)(2,1)S(1)} %slice.602), channel_id=1, source_target_pairs={{0,8},{4,12},{8,0},{12,4},{16,24},{20,28},{24,16},{28,20},{1,9},{5... | collective-permute-start | bytes 1966088 | tf_op jit(solution)/shard_map/ppermute | solution.py:39
  187.1 14.7 %collective-permute-start.18 = (bf16[512,1024]{1,0:T(8,128)(2,1)}, bf16[512,1024]{1,0:T(8,128)(2,1)}, u32[]{:S(2)}, u32[]{:S(2)}) collective-permute-start(bf16[512,1024]{1,0:T(8,128)(2,1)} %convolution_convert_fusion.4), channel_id=1, source_target_pairs={{0,4},{4,0},{8,12},{12,8},{16,20},{20,16},{24,28},{28,24},{1,5},{5... | collective-permute-start | bytes 3145736 | tf_op jit(solution)/shard_map/ppermute | solution.py:39
  193.3 20.0 %collective-permute-start.26 = (bf16[128,2048]{1,0:T(8,128)(2,1)S(1)}, bf16[128,2048]{1,0:T(8,128)(2,1)S(1)}, u32[]{:S(2)}, u32[]{:S(2)}) collective-permute-start(bf16[128,2048]{1,0:T(8,128)(2,1)S(1)} %slice.609), channel_id=1, source_target_pairs={{0,16},{4,20},{8,24},{12,28},{16,0},{20,4},{24,8},{28,12},{1,17},{... | collective-permute-start | bytes 1572872 | tf_op jit(solution)/shard_map/ppermute | solution.py:39
  195.7 17.7 %collective-permute-start.27 = (bf16[128,2048]{1,0:T(8,128)(2,1)S(1)}, bf16[128,2048]{1,0:T(8,128)(2,1)S(1)}, u32[]{:S(2)}, u32[]{:S(2)}) collective-permute-start(bf16[128,2048]{1,0:T(8,128)(2,1)S(1)} %slice.610), channel_id=1, source_target_pairs={{0,8},{4,12},{8,0},{12,4},{16,24},{20,28},{24,16},{28,20},{1,9},{5... | collective-permute-start | bytes 1572872 | tf_op jit(solution)/shard_map/ppermute | solution.py:39
  203.8 17.3 %collective-permute-start.19 = (bf16[512,1024]{1,0:T(8,128)(2,1)S(1)}, bf16[512,1024]{1,0:T(8,128)(2,1)S(1)}, u32[]{:S(2)}, u32[]{:S(2)}) collective-permute-start(bf16[512,1024]{1,0:T(8,128)(2,1)S(1)} %add_convert_fusion.4.here_ref), channel_id=1, source_target_pairs={{1,4},{3,6},{4,1},{6,3},{9,12},{11,14},{12,9},{14,11},{17,20},{19,... | collective-permute-start | bytes 3145736 | tf_op jit(solution)/shard_map/ppermute | solution.py:58
  267.7 38.6 %collective-permute-start.28 = (bf16[512,1024]{1,0:T(8,128)(2,1)}, bf16[512,1024]{1,0:T(8,128)(2,1)S(1)}, u32[]{:S(2)}, u32[]{:S(2)}) collective-permute-start(bf16[512,1024]{1,0:T(8,128)(2,1)} %fusion.26), channel_id=1, source_target_pairs={{0,4},{4,0},{8,12},{12,8},{16,20},{20,16},{24,28},{28,24},{1,5},{5... | collective-permute-start | bytes 3145736 | tf_op jit(solution)/shard_map/ppermute | solution.py:39
  267.9 26.8 %collective-permute-start.30 = (bf16[512,1024]{1,0:T(8,128)(2,1)S(1)}, bf16[512,1024]{1,0:T(8,128)(2,1)S(1)}, u32[]{:S(2)}, u32[]{:S(2)}) collective-permute-start(bf16[512,1024]{1,0:T(8,128)(2,1)S(1)} %fusion.29), channel_id=1, source_target_pairs={{0,4},{4,0},{8,12},{12,8},{16,20},{20,16},{24,28},{28,24},{1,5},{5... | collective-permute-start | bytes 3145736 | tf_op jit(solution)/shard_map/ppermute | solution.py:39
  268.4 13.5 %collective-permute-start.56 = (bf16[128,2048]{1,0:T(8,128)(2,1)S(1)}, bf16[128,2048]{1,0:T(8,128)(2,1)S(1)}, u32[]{:S(2)}, u32[]{:S(2)}) collective-permute-start(bf16[128,2048]{1,0:T(8,128)(2,1)S(1)} %get-tuple-element.87), channel_id=1, source_target_pairs={{0,16},{4,20},{8,24},{12,28},{16,0},{20,4},{24,8},{28,12},{1,17},{... | collective-permute-start | bytes 1572872 | tf_op jit(solution)/shard_map/ppermute | solution.py:39
  268.7 13.4 %collective-permute-start.58 = (bf16[128,2048]{1,0:T(8,128)(2,1)S(1)}, bf16[128,2048]{1,0:T(8,128)(2,1)S(1)}, u32[]{:S(2)}, u32[]{:S(2)}) collective-permute-start(bf16[128,2048]{1,0:T(8,128)(2,1)S(1)} %get-tuple-element.88), channel_id=1, source_target_pairs={{0,8},{4,12},{8,0},{12,4},{16,24},{20,28},{24,16},{28,20},{1,9},{5... | collective-permute-start | bytes 1572872 | tf_op jit(solution)/shard_map/ppermute | solution.py:39
  269.1 24.0 %collective-permute-start.64 = (bf16[128,2048]{1,0:T(8,128)(2,1)S(1)}, bf16[128,2048]{1,0:T(8,128)(2,1)S(1)}, u32[]{:S(2)}, u32[]{:S(2)}) collective-permute-start(bf16[128,2048]{1,0:T(8,128)(2,1)S(1)} %get-tuple-element.81), channel_id=1, source_target_pairs={{0,16},{4,20},{8,24},{12,28},{16,0},{20,4},{24,8},{28,12},{1,17},{... | collective-permute-start | bytes 1572872 | tf_op jit(solution)/shard_map/ppermute | solution.py:39
  281.8 11.9 %collective-permute-start.66 = (bf16[128,2048]{1,0:T(8,128)(2,1)S(1)}, bf16[128,2048]{1,0:T(8,128)(2,1)S(1)}, u32[]{:S(2)}, u32[]{:S(2)}) collective-permute-start(bf16[128,2048]{1,0:T(8,128)(2,1)S(1)} %get-tuple-element.82), channel_id=1, source_target_pairs={{0,8},{4,12},{8,0},{12,4},{16,24},{20,28},{24,16},{28,20},{1,9},{5... | collective-permute-start | bytes 1572872 | tf_op jit(solution)/shard_map/ppermute | solution.py:39
  282.6 33.1 %collective-permute-start.59 = (bf16[256,2048]{1,0:T(8,128)(2,1)S(1)}, bf16[256,2048]{1,0:T(8,128)(2,1)}, u32[]{:S(2)}, u32[]{:S(2)}) collective-permute-start(bf16[256,2048]{1,0:T(8,128)(2,1)S(1)} %pad_maximum_fusion.6), channel_id=1, source_target_pairs={{0,16},{4,20},{8,24},{12,28},{16,0},{20,4},{24,8},{28,12},{1,17},{... | collective-permute-start | bytes 3145736 | tf_op jit(solution)/shard_map/ppermute | solution.py:39
  293.1 23.3 %collective-permute-start.57 = (bf16[256,2048]{1,0:T(8,128)(2,1)S(1)}, bf16[256,2048]{1,0:T(8,128)(2,1)}, u32[]{:S(2)}, u32[]{:S(2)}) collective-permute-start(bf16[256,2048]{1,0:T(8,128)(2,1)S(1)} %pad_maximum_fusion.5), channel_id=1, source_target_pairs={{0,8},{4,12},{8,0},{12,4},{16,24},{20,28},{24,16},{28,20},{1,9},{5... | collective-permute-start | bytes 3145736 | tf_op jit(solution)/shard_map/ppermute | solution.py:39
  294.3 43.8 %collective-permute-start.67 = (bf16[256,2048]{1,0:T(8,128)(2,1)S(1)}, bf16[256,2048]{1,0:T(8,128)(2,1)}, u32[]{:S(2)}, u32[]{:S(2)}) collective-permute-start(bf16[256,2048]{1,0:T(8,128)(2,1)S(1)} %pad_maximum_fusion.8), channel_id=1, source_target_pairs={{0,16},{4,20},{8,24},{12,28},{16,0},{20,4},{24,8},{28,12},{1,17},{... | collective-permute-start | bytes 3145736 | tf_op jit(solution)/shard_map/ppermute | solution.py:39
  294.6 44.7 %collective-permute-start.65 = (bf16[256,2048]{1,0:T(8,128)(2,1)S(1)}, bf16[256,2048]{1,0:T(8,128)(2,1)}, u32[]{:S(2)}, u32[]{:S(2)}) collective-permute-start(bf16[256,2048]{1,0:T(8,128)(2,1)S(1)} %pad_maximum_fusion.7), channel_id=1, source_target_pairs={{0,8},{4,12},{8,0},{12,4},{16,24},{20,28},{24,16},{28,20},{1,9},{5... | collective-permute-start | bytes 3145736 | tf_op jit(solution)/shard_map/ppermute | solution.py:39
  306.2 38.7 %collective-permute-start.31 = (bf16[512,1024]{1,0:T(8,128)(2,1)S(1)}, bf16[512,1024]{1,0:T(8,128)(2,1)S(1)}, u32[]{:S(2)}, u32[]{:S(2)}) collective-permute-start(bf16[512,1024]{1,0:T(8,128)(2,1)S(1)} %get-tuple-element.42), channel_id=1, source_target_pairs={{1,4},{3,6},{4,1},{6,3},{9,12},{11,14},{12,9},{14,11},{17,20},{19,... | collective-permute-start | bytes 3145736 | tf_op jit(solution)/shard_map/ppermute | solution.py:58
  318.8 26.5 %collective-permute-start.62 = (bf16[256,512]{1,0:T(8,128)(2,1)S(1)}, bf16[256,512]{1,0:T(8,128)(2,1)S(1)}, u32[]{:S(2)}, u32[]{:S(2)}) collective-permute-start(bf16[256,512]{1,0:T(8,128)(2,1)S(1)} %get-tuple-element.105), channel_id=1, source_target_pairs={{0,3},{1,0},{2,1},{3,2},{4,7},{5,4},{6,5},{7,6},{8,11},{9,8},{10,9... | collective-permute-start | bytes 786440 | tf_op jit(solution)/shard_map/ppermute | solution.py:48
  322.4 24.2 %collective-permute-start.61 = (bf16[256,512]{1,0:T(8,128)(2,1)S(1)}, bf16[256,512]{1,0:T(8,128)(2,1)S(1)}, u32[]{:S(2)}, u32[]{:S(2)}) collective-permute-start(bf16[256,512]{1,0:T(8,128)(2,1)S(1)} %get-tuple-element.106), channel_id=1, source_target_pairs={{0,2},{1,3},{2,0},{3,1},{4,6},{5,7},{6,4},{7,5},{8,10},{9,11},{10,... | collective-permute-start | bytes 786440 | tf_op jit(solution)/shard_map/ppermute | solution.py:48
  338.1 11.2 %collective-permute-start.60 = (bf16[256,512]{1,0:T(8,128)(2,1)S(1)}, bf16[256,512]{1,0:T(8,128)(2,1)S(1)}, u32[]{:S(2)}, u32[]{:S(2)}) collective-permute-start(bf16[256,512]{1,0:T(8,128)(2,1)S(1)} %get-tuple-element.104), channel_id=1, source_target_pairs={{0,1},{1,2},{2,3},{3,0},{4,5},{5,6},{6,7},{7,4},{8,9},{9,10},{10,1... | collective-permute-start | bytes 786440 | tf_op jit(solution)/shard_map/ppermute | solution.py:48
  341.9 12.7 %collective-permute-start.70 = (bf16[256,512]{1,0:T(8,128)(2,1)S(1)}, bf16[256,512]{1,0:T(8,128)(2,1)S(1)}, u32[]{:S(2)}, u32[]{:S(2)}) collective-permute-start(bf16[256,512]{1,0:T(8,128)(2,1)S(1)} %get-tuple-element.102), channel_id=1, source_target_pairs={{0,3},{1,0},{2,1},{3,2},{4,7},{5,4},{6,5},{7,6},{8,11},{9,8},{10,9... | collective-permute-start | bytes 786440 | tf_op jit(solution)/shard_map/ppermute | solution.py:48
  344.9 26.3 %collective-permute-start.69 = (bf16[256,512]{1,0:T(8,128)(2,1)S(1)}, bf16[256,512]{1,0:T(8,128)(2,1)S(1)}, u32[]{:S(2)}, u32[]{:S(2)}) collective-permute-start(bf16[256,512]{1,0:T(8,128)(2,1)S(1)} %get-tuple-element.103), channel_id=1, source_target_pairs={{0,2},{1,3},{2,0},{3,1},{4,6},{5,7},{6,4},{7,5},{8,10},{9,11},{10,... | collective-permute-start | bytes 786440 | tf_op jit(solution)/shard_map/ppermute | solution.py:48
  345.3 25.8 %collective-permute-start.68 = (bf16[256,512]{1,0:T(8,128)(2,1)S(1)}, bf16[256,512]{1,0:T(8,128)(2,1)S(1)}, u32[]{:S(2)}, u32[]{:S(2)}) collective-permute-start(bf16[256,512]{1,0:T(8,128)(2,1)S(1)} %get-tuple-element.101), channel_id=1, source_target_pairs={{0,1},{1,2},{2,3},{3,0},{4,5},{5,6},{6,7},{7,4},{8,9},{9,10},{10,1... | collective-permute-start | bytes 786440 | tf_op jit(solution)/shard_map/ppermute | solution.py:48
  346.6 30.2 %collective-permute-start.32 = (bf16[512,1024]{1,0:T(8,128)(2,1)S(1)}, bf16[512,1024]{1,0:T(8,128)(2,1)}, u32[]{:S(2)}, u32[]{:S(2)}) collective-permute-start(bf16[512,1024]{1,0:T(8,128)(2,1)S(1)} %broadcast_select_fusion), channel_id=1, source_target_pairs={{0,4},{4,0},{8,12},{12,8},{16,20},{20,16},{24,28},{28,24},{1,5},{5... | collective-permute-start | bytes 3145736 | tf_op jit(solution)/shard_map/ppermute | solution.py:39
  349.5 23.9 %collective-permute-start.63 = (f32[128,512]{1,0:T(8,128)S(1)}, f32[128,512]{1,0:T(8,128)S(1)}, u32[]{:S(2)}, u32[]{:S(2)}) collective-permute-start(f32[128,512]{1,0:T(8,128)S(1)} %get-tuple-element.124), channel_id=1, source_target_pairs={{0,4},{4,0},{8,12},{12,8},{16,20},{20,16},{24,28},{28,24},{1,5},{5... | collective-permute-start | bytes 786440 | tf_op jit(solution)/shard_map/ppermute | solution.py:39
  405.5 42.2 %collective-permute-start.33 = (bf16[512,1024]{1,0:T(8,128)(2,1)}, bf16[512,1024]{1,0:T(8,128)(2,1)}, u32[]{:S(2)}, u32[]{:S(2)}) collective-permute-start(bf16[512,1024]{1,0:T(8,128)(2,1)} %fusion.23), channel_id=1, source_target_pairs={{0,4},{4,0},{8,12},{12,8},{16,20},{20,16},{24,28},{28,24},{1,5},{5... | collective-permute-start | bytes 3145736 | tf_op jit(solution)/shard_map/ppermute | solution.py:39
  415.3 26.9 %collective-permute-start.40 = (bf16[128,1536]{1,0:T(8,128)(2,1)}, bf16[128,1536]{1,0:T(8,128)(2,1)}, u32[]{:S(2)}, u32[]{:S(2)}) collective-permute-start(bf16[128,1536]{1,0:T(8,128)(2,1)} %get-tuple-element.93), channel_id=1, source_target_pairs={{0,16},{4,20},{8,24},{12,28},{16,0},{20,4},{24,8},{28,12},{1,17},{... | collective-permute-start | bytes 1179656 | tf_op jit(solution)/shard_map/ppermute | solution.py:39
  415.6 26.6 %collective-permute-start.42 = (bf16[128,1536]{1,0:T(8,128)(2,1)}, bf16[128,1536]{1,0:T(8,128)(2,1)}, u32[]{:S(2)}, u32[]{:S(2)}) collective-permute-start(bf16[128,1536]{1,0:T(8,128)(2,1)} %get-tuple-element.94), channel_id=1, source_target_pairs={{0,8},{4,12},{8,0},{12,4},{16,24},{20,28},{24,16},{28,20},{1,9},{5... | collective-permute-start | bytes 1179656 | tf_op jit(solution)/shard_map/ppermute | solution.py:39
  415.8 11.7 %collective-permute-start.36 = (f32[16,1024]{1,0:T(8,128)S(1)}, f32[16,1024]{1,0:T(8,128)S(1)}, u32[]{:S(2)}, u32[]{:S(2)}) collective-permute-start(f32[16,1024]{1,0:T(8,128)S(1)} %add.286), channel_id=1, source_target_pairs={{0,8},{4,12},{8,0},{12,4},{16,24},{20,28},{24,16},{28,20},{1,9},{5... | collective-permute-start | bytes 196616 | tf_op jit(solution)/shard_map/ppermute | solution.py:39
  417.2 11.7 %collective-permute-start.48 = (bf16[128,512]{0,1:T(8,128)(2,1)S(1)}, bf16[128,512]{0,1:T(8,128)(2,1)S(1)}, u32[]{:S(2)}, u32[]{:S(2)}) collective-permute-start(bf16[128,512]{0,1:T(8,128)(2,1)S(1)} %get-tuple-element.109), channel_id=1, source_target_pairs={{0,16},{4,20},{8,24},{12,28},{16,0},{20,4},{24,8},{28,12},{1,17},{... | collective-permute-start | bytes 393224 | tf_op jit(solution)/shard_map/ppermute | solution.py:39
  433.2 12.3 %collective-permute-start.51 = (bf16[256,512]{0,1:T(8,128)(2,1)}, bf16[256,512]{0,1:T(8,128)(2,1)}, u32[]{:S(2)}, u32[]{:S(2)}) collective-permute-start(bf16[256,512]{0,1:T(8,128)(2,1)} %pad_maximum_fusion.13), channel_id=1, source_target_pairs={{0,16},{4,20},{8,24},{12,28},{16,0},{20,4},{24,8},{28,12},{1,17},{... | collective-permute-start | bytes 786440 | tf_op jit(solution)/shard_map/ppermute | solution.py:39
  440.0 5.5 %collective-permute-start.49 = (bf16[256,512]{0,1:T(8,128)(2,1)}, bf16[256,512]{0,1:T(8,128)(2,1)}, u32[]{:S(2)}, u32[]{:S(2)}) collective-permute-start(bf16[256,512]{0,1:T(8,128)(2,1)} %pad_maximum_fusion.12), channel_id=1, source_target_pairs={{0,8},{4,12},{8,0},{12,4},{16,24},{20,28},{24,16},{28,20},{1,9},{5... | collective-permute-start | bytes 786440 | tf_op jit(solution)/shard_map/ppermute | solution.py:39
  443.7 14.8 %collective-permute-start.43 = (bf16[256,1536]{1,0:T(8,128)(2,1)S(1)}, bf16[256,1536]{1,0:T(8,128)(2,1)S(1)}, u32[]{:S(2)}, u32[]{:S(2)}) collective-permute-start(bf16[256,1536]{1,0:T(8,128)(2,1)S(1)} %pad_maximum_fusion.10), channel_id=1, source_target_pairs={{0,16},{4,20},{8,24},{12,28},{16,0},{20,4},{24,8},{28,12},{1,17},{... | collective-permute-start | bytes 2359304 | tf_op jit(solution)/shard_map/ppermute | solution.py:39
  444.8 20.4 %collective-permute-start.41 = (bf16[256,1536]{1,0:T(8,128)(2,1)S(1)}, bf16[256,1536]{1,0:T(8,128)(2,1)S(1)}, u32[]{:S(2)}, u32[]{:S(2)}) collective-permute-start(bf16[256,1536]{1,0:T(8,128)(2,1)S(1)} %pad_maximum_fusion.9), channel_id=1, source_target_pairs={{0,8},{4,12},{8,0},{12,4},{16,24},{20,28},{24,16},{28,20},{1,9},{5... | collective-permute-start | bytes 2359304 | tf_op jit(solution)/shard_map/ppermute | solution.py:39
  446.8 18.8 %collective-permute-start.54 = (bf16[256,128]{0,1:T(8,128)(2,1)S(1)}, bf16[256,128]{0,1:T(8,128)(2,1)S(1)}, u32[]{:S(2)}, u32[]{:S(2)}) collective-permute-start(bf16[256,128]{0,1:T(8,128)(2,1)S(1)} %get-tuple-element.140), channel_id=1, source_target_pairs={{0,3},{1,0},{2,1},{3,2},{4,7},{5,4},{6,5},{7,6},{8,11},{9,8},{10,9... | collective-permute-start | bytes 196616 | tf_op jit(solution)/shard_map/ppermute | solution.py:48
  446.9 19.3 %collective-permute-start.53 = (bf16[256,128]{0,1:T(8,128)(2,1)S(1)}, bf16[256,128]{0,1:T(8,128)(2,1)S(1)}, u32[]{:S(2)}, u32[]{:S(2)}) collective-permute-start(bf16[256,128]{0,1:T(8,128)(2,1)S(1)} %get-tuple-element.141), channel_id=1, source_target_pairs={{0,2},{1,3},{2,0},{3,1},{4,6},{5,7},{6,4},{7,5},{8,10},{9,11},{10,... | collective-permute-start | bytes 196616 | tf_op jit(solution)/shard_map/ppermute | solution.py:48
  447.7 19.9 %collective-permute-start.52 = (bf16[256,128]{0,1:T(8,128)(2,1)S(1)}, bf16[256,128]{0,1:T(8,128)(2,1)S(1)}, u32[]{:S(2)}, u32[]{:S(2)}) collective-permute-start(bf16[256,128]{0,1:T(8,128)(2,1)S(1)} %get-tuple-element.139), channel_id=1, source_target_pairs={{0,1},{1,2},{2,3},{3,0},{4,5},{5,6},{6,7},{7,4},{8,9},{9,10},{10,1... | collective-permute-start | bytes 196616 | tf_op jit(solution)/shard_map/ppermute | solution.py:48
  458.5 35.7 %collective-permute-start.34 = (bf16[512,1024]{1,0:T(8,128)(2,1)}, bf16[512,1024]{1,0:T(8,128)(2,1)}, u32[]{:S(2)}, u32[]{:S(2)}) collective-permute-start(bf16[512,1024]{1,0:T(8,128)(2,1)} %add_convert_fusion.3.here_ref), channel_id=1, source_target_pairs={{1,4},{3,6},{4,1},{6,3},{9,12},{11,14},{12,9},{14,11},{17,20},{19,... | collective-permute-start | bytes 3145736 | tf_op jit(solution)/shard_map/ppermute | solution.py:58
  465.6 20.0 %collective-permute-start.46 = (bf16[256,384]{1,0:T(8,128)(2,1)S(1)}, bf16[256,384]{1,0:T(8,128)(2,1)S(1)}, u32[]{:S(2)}, u32[]{:S(2)}) collective-permute-start(bf16[256,384]{1,0:T(8,128)(2,1)S(1)} %get-tuple-element.116), channel_id=1, source_target_pairs={{0,3},{1,0},{2,1},{3,2},{4,7},{5,4},{6,5},{7,6},{8,11},{9,8},{10,9... | collective-permute-start | bytes 589832 | tf_op jit(solution)/shard_map/ppermute | solution.py:48
  465.7 22.0 %collective-permute-start.45 = (bf16[256,384]{1,0:T(8,128)(2,1)S(1)}, bf16[256,384]{1,0:T(8,128)(2,1)S(1)}, u32[]{:S(2)}, u32[]{:S(2)}) collective-permute-start(bf16[256,384]{1,0:T(8,128)(2,1)S(1)} %get-tuple-element.117), channel_id=1, source_target_pairs={{0,2},{1,3},{2,0},{3,1},{4,6},{5,7},{6,4},{7,5},{8,10},{9,11},{10,... | collective-permute-start | bytes 589832 | tf_op jit(solution)/shard_map/ppermute | solution.py:48
  466.2 23.6 %collective-permute-start.44 = (bf16[256,384]{1,0:T(8,128)(2,1)S(1)}, bf16[256,384]{1,0:T(8,128)(2,1)S(1)}, u32[]{:S(2)}, u32[]{:S(2)}) collective-permute-start(bf16[256,384]{1,0:T(8,128)(2,1)S(1)} %get-tuple-element.115), channel_id=1, source_target_pairs={{0,1},{1,2},{2,3},{3,0},{4,5},{5,6},{6,7},{7,4},{8,9},{9,10},{10,1... | collective-permute-start | bytes 589832 | tf_op jit(solution)/shard_map/ppermute | solution.py:48
  467.6 24.6 %collective-permute-start.55 = (f32[128,128]{0,1:T(8,128)S(1)}, f32[128,128]{0,1:T(8,128)S(1)}, u32[]{:S(2)}, u32[]{:S(2)}) collective-permute-start(f32[128,128]{0,1:T(8,128)S(1)} %get-tuple-element.143), channel_id=1, source_target_pairs={{0,4},{4,0},{8,12},{12,8},{16,20},{20,16},{24,28},{28,24},{1,5},{5... | collective-permute-start | bytes 196616 | tf_op jit(solution)/shard_map/ppermute | solution.py:39
  (55 other events, 415.8 us)

commit v2 on v1

--- a/solution.py
+++ b/solution.py
@@ -62,105 +62,143 @@
     return (lax.axis_size("dp") // 2).bit_length() - 1
 
 
-def gather_chips(line, split):
-    bits = chip_bits()
-    if bits == 2:
-        along = swap_bit(line, 1)
-        across = swap_bit(line, 2)
-        far_top = swap_bit(along[:split], 2)
-        far_low = swap_bit(across[split:], 1)
-        return [
-            [line[:split], line[split:]],
-            [along[:split], along[split:]],
-            [across[:split], across[split:]],
-            [far_top, far_low],
-        ]
-    held = line[None]
-    for bit in range(bits):
-        held = jnp.concatenate([held, swap_bit(held, bit + 1)], axis=0)
-    return [[held[r, :split], held[r, split:]] for r in range(1 << bits)]
-
-
-def scatter_chips(grad, rows, split):
-    bits = chip_bits()
-    if bits == 2:
-        block = [grad[r * rows : (r + 1) * rows] for r in range(4)]
-        far_top = swap_bit(block[3][:split], 2)
-        far_low = swap_bit(block[3][split:], 1)
-        top = (block[1][:split].astype(F32) + far_top.astype(F32)).astype(BF)
-        low = (block[2][split:].astype(F32) + far_low.astype(F32)).astype(BF)
-        along = swap_bit(jnp.concatenate([top, block[1][split:]], axis=0), 1)
-        across = swap_bit(jnp.concatenate([block[2][:split], low], axis=0), 2)
-        return block[0].astype(F32) + along.astype(F32) + across.astype(F32)
-    held = grad.reshape(-1, rows, grad.shape[1])
-    for bit in range(bits)[::-1]:
-        half = held.shape[0] // 2
-        got = swap_bit(held[half:], bit + 1)
-        held = (held[:half].astype(F32) + got.astype(F32)).astype(BF)
-    return held[0].astype(F32)
-
-
-def gather_weights(piece, widths, extra=None):
-    size = lax.axis_size("tensor")
-    rows = piece.shape[0]
-    mine = piece if extra is None else jnp.concatenate([piece, extra], axis=0)
-    turned = [mine] + [from_tensor(mine, k) for k in range(1, size)]
+def tie(*values):
+    return lax.optimization_barrier(values)
+
+
+def gather_line(piece, widths, turned, extra_rows=0):
+    rows = piece.shape[0] - extra_rows
+    turned = [piece] + list(turned)
     cols, at = [], 0
     for width in widths:
         cols += [t[:rows, at : at + width] for t in turned]
         at += width
     line = jnp.concatenate(cols, axis=1)
-    if extra is not None:
+    if extra_rows:
         added = functools.reduce(jnp.add, [t[rows:] for t in turned])
         added = jnp.pad(added, ((0, 0), (0, line.shape[1] - added.shape[1])))
         line = jnp.concatenate([line, added], axis=0)
-    got = gather_chips(line, rows // 2)
+    return line
+
+
+def exchange(*moves):
+    values = lax.optimization_barrier(tuple(v for _, v in moves))
+    return lax.optimization_barrier(tuple(move(v) for (move, _), v in zip(moves, values)))
+
+
+def by_bit(bit):
+    return functools.partial(swap_bit, bit=bit)
+
+
+def by_tensor(step):
+    return functools.partial(from_tensor, step=step)
+
+
+def along_tensor(piece):
+    return [(by_tensor(k), piece) for k in range(1, lax.axis_size("tensor"))]
+
+
+def gather_near(line):
+    return [(by_bit(1), line), (by_bit(2), line)] if chip_bits() == 2 else []
+
+
+def gather_far(near, split):
+    return [(by_bit(2), near[0][:split]), (by_bit(1), near[1][split:])] if chip_bits() == 2 else []
+
+
+def gathered(line, near, far, split):
+    if chip_bits() == 2:
+        return [[v[:split], v[split:]] for v in (line, *near)] + [list(far)]
+    held = line[None]
+    for bit in range(chip_bits()):
+        held = jnp.concatenate([held, swap_bit(held, bit + 1)], axis=0)
+    return [[held[r, :split], held[r, split:]] for r in range(held.shape[0])]
+
+
+def join_chips(got, widths, rows):
+    size = lax.axis_size("tensor")
     out, at = [], 0
     for width in widths:
         cut = slice(at, at + size * width)
         out.append(jnp.concatenate([part for top, low in got for part in (top[:, cut], low[: rows - rows // 2, cut])]))
         at += size * width
-    table = None
-    if extra is not None:
-        table = jnp.stack([low[rows - rows // 2 :, : extra.shape[1]] for _, low in got])
-    return out, table
-
-
-def scatter_grads(grad, core):
+    return out
+
+
+def take(grads, low, high):
+    return jnp.concatenate([g[low:high] for g in grads], axis=1) if len(grads) > 1 else grads[0][low:high]
+
+
+def low_half(rows, r, grads, extra):
+    low = take(grads, r * rows + rows // 2, (r + 1) * rows)
+    return low if extra is None else jnp.concatenate([low, extra[r * 16 : (r + 1) * 16]], axis=0)
+
+
+def scatter_far(rows, *grads, extra=None):
+    if chip_bits() != 2:
+        return []
+    return [(by_bit(2), take(grads, 3 * rows, 3 * rows + rows // 2)), (by_bit(1), low_half(rows, 3, grads, extra))]
+
+
+def scatter_near(rows, far, *grads, extra=None):
+    if chip_bits() != 2:
+        return []
+    split = rows // 2
+    top = (take(grads, rows, rows + split).astype(F32) + far[0].astype(F32)).astype(BF)
+    low = (low_half(rows, 2, grads, extra).astype(F32) + far[1].astype(F32)).astype(BF)
+    return [
+        (by_bit(1), jnp.concatenate([top, low_half(rows, 1, grads, extra)], axis=0)),
+        (by_bit(2), jnp.concatenate([take(grads, 2 * rows, 2 * rows + split), low], axis=0)),
+    ]
+
+
+def scattered(rows, near, *grads, extra=None):
+    if chip_bits() == 2:
+        own = jnp.concatenate([take(grads, 0, rows // 2), low_half(rows, 0, grads, extra)], axis=0)
+        return own.astype(F32) + near[0].astype(F32) + near[1].astype(F32)
+    grad = take(grads, 0, grads[0].shape[0])
+    held = grad.reshape(-1, rows, grad.shape[1])
+    for bit in range(chip_bits())[::-1]:
+        half = held.shape[0] // 2
+        got = swap_bit(held[half:], bit + 1)
+        held = (held[:half].astype(F32) + got.astype(F32)).astype(BF)
+    return held[0].astype(F32)
+
+
+def scatter_tensor(blocks):
     size = lax.axis_size("tensor")
-    rows = grad.shape[0] // (lax.axis_size("dp") // 2)
-    width = grad.shape[1] // size
-    line = scatter_chips(grad, rows, rows // 2)
-    total = line[:, :width]
-    for k in range(1, size):
-        part = line[:, k * width : (k + 1) * width].astype(BF)
-        total = total + from_tensor(part, size - k).astype(F32)
-    half = rows // 2
-    keep = lax.dynamic_slice_in_dim(total, core * half, half, 0)
-    give = lax.dynamic_slice_in_dim(total, (1 - core) * half, half, 0)
-    got = swap_core(give)
-    return jnp.where(core == 0, jnp.stack([keep, got], 1), jnp.stack([got, keep], 1))
+    return [(by_tensor(size - k), blocks[k].astype(BF)) for k in range(1, size)]
+
+
+def cut_blocks(line):
+    size = lax.axis_size("tensor")
+    width = line.shape[1] // size
+    return [line[:, k * width : (k + 1) * width] for k in range(size)]
+
+
+def scatter_total(blocks, got):
+    return functools.reduce(jnp.add, [part.astype(F32) for part in (blocks[0], *got)])
+
+
+def core_rows(values, core):
+    half = values.shape[0] // 2
+    keep = lax.dynamic_slice_in_dim(values, core * half, half, 0)
+    return keep, lax.dynamic_slice_in_dim(values, (1 - core) * half, half, 0)
+
+
+def by_core(keep, back, core):
+    return jnp.where(core == 0, jnp.stack([keep, back], 1), jnp.stack([back, keep], 1))
 
 
 def both_halves(mine, other, core):
     return jnp.concatenate([jnp.where(core == 0, mine, other), jnp.where(core == 0, other, mine)], axis=0)
 
 
-def to_sequence(mine, core, keeps):
-    here = jnp.where(keeps, mine, swap_pair(mine))
-    return both_halves(here, swap_core(here), core)
-
-
-def from_sequence(left, weight, core):
-    half = left.shape[0] // 2
-    give = lax.dynamic_slice_in_dim(left, (1 - core) * half, half, 0)
-    got = swap_core(dot_nt(give, weight).astype(BF))
-    own = dot_nt(lax.dynamic_slice_in_dim(left, core * half, half, 0), weight)
-    here = (own + got.astype(F32)).astype(BF)
-    return here, swap_pair(here)
-
-
 BLOCK_Q = 256
+
+
+def cost(microseconds):
+    return pl.CostEstimate(flops=int(microseconds * 1.1e9), bytes_accessed=int(microseconds * 1e6), transcendentals=0)
 
 
 def biased_pair(q, k, slope_ref, group, head):
@@ -184,8 +222,9 @@
     return keys <= lax.broadcasted_iota(jnp.int32, (size, size), 1)
 
 
-def attend_kernel(slope_ref, qkv_ref, ctx_ref, lse_ref):
-    group = pl.program_id(0)
+def attend_kernel(start, slope_ref, qkv_ref, *refs):
+    ctx_ref, lse_ref = refs[-2:]
+    group = pl.program_id(0) + start
     wide = 2 * HD
     seq = qkv_ref.shape[0]
     size = min(BLOCK_Q, seq)
@@ -216,16 +255,17 @@
         ctx_ref[lo:hi, :] = jnp.concatenate(outs, axis=0).T.astype(BF)
 
 
-def attend(qkv, slopes):
-    seq, groups = qkv.shape[0], slopes.shape[0]
+def attend(qkv, slopes, first, groups, *earlier):
+    seq = qkv.shape[0]
     wide = 2 * HD
     return pl.pallas_call(
-        attend_kernel,
+        functools.partial(attend_kernel, first),
         grid=(groups,),
         in_specs=[
             pl.BlockSpec(memory_space=pltpu.SMEM),
-            pl.BlockSpec((seq, 3 * wide), lambda g: (0, g)),
-        ],
+            pl.BlockSpec((seq, 3 * wide), lambda g: (0, g + first)),
+        ]
+        + [pl.BlockSpec(memory_space=pl.ANY)] * len(earlier),
         out_specs=[
             pl.BlockSpec((seq, wide), lambda g: (0, g)),
             pl.BlockSpec((1, 2, seq), lambda g: (g, 0, 0)),
@@ -235,15 +275,14 @@
             jax.ShapeDtypeStruct((groups, 2, seq), F32),
         ],
         compiler_params=pltpu.CompilerParams(vmem_limit_bytes=48 * 1024 * 1024),
-        cost_estimate=pl.CostEstimate(
-            flops=groups * 2 * seq * seq * HD * 4, bytes_accessed=qkv.size * 2 * 2, transcendentals=groups * seq * seq
-        ),
+        cost_estimate=cost(9),
         name="attend",
-    )(slopes, qkv)
-
-
-def attend_back_kernel(slope_ref, qkv_ref, grad_ref, lse_ref, out_ref, bias_ref, dk_ref, dv_ref):
-    group = pl.program_id(0)
+    )(slopes, qkv, *earlier)
+
+
+def attend_back_kernel(start, slope_ref, qkv_ref, grad_ref, lse_ref, *refs):
+    out_ref, bias_ref, dk_ref, dv_ref = refs[-4:]
+    group = pl.program_id(0) + start
     wide = 2 * HD
     seq = qkv_ref.shape[0]
     size = min(BLOCK_Q, seq)
@@ -286,33 +325,32 @@
     bias_ref[0, :, 2 * wide :] = jnp.sum(dv.astype(F32), axis=0, keepdims=True)
 
 
-def attend_back(qkv, slopes, lse, grad_ctx):
-    seq, groups = qkv.shape[0], slopes.shape[0]
+def attend_back(qkv, slopes, lse, grad_ctx, first, groups, *earlier):
+    seq = qkv.shape[0]
     wide = 2 * HD
     return pl.pallas_call(
-        attend_back_kernel,
+        functools.partial(attend_back_kernel, first),
         grid=(groups,),
         in_specs=[
             pl.BlockSpec(memory_space=pltpu.SMEM),
-            pl.BlockSpec((seq, 3 * wide), lambda g: (0, g)),
-            pl.BlockSpec((seq, wide), lambda g: (0, g)),
+            pl.BlockSpec((seq, 3 * wide), lambda g: (0, g + first)),
+            pl.BlockSpec((seq, wide), lambda g: (0, g + first)),
             pl.BlockSpec((1, 2, seq), lambda g: (g, 0, 0)),
-        ],
+        ]
+        + [pl.BlockSpec(memory_space=pl.ANY)] * len(earlier),
         out_specs=[
             pl.BlockSpec((seq, 3 * wide), lambda g: (0, g)),
             pl.BlockSpec((1, 1, 3 * wide), lambda g: (g, 0, 0)),
         ],
         out_shape=[
-            jax.ShapeDtypeStruct(qkv.shape, BF),
+            jax.ShapeDtypeStruct((seq, groups * 3 * wide), BF),
             jax.ShapeDtypeStruct((groups, 1, 3 * wide), F32),
         ],
         scratch_shapes=[pltpu.VMEM((seq, wide), F32), pltpu.VMEM((seq, wide), F32)],
         compiler_params=pltpu.CompilerParams(vmem_limit_bytes=48 * 1024 * 1024),
-        cost_estimate=pl.CostEstimate(
-            flops=groups * 2 * seq * seq * HD * 10, bytes_accessed=qkv.size * 2 * 3, transcendentals=groups * seq * seq
-        ),
+        cost_estimate=cost(11),
         name="attend_back",
-    )(slopes, qkv, grad_ctx, lse)
+    )(slopes, qkv, grad_ctx, lse, *earlier)
 
 
 VMEM_LIMIT = 48 * 1024 * 1024
@@ -374,65 +412,80 @@
         out_specs=[tile] * len(outs) + ([one] if sums else []),
         out_shape=shapes,
         compiler_params=pltpu.CompilerParams(vmem_limit_bytes=VMEM_LIMIT),
-        cost_estimate=pl.CostEstimate(flops=tokens * width * 10, bytes_accessed=moved, transcendentals=0),
+        cost_estimate=cost(3),
         name=name,
     )(ids, *rows, *wholes)
 
 
-def rows_first(chips, mixed, ids, hidden):
-    def body(ids_ref, x_ref, z_ref):
-        z_ref[...] = centre(read_mixed(x_ref, ids_ref, chips, mixed))[0].astype(BF)
-
-    return row_call(body, "rows_first", ids, [hidden], [], [BF], False)[0]
-
-
-def rows_cot(chips, mixed, ids, cot):
-    def body(ids_ref, x_ref, low_ref, sum_ref):
+def chosen(own, swapped_ref, ids_ref):
+    return jnp.where(ids_ref[3] == 1, own, swapped_ref[...].astype(F32))
+
+
+def rows_low(chips, mixed, ids, values, sums):
+    def body(ids_ref, x_ref, low_ref, *sum_refs):
         x = read_mixed(x_ref, ids_ref, chips, mixed)
         low_ref[...] = x.astype(BF)
-        add_sums(sum_ref, [x])
-
-    return row_call(body, "rows_cot", ids, [cot], [], [BF], True)
-
-
-def rows_mid(chips, mixed, ids, hidden, here, swapped, vec):
-    def body(ids_ref, x_ref, here_ref, swapped_ref, vec_ref, res_ref, norm_ref):
-        added = jnp.where(ids_ref[3] == 1, here_ref[...].astype(F32), swapped_ref[...].astype(F32))
-        res = read_mixed(x_ref, ids_ref, chips, mixed) + added + vec_ref[2:3, :]
+        if sums:
+            add_sums(sum_refs[0], [x])
+
+    return row_call(body, "rows_low", ids, [values], [], [BF], sums)
+
+
+def rows_first(chips, mixed, ids, hidden, swapped):
+    def body(ids_ref, x_ref, swapped_ref, here_ref, z_ref):
+        x = chosen(read_mixed(x_ref, ids_ref, chips, mixed), swapped_ref, ids_ref)
+        here_ref[...] = x
+        z_ref[...] = centre(x)[0].astype(BF)
+
+    return row_call(body, "rows_first", ids, [hidden, swapped], [], [F32, BF], False)
+
+
+def rows_mid(ids, hidden, added, vec):
+    def body(ids_ref, x_ref, added_ref, vec_ref, res_ref, norm_ref):
+        res = x_ref[...] + added_ref[...].astype(F32) + vec_ref[2:3, :]
         res_ref[...] = res
         norm_ref[...] = (centre(res)[0] * vec_ref[3:4, :] + vec_ref[4:5, :]).astype(BF)
 
-    return row_call(body, "rows_mid", ids, [hidden, here, swapped], [vec], [F32, BF], False)
-
-
-def rows_out(chips, mixed, ids, residual, own, got, vec):
-    def body(ids_ref, res_ref, own_ref, got_ref, vec_ref, out_ref):
+    return row_call(body, "rows_mid", ids, [hidden, added], [vec], [F32, BF], False)
+
+
+def rows_out(ids, residual, own, got, vec):
+    def body(ids_ref, res_ref, own_ref, got_ref, vec_ref, out_ref, low_ref):
         out = res_ref[...] + (own_ref[...] + got_ref[...].astype(F32)) + vec_ref[5:6, :]
-        write_mixed(out_ref, out, ids_ref, chips, mixed)
-
-    return row_call(body, "rows_out", ids, [residual, own, got], [vec], [F32], False)[0]
-
-
-def rows_mid_back(chips, mixed, ids, cot, residual, own, got, vec):
-    def body(ids_ref, cot_ref, res_ref, own_ref, got_ref, vec_ref, grad_ref, low_ref, sum_ref):
+        out_ref[...] = out
+        low_ref[...] = out.astype(BF)
+
+    return row_call(body, "rows_out", ids, [residual, own, got], [vec], [F32, BF], False)
+
+
+def rows_mid_back(chips, mixed, ids, cot, swapped, residual, own, got, vec):
+    def body(ids_ref, cot_ref, swapped_ref, res_ref, own_ref, got_ref, vec_ref, grad_ref, low_ref, sum_ref):
         z, inv = centre(res_ref[...])
         grad = own_ref[...] + got_ref[...].astype(F32)
-        mid = read_mixed(cot_ref, ids_ref, chips, mixed) + norm_back(grad, vec_ref[3:4, :], z, inv)
+        above = chosen(read_mixed(cot_ref, ids_ref, chips, mixed), swapped_ref, ids_ref)
+        mid = above + norm_back(grad, vec_ref[3:4, :], z, inv)
         grad_ref[...] = mid
         low_ref[...] = mid.astype(BF)
         add_sums(sum_ref, [grad * z, grad, mid])
 
-    return row_call(body, "rows_mid_back", ids, [cot, residual, own, got], [vec], [F32, BF], True)
-
-
-def rows_first_back(chips, mixed, ids, hidden, grad_mid, here, swapped, vec):
-    def body(ids_ref, x_ref, mid_ref, here_ref, swapped_ref, vec_ref, out_ref):
-        z, inv = centre(read_mixed(x_ref, ids_ref, chips, mixed))
-        grad = jnp.where(ids_ref[3] == 1, here_ref[...].astype(F32), swapped_ref[...].astype(F32))
-        out = mid_ref[...] + norm_back(grad, vec_ref[0:1, :], z, inv)
-        write_mixed(out_ref, out, ids_ref, chips, mixed)
-
-    return row_call(body, "rows_first_back", ids, [hidden, grad_mid, here, swapped], [vec], [F32], False)[0]
+    return row_call(body, "rows_mid_back", ids, [cot, swapped, residual, own, got], [vec], [F32, BF], True)
+
+
+def rows_first_back(ids, hidden, grad_mid, own, got, vec):
+    def body(ids_ref, x_ref, mid_ref, own_ref, got_ref, vec_ref, out_ref, low_ref):
+        z, inv = centre(x_ref[...])
+        out = mid_ref[...] + norm_back(own_ref[...] + got_ref[...].astype(F32), vec_ref[0:1, :], z, inv)
+        out_ref[...] = out
+        low_ref[...] = out.astype(BF)
+
+    return row_call(body, "rows_first_back", ids, [hidden, grad_mid, own, got], [vec], [F32, BF], False)
+
+
+def rows_home(chips, mixed, ids, here, swapped):
+    def body(ids_ref, here_ref, swapped_ref, out_ref):
+        write_mixed(out_ref, chosen(here_ref[...], swapped_ref, ids_ref), ids_ref, chips, mixed)
+
+    return row_call(body, "rows_home", ids, [here, swapped], [], [F32], False)[0]
 
 
 class Plan:
@@ -502,7 +555,7 @@
             jax.ShapeDtypeStruct((1, plan.n_u), F32),
         ],
         compiler_params=pltpu.CompilerParams(vmem_limit_bytes=VMEM_LIMIT),
-        cost_estimate=pl.CostEstimate(flops=10**8, bytes_accessed=10**5, transcendentals=0),
+        cost_estimate=cost(2),
         name="spread_small",
     )(ids, table)
 
@@ -539,8 +592,44 @@
         in_specs=[pl.BlockSpec(memory_space=pltpu.SMEM)] + [pl.BlockSpec(memory_space=pltpu.VMEM)] * 4,
         out_shape=jax.ShapeDtypeStruct((-(-lines // 8) * 8, width), F32),
         compiler_params=pltpu.CompilerParams(vmem_limit_bytes=VMEM_LIMIT),
-        cost_estimate=pl.CostEstimate(flops=10**6, bytes_accessed=10**5, transcendentals=0),
+        cost_estimate=cost(1),
         name="pack_small",
+    )(ids, mid_sums, cot_sums, bias_q, bias_u)
+
+
+def pack_rows(plan, ids, width, mid_sums, cot_sums, bias_q, bias_u):
+    size, chips = plan.size, plan.chips
+
+    def body(ids_ref, mid_ref, cot_ref, bq_ref, bu_ref, out_ref):
+        chip, core, tensor = ids_ref[0], ids_ref[1], ids_ref[2]
+
+        def put(where_, values):
+            n = values.shape[1]
+            r, c, t, place = where_(lax.broadcasted_iota(jnp.int32, (1, n), 1))
+            hot = lax.broadcasted_iota(jnp.int32, (width, n), 0) == place
+            row = (r * 2 + c) * size + (t - tensor + size) % size
+            at = lax.broadcasted_iota(jnp.int32, (chips * 2 * size, n), 0) == row
+            return dot_nt(jnp.where(at, values, 0.0).astype(BF), jnp.where(hot, 1.0, 0.0).astype(BF))
+
+        rows = [mid_ref[3:4, :], mid_ref[4:5, :], mid_ref[2:3, :], mid_ref[0:1, :], mid_ref[1:2, :], cot_ref[0:1, :]]
+        total = put(lambda n: plan.query(n, chip, core, tensor), bq_ref[...])
+        total = total + put(lambda n: plan.up(n, chip, core, tensor), bu_ref[...])
+        for v, row in enumerate(rows):
+            total = total + put(functools.partial(plan.vector, v), row)
+        for r in range(chips):
+            lines = [
+                jnp.concatenate([total[(r * 2 + c) * size + k :][:1] for k in range(size)], axis=1) for c in range(2)
+            ]
+            lines.append(jnp.zeros((14, size * width), F32))
+            out_ref[r * 16 : (r + 1) * 16, :] = jnp.concatenate(lines, axis=0).astype(BF)
+
+    return pl.pallas_call(
+        body,
+        in_specs=[pl.BlockSpec(memory_space=pltpu.SMEM)] + [pl.BlockSpec(memory_space=pltpu.VMEM)] * 4,
+        out_shape=jax.ShapeDtypeStruct((chips * 16, size * width), BF),
+        compiler_params=pltpu.CompilerParams(vmem_limit_bytes=VMEM_LIMIT),
+        cost_estimate=cost(2),
+        name="pack_rows",
     )(ids, mid_sums, cot_sums, bias_q, bias_u)
 
 
@@ -558,12 +647,13 @@
     return [vectors[i] for i in range(6)], q, u
 
 
-def qkv_grads(seq_one, grad_qkv, w_qkv, colsum, vec_t):
+def qkv_grads(seq_one, grad_qkv, w_qkv, part, colsum, vec_t, *earlier):
     seq, d_model = seq_one.shape
     width = grad_qkv.shape[1]
     step = min(256, d_model)
 
-    def body(z_ref, grad_ref, w_ref, col_ref, vec_ref, out_ref, sum_ref):
+    def body(z_ref, grad_ref, w_ref, col_ref, vec_ref, *refs):
+        out_ref, sum_ref = refs[-2:]
         g = lax.dot_general(z_ref[...], grad_ref[...], (((0,), (0,)), ((), ())), preferred_element_type=F32)
         w = w_ref[...].astype(F32)
         col = col_ref[...]
@@ -579,18 +669,17 @@
         in_specs=[
             pl.BlockSpec((seq, step), lambda i: (0, i)),
             pl.BlockSpec((seq, width), lambda i: (0, 0)),
-            pl.BlockSpec((step, width), lambda i: (i, 0)),
+            pl.BlockSpec((step, width), lambda i: (i, part)),
             pl.BlockSpec((1, width), lambda i: (0, 0)),
             pl.BlockSpec((step, 128), lambda i: (i, 0)),
-        ],
+        ]
+        + [pl.BlockSpec(memory_space=pl.ANY)] * len(earlier),
         out_specs=[pl.BlockSpec((step, width), lambda i: (i, 0)), pl.BlockSpec((8, step), lambda i: (0, i))],
         out_shape=[jax.ShapeDtypeStruct((d_model, width), BF), jax.ShapeDtypeStruct((8, d_model), F32)],
         compiler_params=pltpu.CompilerParams(vmem_limit_bytes=VMEM_LIMIT),
-        cost_estimate=pl.CostEstimate(
-            flops=2 * seq * d_model * width, bytes_accessed=2 * (seq + 2 * d_model) * width, transcendentals=0
-        ),
+        cost_estimate=cost(5),
         name="qkv_grads",
-    )(seq_one, grad_qkv, w_qkv, colsum, vec_t)
+    )(seq_one, grad_qkv, w_qkv, colsum, vec_t, *earlier)
 
 
 def split_weights(ids, w_qkv, w_out, w_up, w_down):
@@ -616,14 +705,92 @@
         in_specs=[pl.BlockSpec(memory_space=pltpu.SMEM)] + [pl.BlockSpec(memory_space=pltpu.VMEM)] * 4,
         out_shape=[jax.ShapeDtypeStruct((rows, width), BF)] * 2,
         compiler_params=pltpu.CompilerParams(vmem_limit_bytes=VMEM_LIMIT),
-        cost_estimate=pl.CostEstimate(flops=0, bytes_accessed=rows * width * 8, transcendentals=0),
+        cost_estimate=cost(2),
         name="split_weights",
     )(ids, w_qkv, w_out, w_up, w_down)
+
+
+def up_forward(rows, weight, bias):
+    count, depth = rows.shape
+    width = weight.shape[1]
+    step = min(256, width)
+
+    def body(x_ref, w_ref, b_ref, act_ref, slope_ref):
+        u = dot_nn(x_ref[...], w_ref[...]) + b_ref[...]
+        square = u * u
+        inner = u * (0.7978845608028654 + (0.7978845608028654 * 0.044715) * square)
+        t = jnp.tanh(inner)
+        half = 0.5 + 0.5 * t
+        act_ref[...] = (u * half).astype(BF)
+        rise = 0.7978845608028654 + (3 * 0.7978845608028654 * 0.044715) * square
+        slope_ref[...] = (half + (0.5 * u) * (1.0 - t * t) * rise).astype(BF)
+
+    tile = pl.BlockSpec((count, step), lambda i: (0, i))
+    return pl.pallas_call(
+        body,
+        grid=(width // step,),
+        in_specs=[
+            pl.BlockSpec((count, depth), lambda i: (0, 0)),
+            pl.BlockSpec((depth, step), lambda i: (0, i)),
+            pl.BlockSpec((1, step), lambda i: (0, i)),
+        ],
+        out_specs=[tile, tile],
+        out_shape=[jax.ShapeDtypeStruct((count, width), BF)] * 2,
+        compiler_params=pltpu.CompilerParams(vmem_limit_bytes=VMEM_LIMIT),
+        cost_estimate=cost(12),
+        name="up_forward",
+    )(rows, weight, bias)
+
+
+def up_backward(cot_rows, weight, slope):
+    count, depth = cot_rows.shape
+    width = weight.shape[1]
+    step = min(256, width)
+
+    def body(x_ref, w_ref, slope_ref, out_ref, sum_ref):
+        grad = (dot_nn(x_ref[...], w_ref[...]) * slope_ref[...].astype(F32)).astype(BF)
+        out_ref[...] = grad
+        sum_ref[...] = jnp.sum(grad.astype(F32), axis=0, keepdims=True)
+
+    tile = pl.BlockSpec((count, step), lambda i: (0, i))
+    return pl.pallas_call(
+        body,
+        grid=(width // step,),
+        in_specs=[
+            pl.BlockSpec((count, depth), lambda i: (0, 0)),
+            pl.BlockSpec((depth, step), lambda i: (0, i)),
+            tile,
+        ],
+        out_specs=[tile, pl.BlockSpec((1, step), lambda i: (0, i))],
+        out_shape=[jax.ShapeDtypeStruct((count, width), BF), jax.ShapeDtypeStruct((1, width), F32)],
+        compiler_params=pltpu.CompilerParams(vmem_limit_bytes=VMEM_LIMIT),
+        cost_estimate=cost(10),
+        name="up_backward",
+    )(cot_rows, weight, slope)
 
 
 def swap_blocks(values, bit, block):
     count = values.shape[1] // block
     return jnp.concatenate([values[:, (r ^ (1 << bit)) * block : ((r ^ (1 << bit)) + 1) * block] for r in range(count)], axis=1)
+
+
+def add_chips_moves(total):
+    if chip_bits() != 2:
+        return []
+    far = lambda v: lax.ppermute(v, "dp", [(i, i ^ 6) for i in range(lax.axis_size("dp"))])
+    return [(by_bit(1), total), (by_bit(2), total), (far, total)]
+
+
+def add_chips(total, got, block):
+    if chip_bits() == 2:
+        terms = [total, *got]
+        vectors = functools.reduce(jnp.add, [t[:8, r * block : (r + 1) * block] for r, t in enumerate(terms)])
+        vectors = jnp.pad(vectors, ((0, 0), (0, total.shape[1] - block)))
+        return jnp.concatenate([vectors, functools.reduce(jnp.add, [t[8:] for t in terms])], axis=0)
+    for bit in range(chip_bits()):
+        got = swap_bit(total, bit + 1)
+        total = total + jnp.concatenate([swap_blocks(got[:8], bit, block), got[8:]], axis=0)
+    return total
 
 
 def local(
@@ -668,11 +835,7 @@
         )
 
     wide = [qkv_weight.shape[1] // 2, out_weight.shape[0] // 2, up_weight.shape[1] // 2, down_weight.shape[0] // 2]
-    packed = jnp.concatenate(
-        [v.reshape(-1) for v in (ln1_gain, ln1_bias, out_bias, ln2_gain, ln2_bias, down_bias, qkv_bias, up_bias)]
-    )
     pack = wide[0]
-    packed = jnp.pad(packed, (0, pack - packed.shape[0])).reshape(1, pack)
     if mixed:
         own, give = split_weights(ids, qkv_weight, out_weight, up_weight, down_weight)
     else:
@@ -681,73 +844,155 @@
         loc = jnp.concatenate(parts, axis=2).transpose(1, 0, 2)
         own = lax.dynamic_index_in_dim(loc, core, 0, keepdims=False)
         give = lax.dynamic_index_in_dim(loc, 1 - core, 0, keepdims=False)
-    other_pack = swap_core(packed)
-    piece = both_halves(own, swap_core(give), core)
+    packed = jnp.concatenate(
+        [v.reshape(-1) for v in (ln1_gain, ln1_bias, out_bias, ln2_gain, ln2_bias, down_bias, qkv_bias, up_bias)]
+    )
+    packed = jnp.pad(packed, (0, pack - packed.shape[0])).reshape(1, pack)
     slot = jnp.arange(16)[:, None]
     extra = jnp.where(slot == core * size + tensor, packed, jnp.zeros_like(packed))
-    extra = jnp.where(slot == (1 - core) * size + tensor, other_pack, extra)
-
-    hidden = relative(hidden_in)
-    z_one = rows_first(chips, mixed, ids, hidden)
-    seq_one = to_sequence(z_one, core, keeps)
-    (w_qkv,), table = gather_weights(piece[:, : wide[0]], wide[:1], extra)
-    table = table.reshape(chips, 16, pack)[:, : 2 * size].reshape(chips * 2 * size, pack)
-    vec, b_qkv, b_up = spread_small(plan, ids, table)
-    (w_out_t, w_up), _ = gather_weights(piece[:, wide[0] : wide[0] + wide[1] + wide[2]], wide[1:3])
-    (w_down_t,), _ = gather_weights(piece[:, wide[0] + wide[1] + wide[2] :], wide[3:])
-    cot = relative(cotangent)
-    cot_low, cot_sums = rows_cot(chips, mixed, ids, cot)
-    cot_rows = jnp.concatenate([cot_low, swap_core(cot_low)], axis=0)
-
+    other = swap_core(give)
+    extra = extra + swap_core(extra)
+    piece = both_halves(own, other, core)
+    at = [0]
+    for w in wide:
+        at.append(at[-1] + w)
+    extra = jnp.pad(extra, ((0, 0), (0, at[2] - pack)))
+    piece_q = jnp.concatenate([piece[:, : at[2]], extra], axis=0)
+    piece_u, piece_d = piece[:, at[2] : at[3]], piece[:, at[3] :]
+    block_rows = piece.shape[0]
+    split = block_rows // 2
+
+    hidden, cot = relative(hidden_in), relative(cotangent)
+    got_q = exchange(*along_tensor(piece_q))
+    (hidden_low,) = rows_low(chips, mixed, ids, hidden, False)
+    cot_low, cot_sums = rows_low(chips, mixed, ids, cot, True)
+    *got_q, hidden_low, cot_low = tie(*got_q, hidden_low, cot_low)
+    line_q = gather_line(piece_q, wide[:2], got_q, 16)
+    line_q, piece_u = tie(line_q, piece_u)
+    near = gather_near(line_q)
+    swapped_in = swap_pair(hidden_low)
+    got = exchange(*near, *along_tensor(piece_u))
+    near_q, got_u = got[: len(near)], got[len(near) :]
+    here_in, z_one = rows_first(chips, mixed, ids, hidden, swapped_in)
+    far = gather_far(near_q, split)
+    got = exchange(*far, (swap_pair, cot_low), (swap_core, z_one))
+    far_q, swapped_cot, other_one = got[: len(far)], got[-2], got[-1]
+    seq_one = both_halves(z_one, other_one, core)
+
+    *got_u, swapped_cot = tie(*got_u, swapped_cot)
+    line_u = gather_line(piece_u, wide[2:3], got_u)
+    near = gather_near(line_u)
+    line_u, piece_d = tie(line_u, piece_d)
+    near_u = exchange(*near) if near else ()
+    got_d = exchange(*along_tensor(piece_d))
+    here_cot = jnp.where(keeps, cot_low, swapped_cot)
+    cot_rows = jnp.concatenate([here_cot, swap_core(here_cot)], axis=0)
+
+    parts = gathered(line_q, near_q, far_q, split)
+    w_qkv, w_out_t = join_chips(parts, wide[:2], block_rows)
+    table = jnp.stack([low[block_rows - split :, :pack] for _, low in parts])[:, : 2 * size]
+    vec, b_qkv, b_up = spread_small(plan, ids, table.reshape(chips * 2 * size, pack))
     head_ids = ((tensor + jnp.arange(size)) % size)[:, None] * heads_here + core * pair + jnp.arange(pair)[None]
     slopes = jnp.exp2(-8.0 * (head_ids + 1).astype(F32) / H)
-
     rows_one = (seq_one.astype(F32) * vec[0:1] + vec[1:2]).astype(BF)
     qkv = (dot_nn(rows_one, w_qkv) + b_qkv).astype(BF)
-    context, lse = attend(qkv, slopes)
-    here, swapped = from_sequence(context, w_out_t, core)
-    residual, norm_two = rows_mid(chips, mixed, ids, hidden, here, swapped, vec)
-
-    rows_two = jnp.concatenate([norm_two, swap_core(norm_two)], axis=0)
-    up_pre = dot_nn(rows_two, w_up) + b_up
-    active = gelu_tanh(up_pre).astype(BF)
+    context, lse = attend(qkv, slopes, 0, size, got_d[0])
+    own, give = core_rows(context, core)
+    far_u = exchange(*gather_far(near_u, split)) if near_u else ()
+    line_d = gather_line(piece_d, wide[3:], got_d)
+    got_here = swap_core(dot_nt(give, w_out_t).astype(BF))
+    here = (dot_nt(own, w_out_t) + got_here.astype(F32)).astype(BF)
+    near_d = exchange(*gather_near(line_d)) if near_u else ()
+    (w_up,) = join_chips(gathered(line_u, near_u, far_u, split), wide[2:3], block_rows)
+    residual, norm_two = rows_mid(ids, here_in, here, vec)
+    norm_other = swap_core(norm_two)
+    rows_two = jnp.concatenate([norm_two, norm_other], axis=0)
+    active, slope = up_forward(rows_two, w_up, b_up)
+    far_d = exchange(*gather_far(near_d, split)) if near_d else ()
+    g_down_t = dot_tn(cot_rows, active).astype(BF)
+    (w_down_t,) = join_chips(gathered(line_d, near_d, far_d, split), wide[3:], block_rows)
+
+    moves = scatter_far(block_rows, g_down_t)
+    far_gd = exchange(*moves) if moves else ()
+    grad_pre, grad_b_up = up_backward(cot_rows, w_down_t, slope)
+    *far_gd, grad_pre = tie(*far_gd, grad_pre)
+    moves = scatter_near(block_rows, far_gd, g_down_t)
+    near_gd = exchange(*moves) if moves else ()
+    got_two = swap_core(dot_nt(grad_pre[tokens:], w_up).astype(BF))
+    own_two = dot_nt(grad_pre[:tokens], w_up)
+    g_up = dot_tn(rows_two, grad_pre).astype(BF)
+    grad_mid, mid_low, mid_sums = rows_mid_back(chips, mixed, ids, cot, swapped_cot, residual, own_two, got_two, vec)
+    other_mid = swap_core(mid_low)
+    moves = scatter_far(block_rows, g_up)
+    far_gu = exchange(*moves) if moves else ()
+    active, mid_low = tie(active, mid_low)
     got_down = swap_core(dot_nt(active[tokens:], w_down_t).astype(BF))
     own_down = dot_nt(active[:tokens], w_down_t)
-    output = rows_out(chips, mixed, ids, residual, own_down, got_down, vec)
-
-    grad_active = dot_nn(cot_rows, w_down_t)
-    _, gelu_back = jax.vjp(gelu_tanh, up_pre)
-    grad_pre = gelu_back(grad_active)[0].astype(BF)
-    got_two = swap_core(dot_nt(grad_pre[tokens:], w_up).astype(BF))
-    own_two = dot_nt(grad_pre[:tokens], w_up)
-    g_down_t = dot_tn(cot_rows, active).astype(BF)
-    sum_down = scatter_grads(g_down_t, core)
-    g_up = dot_tn(rows_two, grad_pre).astype(BF)
-    sum_up = scatter_grads(g_up, core)
-    grad_b_up = jnp.sum(grad_pre.astype(F32), axis=0, keepdims=True)
-    grad_mid, mid_low, mid_sums = rows_mid_back(chips, mixed, ids, cot, residual, own_two, got_two, vec)
-
-    mid_rows = to_sequence(mid_low, core, keeps)
+    out_here, out_low = rows_out(ids, residual, own_down, got_down, vec)
+    output = rows_home(chips, mixed, ids, out_here, swap_pair(out_low))
+    mid_rows = both_halves(mid_low, other_mid, core)
     grad_context = dot_nn(mid_rows, w_out_t).astype(BF)
     g_out_t = dot_tn(mid_rows, context).astype(BF)
-    grad_qkv, grad_b_qkv = attend_back(qkv, slopes, lse, grad_context)
-    grad_b_qkv = grad_b_qkv.reshape(1, -1)
+    dq, cols = attend_back(qkv, slopes, lse, grad_context, 0, size, g_out_t)
+    cols = cols.reshape(1, -1)
     vec_t = jnp.pad(vec[:8].T, ((0, 0), (0, 120)))
-    g_qkv, one_sums = qkv_grads(seq_one, grad_qkv, w_qkv, grad_b_qkv, vec_t)
-    sum_out = scatter_grads(g_out_t, core)
-    sum_qkv = scatter_grads(g_qkv, core)
-    here, swapped = from_sequence(grad_qkv, w_qkv, core)
-    grad_in = rows_first_back(chips, mixed, ids, hidden, grad_mid, here, swapped, vec)
+    g_q, one_sums = qkv_grads(seq_one, dq, w_qkv, 0, cols, vec_t)
 
     mid_sums = jnp.concatenate([mid_sums[:3], one_sums[:2], mid_sums[5:]], axis=0)
-    total = pack_small(plan, ids, mid_sums, cot_sums, grad_b_qkv, grad_b_up)
-    total = total + swap_core(total)
-    for bit in range(chip_bits()):
-        got = swap_bit(total, bit + 1)
-        total = total + jnp.concatenate([swap_blocks(got[:8], bit, block), got[8:]], axis=0)
-    for bit in range((size - 1).bit_length()):
-        total = total + lax.ppermute(total, "tensor", [(i, i ^ (1 << bit)) for i in range(size)])
-    vector_sums, sum_b_qkv, sum_b_up = own_small(plan, total, index, tensor)
+    riding = chip_bits() == 2
+    both = pack + wide[1]
+    extra = pack_rows(plan, ids, both, mid_sums, cot_sums, cols, grad_b_up) if riding else None
+    got = tie(*near_gd, *far_gu, g_q)
+    near_gd, far_gu, g_q = got[: len(near_gd)], got[len(near_gd) : -1], got[-1]
+    moves = scatter_near(block_rows, far_gu, g_up)
+    n = len(moves)
+    moves = moves + scatter_far(block_rows, g_q, g_out_t, extra=extra)
+    blocks_d = cut_blocks(scattered(block_rows, near_gd, g_down_t))
+    got = exchange(*moves, *scatter_tensor(blocks_d))
+    near_gu, far_q, turn_gd = got[:n], got[n : 2 * n], got[2 * n :]
+    *far_q, dq = tie(*far_q, dq)
+    own, give = core_rows(dq, core)
+    got_one = swap_core(dot_nt(give, w_qkv).astype(BF))
+    own_one = dot_nt(own, w_qkv)
+    grad_here, grad_low = rows_first_back(ids, here_in, grad_mid, own_one, got_one, vec)
+    moves = scatter_near(block_rows, far_q, g_q, g_out_t, extra=extra)
+    blocks_u = cut_blocks(scattered(block_rows, near_gu, g_up))
+    got = exchange(*moves, *scatter_tensor(blocks_u))
+    near_q, turn_gu = got[: len(moves)], got[len(moves) :]
+    line = scattered(block_rows, near_q, g_q, g_out_t, extra=extra)
+    main = line[:block_rows]
+    blocks = [
+        jnp.concatenate(parts, axis=1)
+        for parts in zip(cut_blocks(main[:, : size * pack]), cut_blocks(main[:, size * pack :]))
+    ]
+    if riding:
+        blocks = [jnp.concatenate(parts, axis=0) for parts in zip(blocks, cut_blocks(line[block_rows:]))]
+    turn_q = exchange(*scatter_tensor(blocks))
+    swapped = swap_pair(grad_low)
+    grad_in = rows_home(chips, mixed, ids, grad_here, swapped)
+    keep_d, give_d = core_rows(scatter_total(blocks_d, turn_gd), core)
+    keep_u, give_u = core_rows(scatter_total(blocks_u, turn_gu), core)
+    back_d, back_u = exchange((swap_core, give_d), (swap_core, give_u))
+    sum_up, sum_down = by_core(keep_u, back_u, core), by_core(keep_d, back_d, core)
+    total_q = scatter_total(blocks, turn_q)
+    keep_q, give_q = core_rows(total_q[:block_rows], core)
+    back_q = swap_core(jnp.concatenate([give_q, total_q[block_rows:]], axis=0))
+    sum_both = by_core(keep_q, back_q[: block_rows // 2], core)
+    if riding:
+        small_rows = total_q[block_rows:] + back_q[block_rows // 2 :]
+        mine = lax.dynamic_index_in_dim(small_rows, core, 0, keepdims=False)
+        vector_sums = [mine[i * small : (i + 1) * small] for i in range(6)]
+        start = 6 * small
+        sum_b_qkv = mine[start : start + qkv_bias.size].reshape(qkv_bias.shape)
+        start += qkv_bias.size
+        sum_b_up = mine[start : start + up_bias.size].reshape(up_bias.shape)
+    else:
+        total = pack_small(plan, ids, mid_sums, cot_sums, cols, grad_b_up)
+        total = add_chips(total + swap_core(total), (), block)
+        for bit in range((size - 1).bit_length()):
+            total = total + lax.ppermute(total, "tensor", [(i, i ^ (1 << bit)) for i in range(size)])
+        vector_sums, sum_b_qkv, sum_b_up = own_small(plan, total, index, tensor)
+    sum_qkv, sum_out = sum_both[:, :, :pack], sum_both[:, :, pack:]
 
     sum_w_qkv = sum_qkv.reshape(rows, 2, 3, pair, HD).transpose(0, 1, 3, 2, 4).reshape(rows, -1)
     return (

time: 504 us -> 449 us (0.89)
  waiting for transfers between devices: 190 us -> 120 us
  Pallas kernels: 67.9 us -> 97.8 us
  matrix products: 64.4 us -> 48.3 us
  starting transfers between devices: 94.3 us -> 81.6 us
  local copies, waits for them, and re-layouts: 54.1 us -> 66.4 us
    ppermute x45 -> x37, waiting for transfers between devices: 95.5 us -> 43.5 us  [swap_bit(): return lax.ppermute(values, 'dp', [(i, i ^ 1 << bit) for i in range(size)])]
    pallas_call x3 -> x5, Pallas kernels: 39.3 us -> 63 us  [the longest x1 20.9 us: attend_back(): pl.pallas_call(functools.partial(attend_back_kernel, first), grid=(groups...]
    ppermute x21 -> x18, waiting for transfers between devices: 81.7 us -> 59.8 us  [from_tensor(): lax.ppermute(values, 'tensor', [(i, (i - step) % size) for i in range(siz...]
    dot_general x4 -> x2, matrix products: 29.1 us -> 8.12 us  [dot_nn(): lax.dot_general(left, right, (((1,), (0,)), ((), ())), preferred_element_...]
    ppermute x21 -> x18, starting transfers between devices: 30.7 us -> 19.7 us  [from_tensor(): lax.ppermute(values, 'tensor', [(i, (i - step) % size) for i in range(siz...]
    unnamed x113 -> x132, local copies, waits for them, and re-layouts: 27.4 us -> 38 us
    ppermute x4, waiting for transfers between devices: 7.56 us -> 17.1 us  [swap_pair(): return lax.ppermute(values, ('dp', 'tensor'), pairs)]
    pallas_call x6 -> x9, Pallas kernels: 17.9 us -> 24.5 us  [row_call(): pl.pallas_call(body, grid=(tokens // step,), in_specs=[pl.BlockSpec(memor...]
  transfers between devices with their start and end apart: 72 -> 59, of which waited for: 28 -> 21; matrix products, arithmetic and copies ran while one was open for 17% -> 22% of each run, Pallas kernels for 7% -> 18%
where the time goes in v2:
time: 449 us; the launch traced here: 443 us
  waiting for transfers between devices  120 us (27%)
  Pallas kernels  97.8 us (22%)
  starting transfers between devices  81.6 us (18%)
  local copies, waits for them, and re-layouts  66.4 us (15%)
  matrix products  48.3 us (11%)
  other arithmetic  26.1 us (6%)
    ppermute x18, waiting for transfers between devices, from_tensor(): lax.ppermute(values, 'tensor', [(i, (i - step) % size) for i in range(siz...  59.8 us
    ppermute x37, starting transfers between devices, swap_bit(): return lax.ppermute(values, 'dp', [(i, i ^ 1 << bit) for i in range(size)])  43.9 us
    ppermute x37, waiting for transfers between devices, swap_bit(): return lax.ppermute(values, 'dp', [(i, i ^ 1 << bit) for i in range(size)])  43.5 us
    unnamed x132, local copies, waits for them, and re-layouts  38 us
    dot_general x8, matrix products, dot_nt(): lax.dot_general(left, right, (((1,), (1,)), ((), ())), preferred_element_...  26.9 us
    pallas_call x9, Pallas kernels, row_call(): pl.pallas_call(body, grid=(tokens // step,), in_specs=[pl.BlockSpec(memor...  24.5 us
    pallas_call x1, Pallas kernels, attend_back(): pl.pallas_call(functools.partial(attend_back_kernel, first), grid=(groups...  20.9 us
    ppermute x18, starting transfers between devices, from_tensor(): lax.ppermute(values, 'tensor', [(i, (i - step) % size) for i in range(siz...  19.7 us
  transfers between devices with their start and end apart: 59, of which 21 were waited for; matrix products, arithmetic and copies ran while one was open for 22% of the time, Pallas kernels for 18%

profile of v2, /device:TPU:1, one launch (start us, length us, event | category | flops | bytes accessed | tf_op | source)
XLA Modules:
  0.0 443.0 jit_solution(14443158133834877111)
XLA Ops:
  2.2 4.1 concatenate.140
  14.6 4.8 %collective-permute-start.2 = (bf16[272,512]{1,0:T(8,128)(2,1)S(1)}, bf16[272,512]{1,0:T(8,128)(2,1)S(1)}, u32[]{:S(2)}, u32[]{:S(2)}) collective-permute-start(bf16[272,512]{1,0:T(8,128)(2,1)S(1)} %pad_maximum_fusion.15), channel_id=1, source_target_pairs={{0,3},{1,0},{2,1},{3,2},{4,7},{5,4},{6,5},{7,6},{8,11},{9,8},{10,9... | collective-permute-start | bytes 835592 | tf_op jit(solution)/shard_map/ppermute | solution.py:48
  20.0 5.6 %collective-permute-done.2 = bf16[272,512]{1,0:T(8,128)(2,1)S(1)} collective-permute-done((bf16[272,512]{1,0:T(8,128)(2,1)S(1)}, bf16[272,512]{1,0:T(8,128)(2,1)S(1)}, u32[]{:S(2)}, u32[]{:S(2)}) %collective-permute-start.2) | collective-permute-done | bytes 278560 | tf_op jit(solution)/shard_map/ppermute | solution.py:48
  25.6 17.7 %collective-permute-done.3 = bf16[272,512]{1,0:T(8,128)(2,1)S(1)} collective-permute-done((bf16[272,512]{1,0:T(8,128)(2,1)S(1)}, bf16[272,512]{1,0:T(8,128)(2,1)S(1)}, u32[]{:S(2)}, u32[]{:S(2)}) %collective-permute-start.3) | collective-permute-done | bytes 278560 | tf_op jit(solution)/shard_map/ppermute | solution.py:48
  43.8 2.3 collective-permute-start.9
  46.0 4.9 %collective-permute-start.5 = (bf16[512,1024]{1,0:T(8,128)(2,1)S(1)}, bf16[512,1024]{1,0:T(8,128)(2,1)S(1)}, u32[]{:S(2)}, u32[]{:S(2)}) collective-permute-start(bf16[512,1024]{1,0:T(8,128)(2,1)S(1)} %rows_low.2), channel_id=1, source_target_pairs={{1,4},{3,6},{4,1},{6,3},{9,12},{11,14},{12,9},{14,11},{17,20},{19,... | collective-permute-start | bytes 3145736 | tf_op jit(solution)/shard_map/ppermute | solution.py:58
  54.3 14.7 %collective-permute-done.5.swapped_ref = bf16[512,1024]{1,0:T(8,128)(2,1)S(1)} collective-permute-done((bf16[512,1024]{1,0:T(8,128)(2,1)S(1)}, bf16[512,1024]{1,0:T(8,128)(2,1)S(1)}, u32[]{:S(2)}, u32[]{:S(2)}) %collective-permute-start.5) | collective-permute-done | bytes 1048608 | tf_op jit(solution)/shard_map/ppermute | solution.py:58
  68.9 2.9 rows_first.1
  71.9 6.1 %collective-permute-done.10 = bf16[256,512]{1,0:T(8,128)(2,1)S(1)} collective-permute-done((bf16[256,512]{1,0:T(8,128)(2,1)S(1)}, bf16[256,512]{1,0:T(8,128)(2,1)S(1)}, u32[]{:S(2)}, u32[]{:S(2)}) %collective-permute-start.10) | collective-permute-done | bytes 262176 | tf_op jit(solution)/shard_map/ppermute | solution.py:48
  79.4 1.9 collective-permute-start.13
  82.9 8.9 %collective-permute-done.11 = bf16[128,2048]{1,0:T(8,128)(2,1)S(1)} collective-permute-done((bf16[128,2048]{1,0:T(8,128)(2,1)S(1)}, bf16[128,2048]{1,0:T(8,128)(2,1)S(1)}, u32[]{:S(2)}, u32[]{:S(2)}) %collective-permute-start.11) | collective-permute-done | bytes 524320 | tf_op jit(solution)/shard_map/ppermute | solution.py:39
  91.8 4.1 collective-permute-done.12
  100.6 1.9 spread_small.1
  102.6 2.5 collective-permute-start.15
  110.4 6.9 %add_convert_fusion.qkv_ref = bf16[1024,1536]{1,0:T(8,128)(2,1)S(1)} fusion(bf16[1024,1536]{1,0:T(8,128)(2,1)} %copy-done.43, f32[1536]{0:T(1024)S(1)} %reduce, f32[1024]{0:T(1024)S(1)} %bitcast.76, f32[1024]{0:T(1024)S(1)} %bitcast.75, bf16[512,1024]{1,0:T(8,128)(2,1)S(1)} %copy-done.18, bf16[512,1024]{1,0:T(8,128)(2,1)S(1)} %get-tuple-element.348), kind=kOutput, calls=%fused_computation | convolution fusion | flops 3231711232 | bytes 8402944 | tf_op jit(solution)/shard_map/dot_general | solution.py:26
  118.4 3.0 constant_dynamic-update-slice_fusion.14
  121.4 2.7 collective-permute-start.24
  124.2 4.7 %collective-permute-done.16 = bf16[256,512]{1,0:T(8,128)(2,1)} collective-permute-done((bf16[256,512]{1,0:T(8,128)(2,1)}, bf16[256,512]{1,0:T(8,128)(2,1)}, u32[]{:S(2)}, u32[]{:S(2)}) %collective-permute-start.16) | collective-permute-done | bytes 262176 | tf_op jit(solution)/shard_map/ppermute | solution.py:48
  131.7 17.0 %attend.1 = (bf16[1024,512]{1,0:T(8,128)(2,1)S(1)}, f32[4,2,1024]{2,1,0:T(2,128)S(1)}) custom-call(f32[4,2]{1,0:T(4,128)S(1)} %multiply_exponential_fusion.slope_ref, bf16[1024,1536]{1,0:T(8,128)(2,1)S(1)} %add_convert_fusion.qkv_ref, bf16[256,512]{1,0:T(8,128)(2,1)S(1)} %collective-permute-done.15.refs_0_), custom_call_target="tpu_custom_call" | custom-call | flops 9900000256 | bytes 9000000 | tf_op jit(solution)/shard_map/attend/pallas_call | solution.py:261
  149.4 2.3 collective-permute-start.18
  154.2 1.7 constant_dynamic-update-slice_fusion.20
  161.5 2.3 constant_dynamic-update-slice_fusion.13
  163.8 2.3 constant_dynamic-update-slice_fusion.12
  170.1 3.0 rows_mid.1
  178.4 6.4 %collective-permute-done.29 = bf16[128,2048]{1,0:T(8,128)(2,1)S(1)} collective-permute-done((bf16[128,2048]{1,0:T(8,128)(2,1)}, bf16[128,2048]{1,0:T(8,128)(2,1)S(1)}, u32[]{:S(2)}, u32[]{:S(2)}) %collective-permute-start.29) | collective-permute-done | bytes 524320 | tf_op jit(solution)/shard_map/ppermute | solution.py:39
  186.5 1.9 constant_dynamic-update-slice_fusion.15.w_ref
  188.5 12.1 %up_forward.1 = (bf16[1024,2048]{1,0:T(8,128)(2,1)}, bf16[1024,2048]{1,0:T(8,128)(2,1)}) custom-call(bf16[1024,1024]{1,0:T(8,128)(2,1)S(1)} %constant_dynamic-update-slice_fusion.8.x_ref, bf16[1024,2048]{1,0:T(8,128)(2,1)} %constant_dynamic-update-slice_fusion.10.w_ref, f32[1,2048]{1,0:T(1,128)S(1)} %get-tuple-element.218.b_ref), custom_call_target="tpu_custom_call" | custom-call | flops 13200000000 | bytes 12000000 | tf_op jit(solution)/shard_map/up_forward/pallas_call | solution.py:729
  200.7 7.0 %convolution_convert_fusion.1 = bf16[1024,2048]{1,0:T(8,128)(2,1)S(1)} fusion(bf16[1024,2048]{1,0:T(8,128)(2,1)} %get-tuple-element.239, bf16[512,1024]{1,0:T(8,128)(2,1)S(1)} %collective-permute-done.24, bf16[512,1024]{1,0:T(8,128)(2,1)S(1)} %copy-done.19), kind=kOutput, calls=%fused_computation.3 | convolution fusion | flops 4301258752 | bytes 10485760 | tf_op jit(solution)/shard_map/dot_general | solution.py:30
  208.6 10.7 %up_backward.1 = (bf16[1024,2048]{1,0:T(8,128)(2,1)}, f32[1,2048]{1,0:T(1,128)S(1)}) custom-call(bf16[1024,1024]{1,0:T(8,128)(2,1)S(1)} %pad_maximum_fusion.1.x_ref, bf16[1024,2048]{1,0:T(8,128)(2,1)} %constant_dynamic-update-slice_fusion.15.w_ref, bf16[1024,2048]{1,0:T(8,128)(2,1)} %get-tuple-element.235.slope_ref), custom_call_target="tpu_custom_call" | custom-call | flops 11000000512 | bytes 10000000 | tf_op jit(solution)/shard_map/up_backward/pallas_call | solution.py:756
  221.3 5.3 %fusion.18 = bf16[512,1024]{1,0:T(8,128)(2,1)S(1)} fusion(bf16[1024,2048]{1,0:T(8,128)(2,1)} %constant_dynamic-update-slice_fusion.10.w_ref, bf16[1024,2048]{1,0:T(8,128)(2,1)} %get-tuple-element.237), kind=kOutput, calls=%fused_computation.31 | convolution fusion | flops 2148007936 | bytes 7340032 | tf_op jit(solution)/shard_map/dot_general | solution.py:34
  226.6 4.9 %convolution_convert_fusion = bf16[1024,2048]{1,0:T(8,128)(2,1)S(1)} fusion(bf16[1024,1024]{1,0:T(8,128)(2,1)S(1)} %constant_dynamic-update-slice_fusion.8.x_ref, bf16[1024,2048]{1,0:T(8,128)(2,1)S(1)} %copy-done.50), kind=kOutput, calls=%fused_computation.2 | convolution fusion | flops 4297064448 | bytes 10485760 | tf_op jit(solution)/shard_map/dot_general | solution.py:30
  231.6 2.2 collective-permute-start.31
  238.1 3.7 fusion.7.own_ref
  244.5 4.9 %rows_mid_back.1 = (f32[512,1024]{1,0:T(8,128)S(1)}, bf16[512,1024]{1,0:T(8,128)(2,1)S(1)}, f32[8,1024]{1,0:T(8,128)S(1)}) custom-call(s32[4]{0:T(128)S(1)} %pad_add_fusion.ids_ref, f32[512,1024]{1,0:T(8,128)} %cot_ref.1, bf16[512,1024]{1,0:T(8,128)(2,1)S(1)} %collective-permute-done.13.swapped_ref, f32[512,1024]{1,0:T(8,128)} %copy-done.9, ...), custom_call_target="tpu_custom_call" | custom-call | flops 3300000000 | bytes 3000000 | tf_op jit(solution)/shard_map/rows_mid_back/pallas_call | solution.py:408
  256.4 4.9 %fusion.21 = bf16[512,1024]{1,0:T(8,128)(2,1)} fusion(bf16[1024,2048]{1,0:T(8,128)(2,1)S(1)} %copy-done.49, bf16[1024,2048]{1,0:T(8,128)(2,1)} %get-tuple-element.239), kind=kOutput, calls=%fused_computation.32 | convolution fusion | flops 2148007936 | bytes 7340032 | tf_op jit(solution)/shard_map/dot_general | solution.py:34
  261.4 11.1 %collective-permute-done.34 = bf16[256,2048]{1,0:T(8,128)(2,1)} collective-permute-done((bf16[256,2048]{1,0:T(8,128)(2,1)}, bf16[256,2048]{1,0:T(8,128)(2,1)}, u32[]{:S(2)}, u32[]{:S(2)}) %collective-permute-start.34) | collective-permute-done | bytes 1048608 | tf_op jit(solution)/shard_map/ppermute | solution.py:39
  277.2 20.9 %attend_back.1 = (bf16[1024,1536]{1,0:T(8,128)(2,1)S(1)}, f32[4,1,384]{2,1,0:T(1,128)S(1)}) custom-call(f32[4,2]{1,0:T(4,128)S(1)} %multiply_exponential_fusion.slope_ref, bf16[1024,1536]{1,0:T(8,128)(2,1)} %copy-done.13, bf16[1024,512]{1,0:T(8,128)(2,1)S(1)} %convolution_convert_fusion.3.grad_ref, f32[4,2,1024]{2,1,0:T(2,128)S(1)} %get-tuple-element.254.lse_ref, ...), custom_call_target="tpu_custom_call" | custom-call | flops 12099999744 | bytes 11000000 | tf_op jit(solution)/shard_map/attend_back/pallas_call | solution.py:331
  299.8 7.6 %qkv_grads.1 = (bf16[1024,1536]{1,0:T(8,128)(2,1)S(1)}, f32[8,1024]{1,0:T(8,128)S(1)}) custom-call(bf16[1024,1024]{1,0:T(8,128)(2,1)S(1)} %pad_maximum_fusion.z_ref, bf16[1024,1536]{1,0:T(8,128)(2,1)} %copy-done.6, bf16[1024,1536]{1,0:T(8,128)(2,1)} %copy-done.43, f32[1,1536]{1,0:T(1,128)S(1)} %bitcast.65, f32[1024,128]{1,0:T(8,128)S(1)} %pad.14.vec_ref), custom_call_target="tpu_custom_call" | custom-call | flops 5500000256 | bytes 5000000 | tf_op jit(solution)/shard_map/qkv_grads/pallas_call | solution.py:666
  307.5 2.3 pack_rows.1
  311.9 2.4 fusion.55
  314.3 1.9 add_convert_fusion.6
  324.0 6.0 %collective-permute-done.43 = bf16[256,512]{1,0:T(8,128)(2,1)} collective-permute-done((bf16[256,512]{1,0:T(8,128)(2,1)}, bf16[256,512]{1,0:T(8,128)(2,1)}, u32[]{:S(2)}, u32[]{:S(2)}) %collective-permute-start.43) | collective-permute-done | bytes 262176 | tf_op jit(solution)/shard_map/ppermute | solution.py:48
  330.2 6.5 %fusion.3.own_ref = f32[512,1024]{1,0:T(8,128)} fusion(bf16[1024,2048]{1,0:T(8,128)(2,1)} %constant_dynamic-update-slice_fusion.15.w_ref, bf16[1024,2048]{1,0:T(8,128)(2,1)} %get-tuple-element.239), kind=kOutput, calls=%fused_computation.14 | convolution fusion | flops 2147483648 | bytes 8388608 | tf_op jit(solution)/shard_map/dot_general | solution.py:34
  336.7 5.2 %collective-permute-done.44 = bf16[256,512]{1,0:T(8,128)(2,1)S(1)} collective-permute-done((bf16[256,512]{1,0:T(8,128)(2,1)}, bf16[256,512]{1,0:T(8,128)(2,1)S(1)}, u32[]{:S(2)}, u32[]{:S(2)}) %collective-permute-start.44) | collective-permute-done | bytes 262176 | tf_op jit(solution)/shard_map/ppermute | solution.py:48
  341.8 3.1 rows_out.1
  344.9 3.9 collective-permute-done.45
  348.8 3.7 collective-permute-start.33
  352.4 3.6 collective-permute-done.41
  357.5 2.5 fusion.54
  362.8 2.0 collective-permute-start.51
  366.6 1.8 fusion.15
  368.4 3.1 fusion.13.own_ref
  372.2 2.4 rows_home.2
  374.6 3.1 collective-permute-start.46
  377.8 4.5 %collective-permute-done.51 = bf16[256,512]{1,0:T(8,128)(2,1)S(1)} collective-permute-done((bf16[256,512]{1,0:T(8,128)(2,1)S(1)}, bf16[256,512]{1,0:T(8,128)(2,1)S(1)}, u32[]{:S(2)}, u32[]{:S(2)}) %collective-permute-start.51) | collective-permute-done | bytes 262176 | tf_op jit(solution)/shard_map/ppermute | solution.py:48
  382.3 5.8 %collective-permute-done.48 = bf16[272,2048]{1,0:T(8,128)(2,1)S(1)} collective-permute-done((bf16[272,2048]{1,0:T(8,128)(2,1)S(1)}, bf16[272,2048]{1,0:T(8,128)(2,1)S(1)}, u32[]{:S(2)}, u32[]{:S(2)}) %collective-permute-start.48) | collective-permute-done | bytes 1114144 | tf_op jit(solution)/shard_map/ppermute | solution.py:39
  389.9 2.4 collective-permute-start.55
  392.5 4.6 %collective-permute-start.57 = (f32[128,512]{1,0:T(8,128)S(1)}, f32[128,512]{1,0:T(8,128)S(1)}, u32[]{:S(2)}, u32[]{:S(2)}) collective-permute-start(f32[128,512]{1,0:T(8,128)S(1)} %get-tuple-element.302), channel_id=1, source_target_pairs={{0,4},{4,0},{8,12},{12,8},{16,20},{20,16},{24,28},{28,24},{1,5},{5... | collective-permute-start | bytes 786440 | tf_op jit(solution)/shard_map/ppermute | solution.py:39
  397.1 7.4 %collective-permute-start.58 = (f32[128,512]{1,0:T(8,128)S(1)}, f32[128,512]{1,0:T(8,128)S(1)}, u32[]{:S(2)}, u32[]{:S(2)}) collective-permute-start(f32[128,512]{1,0:T(8,128)S(1)} %get-tuple-element.303), channel_id=1, source_target_pairs={{0,4},{4,0},{8,12},{12,8},{16,20},{20,16},{24,28},{28,24},{1,5},{5... | collective-permute-start | bytes 786440 | tf_op jit(solution)/shard_map/ppermute | solution.py:39
  404.5 6.2 %collective-permute-done.54 = bf16[272,512]{1,0:T(8,128)(2,1)S(1)} collective-permute-done((bf16[272,512]{1,0:T(8,128)(2,1)S(1)}, bf16[272,512]{1,0:T(8,128)(2,1)S(1)}, u32[]{:S(2)}, u32[]{:S(2)}) %collective-permute-start.54) | collective-permute-done | bytes 278560 | tf_op jit(solution)/shard_map/ppermute | solution.py:48
  413.0 4.2 rows_first_back.1
  418.5 7.5 %collective-permute-start.47 = (bf16[512,1024]{1,0:T(8,128)(2,1)S(1)}, bf16[512,1024]{1,0:T(8,128)(2,1)S(1)}, u32[]{:S(2)}, u32[]{:S(2)}) collective-permute-start(bf16[512,1024]{1,0:T(8,128)(2,1)S(1)} %get-tuple-element.278), channel_id=1, source_target_pairs={{1,4},{3,6},{4,1},{6,3},{9,12},{11,14},{12,9},{14,11},{17,20},{19,... | collective-permute-start | bytes 3145736 | tf_op jit(solution)/shard_map/ppermute | solution.py:58
  436.1 2.4 collective-permute-done.47.swapped_ref
  440.1 2.4 rows_home.3
  (322 shorter events, 107.6 us)
Async XLA Ops:
  6.4 7.3 %collective-permute-start.1 = (bf16[16,384]{1,0:T(8,128)(2,1)S(1)}, bf16[16,384]{1,0:T(8,128)(2,1)S(1)}, u32[]{:S(2)}, u32[]{:S(2)}) collective-permute-start(bf16[16,384]{1,0:T(8,128)(2,1)S(1)} %broadcast_select_fusion.7), channel_id=1, source_target_pairs={{0,4},{4,0},{8,12},{12,8},{16,20},{20,16},{24,28},{28,24},{1,5},{5... | collective-permute-start | bytes 36872 | tf_op jit(solution)/shard_map/ppermute | solution.py:39
  11.0 2.8 collective-permute-start
  14.6 11.0 %collective-permute-start.2 = (bf16[272,512]{1,0:T(8,128)(2,1)S(1)}, bf16[272,512]{1,0:T(8,128)(2,1)S(1)}, u32[]{:S(2)}, u32[]{:S(2)}) collective-permute-start(bf16[272,512]{1,0:T(8,128)(2,1)S(1)} %pad_maximum_fusion.15), channel_id=1, source_target_pairs={{0,3},{1,0},{2,1},{3,2},{4,7},{5,4},{6,5},{7,6},{8,11},{9,8},{10,9... | collective-permute-start | bytes 835592 | tf_op jit(solution)/shard_map/ppermute | solution.py:48
  19.4 23.8 %collective-permute-start.3 = (bf16[272,512]{1,0:T(8,128)(2,1)S(1)}, bf16[272,512]{1,0:T(8,128)(2,1)S(1)}, u32[]{:S(2)}, u32[]{:S(2)}) collective-permute-start(bf16[272,512]{1,0:T(8,128)(2,1)S(1)} %pad_maximum_fusion.15), channel_id=1, source_target_pairs={{0,2},{1,3},{2,0},{3,1},{4,6},{5,7},{6,4},{7,5},{8,10},{9,11},{10,... | collective-permute-start | bytes 835592 | tf_op jit(solution)/shard_map/ppermute | solution.py:48
  19.5 23.8 %collective-permute-start.4 = (bf16[272,512]{1,0:T(8,128)(2,1)S(1)}, bf16[272,512]{1,0:T(8,128)(2,1)S(1)}, u32[]{:S(2)}, u32[]{:S(2)}) collective-permute-start(bf16[272,512]{1,0:T(8,128)(2,1)S(1)} %pad_maximum_fusion.15), channel_id=1, source_target_pairs={{0,1},{1,2},{2,3},{3,0},{4,5},{5,6},{6,7},{7,4},{8,9},{9,10},{10,1... | collective-permute-start | bytes 835592 | tf_op jit(solution)/shard_map/ppermute | solution.py:48
  43.7 28.2 %collective-permute-start.8 = (bf16[256,512]{1,0:T(8,128)(2,1)S(1)}, bf16[256,512]{1,0:T(8,128)(2,1)S(1)}, u32[]{:S(2)}, u32[]{:S(2)}) collective-permute-start(bf16[256,512]{1,0:T(8,128)(2,1)S(1)} %get-tuple-element.181), channel_id=1, source_target_pairs={{0,3},{1,0},{2,1},{3,2},{4,7},{5,4},{6,5},{7,6},{8,11},{9,8},{10,9... | collective-permute-start | bytes 786440 | tf_op jit(solution)/shard_map/ppermute | solution.py:48
  43.8 28.1 %collective-permute-start.9 = (bf16[256,512]{1,0:T(8,128)(2,1)S(1)}, bf16[256,512]{1,0:T(8,128)(2,1)S(1)}, u32[]{:S(2)}, u32[]{:S(2)}) collective-permute-start(bf16[256,512]{1,0:T(8,128)(2,1)S(1)} %get-tuple-element.181), channel_id=1, source_target_pairs={{0,2},{1,3},{2,0},{3,1},{4,6},{5,7},{6,4},{7,5},{8,10},{9,11},{10,... | collective-permute-start | bytes 786440 | tf_op jit(solution)/shard_map/ppermute | solution.py:48
  46.0 22.9 %collective-permute-start.5 = (bf16[512,1024]{1,0:T(8,128)(2,1)S(1)}, bf16[512,1024]{1,0:T(8,128)(2,1)S(1)}, u32[]{:S(2)}, u32[]{:S(2)}) collective-permute-start(bf16[512,1024]{1,0:T(8,128)(2,1)S(1)} %rows_low.2), channel_id=1, source_target_pairs={{1,4},{3,6},{4,1},{6,3},{9,12},{11,14},{12,9},{14,11},{17,20},{19,... | collective-permute-start | bytes 3145736 | tf_op jit(solution)/shard_map/ppermute | solution.py:58
  50.9 27.1 %collective-permute-start.6 = (bf16[272,2048]{1,0:T(8,128)(2,1)S(1)}, bf16[272,2048]{1,0:T(8,128)(2,1)S(1)}, u32[]{:S(2)}, u32[]{:S(2)}) collective-permute-start(bf16[272,2048]{1,0:T(8,128)(2,1)S(1)} %fusion.24), channel_id=1, source_target_pairs={{0,8},{4,12},{8,0},{12,4},{16,24},{20,28},{24,16},{28,20},{1,9},{5... | collective-permute-start | bytes 3342344 | tf_op jit(solution)/shard_map/ppermute | solution.py:39
  52.2 25.8 %collective-permute-start.7 = (bf16[272,2048]{1,0:T(8,128)(2,1)S(1)}, bf16[272,2048]{1,0:T(8,128)(2,1)S(1)}, u32[]{:S(2)}, u32[]{:S(2)}) collective-permute-start(bf16[272,2048]{1,0:T(8,128)(2,1)S(1)} %fusion.24), channel_id=1, source_target_pairs={{0,16},{4,20},{8,24},{12,28},{16,0},{20,4},{24,8},{28,12},{1,17},{... | collective-permute-start | bytes 3342344 | tf_op jit(solution)/shard_map/ppermute | solution.py:39
  68.9 9.0 %collective-permute-start.10 = (bf16[256,512]{1,0:T(8,128)(2,1)S(1)}, bf16[256,512]{1,0:T(8,128)(2,1)S(1)}, u32[]{:S(2)}, u32[]{:S(2)}) collective-permute-start(bf16[256,512]{1,0:T(8,128)(2,1)S(1)} %get-tuple-element.181), channel_id=1, source_target_pairs={{0,1},{1,2},{2,3},{3,0},{4,5},{5,6},{6,7},{7,4},{8,9},{9,10},{10,1... | collective-permute-start | bytes 786440 | tf_op jit(solution)/shard_map/ppermute | solution.py:48
  78.1 13.7 %collective-permute-start.11 = (bf16[128,2048]{1,0:T(8,128)(2,1)S(1)}, bf16[128,2048]{1,0:T(8,128)(2,1)S(1)}, u32[]{:S(2)}, u32[]{:S(2)}) collective-permute-start(bf16[128,2048]{1,0:T(8,128)(2,1)S(1)} %slice.456), channel_id=1, source_target_pairs={{0,16},{4,20},{8,24},{12,28},{16,0},{20,4},{24,8},{28,12},{1,17},{... | collective-permute-start | bytes 1572872 | tf_op jit(solution)/shard_map/ppermute | solution.py:39
  79.4 16.5 %collective-permute-start.13 = (bf16[512,1024]{1,0:T(8,128)(2,1)S(1)}, bf16[512,1024]{1,0:T(8,128)(2,1)S(1)}, u32[]{:S(2)}, u32[]{:S(2)}) collective-permute-start(bf16[512,1024]{1,0:T(8,128)(2,1)S(1)} %get-tuple-element.187), channel_id=1, source_target_pairs={{1,4},{3,6},{4,1},{6,3},{9,12},{11,14},{12,9},{14,11},{17,20},{19,... | collective-permute-start | bytes 3145736 | tf_op jit(solution)/shard_map/ppermute | solution.py:58
  81.3 14.6 %collective-permute-start.14 = (bf16[512,1024]{1,0:T(8,128)(2,1)S(1)}, bf16[512,1024]{1,0:T(8,128)(2,1)S(1)}, u32[]{:S(2)}, u32[]{:S(2)}) collective-permute-start(bf16[512,1024]{1,0:T(8,128)(2,1)S(1)} %get-tuple-element.188), channel_id=1, source_target_pairs={{0,4},{4,0},{8,12},{12,8},{16,20},{20,16},{24,28},{28,24},{1,5},{5... | collective-permute-start | bytes 3145736 | tf_op jit(solution)/shard_map/ppermute | solution.py:39
  81.5 14.5 %collective-permute-start.12 = (bf16[144,2048]{1,0:T(8,128)(2,1)S(1)}, bf16[144,2048]{1,0:T(8,128)(2,1)S(1)}, u32[]{:S(2)}, u32[]{:S(2)}) collective-permute-start(bf16[144,2048]{1,0:T(8,128)(2,1)S(1)} %slice.457), channel_id=1, source_target_pairs={{0,8},{4,12},{8,0},{12,4},{16,24},{20,28},{24,16},{28,20},{1,9},{5... | collective-permute-start | bytes 1769480 | tf_op jit(solution)/shard_map/ppermute | solution.py:39
  102.6 18.9 %collective-permute-start.15 = (bf16[256,512]{1,0:T(8,128)(2,1)}, bf16[256,512]{1,0:T(8,128)(2,1)S(1)}, u32[]{:S(2)}, u32[]{:S(2)}) collective-permute-start(bf16[256,512]{1,0:T(8,128)(2,1)} %get-tuple-element.204), channel_id=1, source_target_pairs={{0,3},{1,0},{2,1},{3,2},{4,7},{5,4},{6,5},{7,6},{8,11},{9,8},{10,9... | collective-permute-start | bytes 786440 | tf_op jit(solution)/shard_map/ppermute | solution.py:48
  105.1 23.8 %collective-permute-start.16 = (bf16[256,512]{1,0:T(8,128)(2,1)}, bf16[256,512]{1,0:T(8,128)(2,1)}, u32[]{:S(2)}, u32[]{:S(2)}) collective-permute-start(bf16[256,512]{1,0:T(8,128)(2,1)} %get-tuple-element.204), channel_id=1, source_target_pairs={{0,2},{1,3},{2,0},{3,1},{4,6},{5,7},{6,4},{7,5},{8,10},{9,11},{10,... | collective-permute-start | bytes 786440 | tf_op jit(solution)/shard_map/ppermute | solution.py:48
  106.2 22.7 %collective-permute-start.17 = (bf16[256,512]{1,0:T(8,128)(2,1)}, bf16[256,512]{1,0:T(8,128)(2,1)}, u32[]{:S(2)}, u32[]{:S(2)}) collective-permute-start(bf16[256,512]{1,0:T(8,128)(2,1)} %get-tuple-element.204), channel_id=1, source_target_pairs={{0,1},{1,2},{2,3},{3,0},{4,5},{5,6},{6,7},{7,4},{8,9},{9,10},{10,1... | collective-permute-start | bytes 786440 | tf_op jit(solution)/shard_map/ppermute | solution.py:48
  106.2 43.2 %collective-permute-start.20 = (bf16[256,2048]{1,0:T(8,128)(2,1)}, bf16[256,2048]{1,0:T(8,128)(2,1)}, u32[]{:S(2)}, u32[]{:S(2)}) collective-permute-start(bf16[256,2048]{1,0:T(8,128)(2,1)} %constant_dynamic-update-slice_fusion.4), channel_id=1, source_target_pairs={{0,8},{4,12},{8,0},{12,4},{16,24},{20,28},{24,16},{28,20},{1,9},{5... | collective-permute-start | bytes 3145736 | tf_op jit(solution)/shard_map/ppermute | solution.py:39
  107.4 50.2 %collective-permute-start.21 = (bf16[256,2048]{1,0:T(8,128)(2,1)}, bf16[256,2048]{1,0:T(8,128)(2,1)}, u32[]{:S(2)}, u32[]{:S(2)}) collective-permute-start(bf16[256,2048]{1,0:T(8,128)(2,1)} %constant_dynamic-update-slice_fusion.4), channel_id=1, source_target_pairs={{0,16},{4,20},{8,24},{12,28},{16,0},{20,4},{24,8},{28,12},{1,17},{... | collective-permute-start | bytes 3145736 | tf_op jit(solution)/shard_map/ppermute | solution.py:39
  118.4 50.9 %copy-start.47 = (bf16[1024,512]{1,0:T(8,128)(2,1)}, bf16[1024,512]{1,0:T(8,128)(2,1)S(1)}, u32[]{:S(2)}) copy-start(bf16[1024,512]{1,0:T(8,128)(2,1)S(1)} %slice_dynamic-update-slice_fusion.11) | copy-start | bytes 3145732
  121.4 39.7 %collective-permute-start.24 = (bf16[512,1024]{1,0:T(8,128)(2,1)S(1)}, bf16[512,1024]{1,0:T(8,128)(2,1)S(1)}, u32[]{:S(2)}, u32[]{:S(2)}) collective-permute-start(bf16[512,1024]{1,0:T(8,128)(2,1)S(1)} %copy-done.19), channel_id=1, source_target_pairs={{0,4},{4,0},{8,12},{12,8},{16,20},{20,16},{24,28},{28,24},{1,5},{5... | collective-permute-start | bytes 3145736 | tf_op jit(solution)/shard_map/ppermute | solution.py:39
  130.2 36.0 %collective-permute-start.27 = (bf16[256,2048]{1,0:T(8,128)(2,1)S(1)}, bf16[256,2048]{1,0:T(8,128)(2,1)S(1)}, u32[]{:S(2)}, u32[]{:S(2)}) collective-permute-start(bf16[256,2048]{1,0:T(8,128)(2,1)S(1)} %pad_maximum_fusion.7), channel_id=1, source_target_pairs={{0,8},{4,12},{8,0},{12,4},{16,24},{20,28},{24,16},{28,20},{1,9},{5... | collective-permute-start | bytes 3145736 | tf_op jit(solution)/shard_map/ppermute | solution.py:39
  131.4 34.8 %collective-permute-start.28 = (bf16[256,2048]{1,0:T(8,128)(2,1)S(1)}, bf16[256,2048]{1,0:T(8,128)(2,1)S(1)}, u32[]{:S(2)}, u32[]{:S(2)}) collective-permute-start(bf16[256,2048]{1,0:T(8,128)(2,1)S(1)} %pad_maximum_fusion.7), channel_id=1, source_target_pairs={{0,16},{4,20},{8,24},{12,28},{16,0},{20,4},{24,8},{28,12},{1,17},{... | collective-permute-start | bytes 3145736 | tf_op jit(solution)/shard_map/ppermute | solution.py:39
  149.4 19.9 %collective-permute-start.18 = (bf16[512,1024]{1,0:T(8,128)(2,1)S(1)}, bf16[512,1024]{1,0:T(8,128)(2,1)S(1)}, u32[]{:S(2)}, u32[]{:S(2)}) collective-permute-start(bf16[512,1024]{1,0:T(8,128)(2,1)S(1)} %convolution_convert_fusion.4), channel_id=1, source_target_pairs={{0,4},{4,0},{8,12},{12,8},{16,20},{20,16},{24,28},{28,24},{1,5},{5... | collective-permute-start | bytes 3145736 | tf_op jit(solution)/shard_map/ppermute | solution.py:39
  159.8 16.8 %collective-permute-start.22 = (bf16[128,2048]{1,0:T(8,128)(2,1)S(1)}, bf16[128,2048]{1,0:T(8,128)(2,1)S(1)}, u32[]{:S(2)}, u32[]{:S(2)}) collective-permute-start(bf16[128,2048]{1,0:T(8,128)(2,1)S(1)} %slice.476), channel_id=1, source_target_pairs={{0,16},{4,20},{8,24},{12,28},{16,0},{20,4},{24,8},{28,12},{1,17},{... | collective-permute-start | bytes 1572872 | tf_op jit(solution)/shard_map/ppermute | solution.py:39
  161.1 15.5 %collective-permute-start.23 = (bf16[128,2048]{1,0:T(8,128)(2,1)S(1)}, bf16[128,2048]{1,0:T(8,128)(2,1)S(1)}, u32[]{:S(2)}, u32[]{:S(2)}) collective-permute-start(bf16[128,2048]{1,0:T(8,128)(2,1)S(1)} %slice.477), channel_id=1, source_target_pairs={{0,8},{4,12},{8,0},{12,4},{16,24},{20,28},{24,16},{28,20},{1,9},{5... | collective-permute-start | bytes 1572872 | tf_op jit(solution)/shard_map/ppermute | solution.py:39
  167.9 16.9 %collective-permute-start.29 = (bf16[128,2048]{1,0:T(8,128)(2,1)}, bf16[128,2048]{1,0:T(8,128)(2,1)S(1)}, u32[]{:S(2)}, u32[]{:S(2)}) collective-permute-start(bf16[128,2048]{1,0:T(8,128)(2,1)} %slice.480), channel_id=1, source_target_pairs={{0,16},{4,20},{8,24},{12,28},{16,0},{20,4},{24,8},{28,12},{1,17},{... | collective-permute-start | bytes 1572872 | tf_op jit(solution)/shard_map/ppermute | solution.py:39
  168.1 17.6 %collective-permute-start.30 = (bf16[128,2048]{1,0:T(8,128)(2,1)}, bf16[128,2048]{1,0:T(8,128)(2,1)}, u32[]{:S(2)}, u32[]{:S(2)}) collective-permute-start(bf16[128,2048]{1,0:T(8,128)(2,1)} %slice.481), channel_id=1, source_target_pairs={{0,8},{4,12},{8,0},{12,4},{16,24},{20,28},{24,16},{28,20},{1,9},{5... | collective-permute-start | bytes 1572872 | tf_op jit(solution)/shard_map/ppermute | solution.py:39
  173.1 15.3 %collective-permute-start.19 = (bf16[512,1024]{1,0:T(8,128)(2,1)S(1)}, bf16[512,1024]{1,0:T(8,128)(2,1)S(1)}, u32[]{:S(2)}, u32[]{:S(2)}) collective-permute-start(bf16[512,1024]{1,0:T(8,128)(2,1)S(1)} %get-tuple-element.208), channel_id=1, source_target_pairs={{0,4},{4,0},{8,12},{12,8},{16,20},{20,16},{24,28},{28,24},{1,5},{5... | collective-permute-start | bytes 3145736 | tf_op jit(solution)/shard_map/ppermute | solution.py:39
  207.7 28.9 %copy-start.15 = (bf16[1024,2048]{1,0:T(8,128)(2,1)}, bf16[1024,2048]{1,0:T(8,128)(2,1)S(1)}, u32[]{:S(2)}) copy-start(bf16[1024,2048]{1,0:T(8,128)(2,1)S(1)} %convolution_convert_fusion.1) | copy-start | bytes 12582916
  207.9 12.4 %collective-permute-start.25 = (bf16[128,2048]{1,0:T(8,128)(2,1)S(1)}, bf16[128,2048]{1,0:T(8,128)(2,1)S(1)}, u32[]{:S(2)}, u32[]{:S(2)}) collective-permute-start(bf16[128,2048]{1,0:T(8,128)(2,1)S(1)} %get-tuple-element.221), channel_id=1, source_target_pairs={{0,16},{4,20},{8,24},{12,28},{16,0},{20,4},{24,8},{28,12},{1,17},{... | collective-permute-start | bytes 1572872 | tf_op jit(solution)/shard_map/ppermute | solution.py:39
  208.3 12.1 %collective-permute-start.26 = (bf16[128,2048]{1,0:T(8,128)(2,1)S(1)}, bf16[128,2048]{1,0:T(8,128)(2,1)S(1)}, u32[]{:S(2)}, u32[]{:S(2)}) collective-permute-start(bf16[128,2048]{1,0:T(8,128)(2,1)S(1)} %get-tuple-element.222), channel_id=1, source_target_pairs={{0,8},{4,12},{8,0},{12,4},{16,24},{20,28},{24,16},{28,20},{1,9},{5... | collective-permute-start | bytes 1572872 | tf_op jit(solution)/shard_map/ppermute | solution.py:39
  231.6 12.9 %collective-permute-start.31 = (bf16[512,1024]{1,0:T(8,128)(2,1)S(1)}, bf16[512,1024]{1,0:T(8,128)(2,1)S(1)}, u32[]{:S(2)}, u32[]{:S(2)}) collective-permute-start(bf16[512,1024]{1,0:T(8,128)(2,1)S(1)} %fusion.18), channel_id=1, source_target_pairs={{0,4},{4,0},{8,12},{12,8},{16,20},{20,16},{24,28},{28,24},{1,5},{5... | collective-permute-start | bytes 3145736 | tf_op jit(solution)/shard_map/ppermute | solution.py:39
  235.2 20.3 %collective-permute-start.36 = (bf16[128,2048]{1,0:T(8,128)(2,1)}, bf16[128,2048]{1,0:T(8,128)(2,1)}, u32[]{:S(2)}, u32[]{:S(2)}) collective-permute-start(bf16[128,2048]{1,0:T(8,128)(2,1)} %get-tuple-element.249), channel_id=1, source_target_pairs={{0,16},{4,20},{8,24},{12,28},{16,0},{20,4},{24,8},{28,12},{1,17},{... | collective-permute-start | bytes 1572872 | tf_op jit(solution)/shard_map/ppermute | solution.py:39
  236.4 19.2 %collective-permute-start.37 = (bf16[128,2048]{1,0:T(8,128)(2,1)}, bf16[128,2048]{1,0:T(8,128)(2,1)}, u32[]{:S(2)}, u32[]{:S(2)}) collective-permute-start(bf16[128,2048]{1,0:T(8,128)(2,1)} %get-tuple-element.250), channel_id=1, source_target_pairs={{0,8},{4,12},{8,0},{12,4},{16,24},{20,28},{24,16},{28,20},{1,9},{5... | collective-permute-start | bytes 1572872 | tf_op jit(solution)/shard_map/ppermute | solution.py:39
  243.0 29.4 %collective-permute-start.34 = (bf16[256,2048]{1,0:T(8,128)(2,1)}, bf16[256,2048]{1,0:T(8,128)(2,1)}, u32[]{:S(2)}, u32[]{:S(2)}) collective-permute-start(bf16[256,2048]{1,0:T(8,128)(2,1)} %pad_maximum_fusion.8), channel_id=1, source_target_pairs={{0,8},{4,12},{8,0},{12,4},{16,24},{20,28},{24,16},{28,20},{1,9},{5... | collective-permute-start | bytes 3145736 | tf_op jit(solution)/shard_map/ppermute | solution.py:39
  244.2 28.2 %collective-permute-start.35 = (bf16[256,2048]{1,0:T(8,128)(2,1)}, bf16[256,2048]{1,0:T(8,128)(2,1)}, u32[]{:S(2)}, u32[]{:S(2)}) collective-permute-start(bf16[256,2048]{1,0:T(8,128)(2,1)} %pad_maximum_fusion.9), channel_id=1, source_target_pairs={{0,16},{4,20},{8,24},{12,28},{16,0},{20,4},{24,8},{28,12},{1,17},{... | collective-permute-start | bytes 3145736 | tf_op jit(solution)/shard_map/ppermute | solution.py:39
  250.7 21.7 %collective-permute-start.38 = (bf16[512,1024]{1,0:T(8,128)(2,1)S(1)}, bf16[512,1024]{1,0:T(8,128)(2,1)}, u32[]{:S(2)}, u32[]{:S(2)}) collective-permute-start(bf16[512,1024]{1,0:T(8,128)(2,1)S(1)} %get-tuple-element.253), channel_id=1, source_target_pairs={{0,4},{4,0},{8,12},{12,8},{16,20},{20,16},{24,28},{28,24},{1,5},{5... | collective-permute-start | bytes 3145736 | tf_op jit(solution)/shard_map/ppermute | solution.py:39
  261.4 61.5 %collective-permute-start.32 = (bf16[512,1024]{1,0:T(8,128)(2,1)}, bf16[512,1024]{1,0:T(8,128)(2,1)S(1)}, u32[]{:S(2)}, u32[]{:S(2)}) collective-permute-start(bf16[512,1024]{1,0:T(8,128)(2,1)} %fusion.21), channel_id=1, source_target_pairs={{0,4},{4,0},{8,12},{12,8},{16,20},{20,16},{24,28},{28,24},{1,5},{5... | collective-permute-start | bytes 3145736 | tf_op jit(solution)/shard_map/ppermute | solution.py:39
  321.1 8.9 %collective-permute-start.43 = (bf16[256,512]{1,0:T(8,128)(2,1)}, bf16[256,512]{1,0:T(8,128)(2,1)}, u32[]{:S(2)}, u32[]{:S(2)}) collective-permute-start(bf16[256,512]{1,0:T(8,128)(2,1)} %get-tuple-element.271), channel_id=1, source_target_pairs={{0,1},{1,2},{2,3},{3,0},{4,5},{5,6},{6,7},{7,4},{8,9},{9,10},{10,1... | collective-permute-start | bytes 786440 | tf_op jit(solution)/shard_map/ppermute | solution.py:48
  321.1 36.4 %collective-permute-start.39 = (bf16[256,2048]{1,0:T(8,128)(2,1)}, bf16[256,2048]{1,0:T(8,128)(2,1)}, u32[]{:S(2)}, u32[]{:S(2)}) collective-permute-start(bf16[256,2048]{1,0:T(8,128)(2,1)} %pad_maximum_fusion.10), channel_id=1, source_target_pairs={{0,8},{4,12},{8,0},{12,4},{16,24},{20,28},{24,16},{28,20},{1,9},{5... | collective-permute-start | bytes 3145736 | tf_op jit(solution)/shard_map/ppermute | solution.py:39
  321.3 36.2 %collective-permute-start.40 = (bf16[256,2048]{1,0:T(8,128)(2,1)}, bf16[256,2048]{1,0:T(8,128)(2,1)}, u32[]{:S(2)}, u32[]{:S(2)}) collective-permute-start(bf16[256,2048]{1,0:T(8,128)(2,1)} %pad_maximum_fusion.11), channel_id=1, source_target_pairs={{0,16},{4,20},{8,24},{12,28},{16,0},{20,4},{24,8},{28,12},{1,17},{... | collective-permute-start | bytes 3145736 | tf_op jit(solution)/shard_map/ppermute | solution.py:39
  321.6 20.2 %copy-start.41 = (bf16[256,512]{1,0:T(8,128)(2,1)S(1)}, bf16[256,512]{1,0:T(8,128)(2,1)}, u32[]{:S(2)}) copy-start(bf16[256,512]{1,0:T(8,128)(2,1)} %get-tuple-element.273) | copy-start | bytes 786436
  321.6 20.2 %collective-permute-start.44 = (bf16[256,512]{1,0:T(8,128)(2,1)}, bf16[256,512]{1,0:T(8,128)(2,1)S(1)}, u32[]{:S(2)}, u32[]{:S(2)}) collective-permute-start(bf16[256,512]{1,0:T(8,128)(2,1)} %get-tuple-element.272), channel_id=1, source_target_pairs={{0,2},{1,3},{2,0},{3,1},{4,6},{5,7},{6,4},{7,5},{8,10},{9,11},{10,... | collective-permute-start | bytes 786440 | tf_op jit(solution)/shard_map/ppermute | solution.py:48
  322.9 33.2 %collective-permute-start.41 = (bf16[128,2048]{1,0:T(8,128)(2,1)}, bf16[128,2048]{1,0:T(8,128)(2,1)S(1)}, u32[]{:S(2)}, u32[]{:S(2)}) collective-permute-start(bf16[128,2048]{1,0:T(8,128)(2,1)} %pad_maximum_fusion.13), channel_id=1, source_target_pairs={{0,16},{4,20},{8,24},{12,28},{16,0},{20,4},{24,8},{28,12},{1,17},{... | collective-permute-start | bytes 1572872 | tf_op jit(solution)/shard_map/ppermute | solution.py:39
  330.0 27.5 %collective-permute-start.42 = (bf16[144,2048]{1,0:T(8,128)(2,1)}, bf16[144,2048]{1,0:T(8,128)(2,1)S(1)}, u32[]{:S(2)}, u32[]{:S(2)}) collective-permute-start(bf16[144,2048]{1,0:T(8,128)(2,1)} %pad_maximum_fusion.12), channel_id=1, source_target_pairs={{0,8},{4,12},{8,0},{12,4},{16,24},{20,28},{24,16},{28,20},{1,9},{5... | collective-permute-start | bytes 1769480 | tf_op jit(solution)/shard_map/ppermute | solution.py:39
  341.8 6.9 %collective-permute-start.45 = (bf16[256,512]{1,0:T(8,128)(2,1)S(1)}, bf16[256,512]{1,0:T(8,128)(2,1)S(1)}, u32[]{:S(2)}, u32[]{:S(2)}) collective-permute-start(bf16[256,512]{1,0:T(8,128)(2,1)S(1)} %copy-done.41), channel_id=1, source_target_pairs={{0,3},{1,0},{2,1},{3,2},{4,7},{5,4},{6,5},{7,6},{8,11},{9,8},{10,9... | collective-permute-start | bytes 786440 | tf_op jit(solution)/shard_map/ppermute | solution.py:48
  348.8 22.8 %collective-permute-start.33 = (bf16[512,1024]{1,0:T(8,128)(2,1)S(1)}, bf16[512,1024]{1,0:T(8,128)(2,1)S(1)}, u32[]{:S(2)}, u32[]{:S(2)}) collective-permute-start(bf16[512,1024]{1,0:T(8,128)(2,1)S(1)} %get-tuple-element.241), channel_id=1, source_target_pairs={{1,4},{3,6},{4,1},{6,3},{9,12},{11,14},{12,9},{14,11},{17,20},{19,... | collective-permute-start | bytes 3145736 | tf_op jit(solution)/shard_map/ppermute | solution.py:58
  361.5 13.1 %collective-permute-start.50 = (bf16[256,512]{1,0:T(8,128)(2,1)S(1)}, bf16[256,512]{1,0:T(8,128)(2,1)S(1)}, u32[]{:S(2)}, u32[]{:S(2)}) collective-permute-start(bf16[256,512]{1,0:T(8,128)(2,1)S(1)} %get-tuple-element.285), channel_id=1, source_target_pairs={{0,1},{1,2},{2,3},{3,0},{4,5},{5,6},{6,7},{7,4},{8,9},{9,10},{10,1... | collective-permute-start | bytes 786440 | tf_op jit(solution)/shard_map/ppermute | solution.py:48
  362.8 19.5 %collective-permute-start.51 = (bf16[256,512]{1,0:T(8,128)(2,1)S(1)}, bf16[256,512]{1,0:T(8,128)(2,1)S(1)}, u32[]{:S(2)}, u32[]{:S(2)}) collective-permute-start(bf16[256,512]{1,0:T(8,128)(2,1)S(1)} %get-tuple-element.286), channel_id=1, source_target_pairs={{0,2},{1,3},{2,0},{3,1},{4,6},{5,7},{6,4},{7,5},{8,10},{9,11},{10,... | collective-permute-start | bytes 786440 | tf_op jit(solution)/shard_map/ppermute | solution.py:48
  364.9 23.2 %collective-permute-start.48 = (bf16[272,2048]{1,0:T(8,128)(2,1)S(1)}, bf16[272,2048]{1,0:T(8,128)(2,1)S(1)}, u32[]{:S(2)}, u32[]{:S(2)}) collective-permute-start(bf16[272,2048]{1,0:T(8,128)(2,1)S(1)} %pad_maximum_fusion.5), channel_id=1, source_target_pairs={{0,8},{4,12},{8,0},{12,4},{16,24},{20,28},{24,16},{28,20},{1,9},{5... | collective-permute-start | bytes 3342344 | tf_op jit(solution)/shard_map/ppermute | solution.py:39
  365.1 23.0 %collective-permute-start.49 = (bf16[272,2048]{1,0:T(8,128)(2,1)S(1)}, bf16[272,2048]{1,0:T(8,128)(2,1)S(1)}, u32[]{:S(2)}, u32[]{:S(2)}) collective-permute-start(bf16[272,2048]{1,0:T(8,128)(2,1)S(1)} %pad_maximum_fusion.6), channel_id=1, source_target_pairs={{0,16},{4,20},{8,24},{12,28},{16,0},{20,4},{24,8},{28,12},{1,17},{... | collective-permute-start | bytes 3342344 | tf_op jit(solution)/shard_map/ppermute | solution.py:39
  371.6 10.7 %collective-permute-start.52 = (bf16[256,512]{1,0:T(8,128)(2,1)S(1)}, bf16[256,512]{1,0:T(8,128)(2,1)S(1)}, u32[]{:S(2)}, u32[]{:S(2)}) collective-permute-start(bf16[256,512]{1,0:T(8,128)(2,1)S(1)} %get-tuple-element.287), channel_id=1, source_target_pairs={{0,3},{1,0},{2,1},{3,2},{4,7},{5,4},{6,5},{7,6},{8,11},{9,8},{10,9... | collective-permute-start | bytes 786440 | tf_op jit(solution)/shard_map/ppermute | solution.py:48
  372.2 15.9 %copy-start.22 = (bf16[128,1536]{1,0:T(8,128)(2,1)S(1)}, bf16[128,1536]{1,0:T(8,128)(2,1)}, u32[]{:S(2)}) copy-start(bf16[128,1536]{1,0:T(8,128)(2,1)} %get-tuple-element.338) | copy-start | bytes 1179652
  372.2 15.9 %copy-start.23 = (bf16[128,1536]{1,0:T(8,128)(2,1)S(1)}, bf16[128,1536]{1,0:T(8,128)(2,1)}, u32[]{:S(2)}) copy-start(bf16[128,1536]{1,0:T(8,128)(2,1)} %get-tuple-element.343) | copy-start | bytes 1179652
  374.6 38.4 %collective-permute-start.46 = (bf16[512,1024]{1,0:T(8,128)(2,1)S(1)}, bf16[512,1024]{1,0:T(8,128)(2,1)S(1)}, u32[]{:S(2)}, u32[]{:S(2)}) collective-permute-start(bf16[512,1024]{1,0:T(8,128)(2,1)S(1)} %fusion.15), channel_id=1, source_target_pairs={{0,4},{4,0},{8,12},{12,8},{16,20},{20,16},{24,28},{28,24},{1,5},{5... | collective-permute-start | bytes 3145736 | tf_op jit(solution)/shard_map/ppermute | solution.py:39
  389.0 8.2 %collective-permute-start.53 = (bf16[272,512]{1,0:T(8,128)(2,1)S(1)}, bf16[272,512]{1,0:T(8,128)(2,1)S(1)}, u32[]{:S(2)}, u32[]{:S(2)}) collective-permute-start(bf16[272,512]{1,0:T(8,128)(2,1)S(1)} %pad_maximum_fusion.16), channel_id=1, source_target_pairs={{0,1},{1,2},{2,3},{3,0},{4,5},{5,6},{6,7},{7,4},{8,9},{9,10},{10,1... | collective-permute-start | bytes 835592 | tf_op jit(solution)/shard_map/ppermute | solution.py:48
  389.6 21.1 %collective-permute-start.54 = (bf16[272,512]{1,0:T(8,128)(2,1)S(1)}, bf16[272,512]{1,0:T(8,128)(2,1)S(1)}, u32[]{:S(2)}, u32[]{:S(2)}) collective-permute-start(bf16[272,512]{1,0:T(8,128)(2,1)S(1)} %pad_maximum_fusion.17), channel_id=1, source_target_pairs={{0,2},{1,3},{2,0},{3,1},{4,6},{5,7},{6,4},{7,5},{8,10},{9,11},{10,... | collective-permute-start | bytes 835592 | tf_op jit(solution)/shard_map/ppermute | solution.py:48
  389.9 20.8 %collective-permute-start.55 = (bf16[272,512]{1,0:T(8,128)(2,1)S(1)}, bf16[272,512]{1,0:T(8,128)(2,1)S(1)}, u32[]{:S(2)}, u32[]{:S(2)}) collective-permute-start(bf16[272,512]{1,0:T(8,128)(2,1)S(1)} %pad_maximum_fusion.18), channel_id=1, source_target_pairs={{0,3},{1,0},{2,1},{3,2},{4,7},{5,4},{6,5},{7,6},{8,11},{9,8},{10,9... | collective-permute-start | bytes 835592 | tf_op jit(solution)/shard_map/ppermute | solution.py:48
  392.5 33.6 %collective-permute-start.57 = (f32[128,512]{1,0:T(8,128)S(1)}, f32[128,512]{1,0:T(8,128)S(1)}, u32[]{:S(2)}, u32[]{:S(2)}) collective-permute-start(f32[128,512]{1,0:T(8,128)S(1)} %get-tuple-element.302), channel_id=1, source_target_pairs={{0,4},{4,0},{8,12},{12,8},{16,20},{20,16},{24,28},{28,24},{1,5},{5... | collective-permute-start | bytes 786440 | tf_op jit(solution)/shard_map/ppermute | solution.py:39
  397.1 29.0 %collective-permute-start.58 = (f32[128,512]{1,0:T(8,128)S(1)}, f32[128,512]{1,0:T(8,128)S(1)}, u32[]{:S(2)}, u32[]{:S(2)}) collective-permute-start(f32[128,512]{1,0:T(8,128)S(1)} %get-tuple-element.303), channel_id=1, source_target_pairs={{0,4},{4,0},{8,12},{12,8},{16,20},{20,16},{24,28},{28,24},{1,5},{5... | collective-permute-start | bytes 786440 | tf_op jit(solution)/shard_map/ppermute | solution.py:39
  411.6 16.2 %collective-permute-start.56 = (f32[144,512]{1,0:T(8,128)}, f32[144,512]{1,0:T(8,128)S(1)}, u32[]{:S(2)}, u32[]{:S(2)}) collective-permute-start(f32[144,512]{1,0:T(8,128)} %pad_maximum_fusion.14), channel_id=1, source_target_pairs={{0,4},{4,0},{8,12},{12,8},{16,20},{20,16},{24,28},{28,24},{1,5},{5... | collective-permute-start | bytes 884744 | tf_op jit(solution)/shard_map/ppermute | solution.py:39
  418.5 20.0 %collective-permute-start.47 = (bf16[512,1024]{1,0:T(8,128)(2,1)S(1)}, bf16[512,1024]{1,0:T(8,128)(2,1)S(1)}, u32[]{:S(2)}, u32[]{:S(2)}) collective-permute-start(bf16[512,1024]{1,0:T(8,128)(2,1)S(1)} %get-tuple-element.278), channel_id=1, source_target_pairs={{1,4},{3,6},{4,1},{6,3},{9,12},{11,14},{12,9},{14,11},{17,20},{19,... | collective-permute-start | bytes 3145736 | tf_op jit(solution)/shard_map/ppermute | solution.py:58
  (47 other events, 174.3 us)

commit v3 on v2

--- a/solution.py
+++ b/solution.py
@@ -713,7 +713,7 @@
 def up_forward(rows, weight, bias):
     count, depth = rows.shape
     width = weight.shape[1]
-    step = min(256, width)
+    step = min(512, width)
 
     def body(x_ref, w_ref, b_ref, act_ref, slope_ref):
         u = dot_nn(x_ref[...], w_ref[...]) + b_ref[...]
@@ -745,7 +745,7 @@
 def up_backward(cot_rows, weight, slope):
     count, depth = cot_rows.shape
     width = weight.shape[1]
-    step = min(256, width)
+    step = min(512, width)
 
     def body(x_ref, w_ref, slope_ref, out_ref, sum_ref):
         grad = (dot_nn(x_ref[...], w_ref[...]) * slope_ref[...].astype(F32)).astype(BF)

time: 449 us -> 448 us (level)
  no operation moved by 1% of the time
where the time goes in v3:
time: 448 us; the launch traced here: 443 us
  waiting for transfers between devices  122 us (27%)
  Pallas kernels  95.8 us (21%)
  starting transfers between devices  82 us (18%)
  local copies, waits for them, and re-layouts  66.4 us (15%)
  matrix products  48 us (11%)
  other arithmetic  26.1 us (6%)
    ppermute x18, waiting for transfers between devices, from_tensor(): lax.ppermute(values, 'tensor', [(i, (i - step) % size) for i in range(siz...  59.8 us
    ppermute x37, waiting for transfers between devices, swap_bit(): return lax.ppermute(values, 'dp', [(i, i ^ 1 << bit) for i in range(size)])  44.9 us
    ppermute x37, starting transfers between devices, swap_bit(): return lax.ppermute(values, 'dp', [(i, i ^ 1 << bit) for i in range(size)])  43.8 us
    unnamed x132, local copies, waits for them, and re-layouts  38 us
    dot_general x8, matrix products, dot_nt(): lax.dot_general(left, right, (((1,), (1,)), ((), ())), preferred_element_...  26.9 us
    pallas_call x9, Pallas kernels, row_call(): pl.pallas_call(body, grid=(tokens // step,), in_specs=[pl.BlockSpec(memor...  24.5 us
    pallas_call x1, Pallas kernels, attend_back(): pl.pallas_call(functools.partial(attend_back_kernel, first), grid=(groups...  20.9 us
    ppermute x18, starting transfers between devices, from_tensor(): lax.ppermute(values, 'tensor', [(i, (i - step) % size) for i in range(siz...  20.2 us
  transfers between devices with their start and end apart: 59, of which 21 were waited for; matrix products, arithmetic and copies ran while one was open for 22% of the time, Pallas kernels for 18%

profile of v3, /device:TPU:1, one launch (start us, length us, event | category | flops | bytes accessed | tf_op | source)
XLA Modules:
  0.0 442.6 jit_solution(5688387457437374631)
XLA Ops:
  2.2 4.1 concatenate.140
  14.6 4.8 %collective-permute-start.2 = (bf16[272,512]{1,0:T(8,128)(2,1)S(1)}, bf16[272,512]{1,0:T(8,128)(2,1)S(1)}, u32[]{:S(2)}, u32[]{:S(2)}) collective-permute-start(bf16[272,512]{1,0:T(8,128)(2,1)S(1)} %pad_maximum_fusion.15), channel_id=1, source_target_pairs={{0,3},{1,0},{2,1},{3,2},{4,7},{5,4},{6,5},{7,6},{8,11},{9,8},{10,9... | collective-permute-start | bytes 835592 | tf_op jit(solution)/shard_map/ppermute | solution.py:48
  20.0 5.6 %collective-permute-done.2 = bf16[272,512]{1,0:T(8,128)(2,1)S(1)} collective-permute-done((bf16[272,512]{1,0:T(8,128)(2,1)S(1)}, bf16[272,512]{1,0:T(8,128)(2,1)S(1)}, u32[]{:S(2)}, u32[]{:S(2)}) %collective-permute-start.2) | collective-permute-done | bytes 278560 | tf_op jit(solution)/shard_map/ppermute | solution.py:48
  25.6 17.7 %collective-permute-done.3 = bf16[272,512]{1,0:T(8,128)(2,1)S(1)} collective-permute-done((bf16[272,512]{1,0:T(8,128)(2,1)S(1)}, bf16[272,512]{1,0:T(8,128)(2,1)S(1)}, u32[]{:S(2)}, u32[]{:S(2)}) %collective-permute-start.3) | collective-permute-done | bytes 278560 | tf_op jit(solution)/shard_map/ppermute | solution.py:48
  43.8 2.3 collective-permute-start.9
  46.0 4.9 %collective-permute-start.5 = (bf16[512,1024]{1,0:T(8,128)(2,1)S(1)}, bf16[512,1024]{1,0:T(8,128)(2,1)S(1)}, u32[]{:S(2)}, u32[]{:S(2)}) collective-permute-start(bf16[512,1024]{1,0:T(8,128)(2,1)S(1)} %rows_low.2), channel_id=1, source_target_pairs={{1,4},{3,6},{4,1},{6,3},{9,12},{11,14},{12,9},{14,11},{17,20},{19,... | collective-permute-start | bytes 3145736 | tf_op jit(solution)/shard_map/ppermute | solution.py:58
  54.3 14.7 %collective-permute-done.5.swapped_ref = bf16[512,1024]{1,0:T(8,128)(2,1)S(1)} collective-permute-done((bf16[512,1024]{1,0:T(8,128)(2,1)S(1)}, bf16[512,1024]{1,0:T(8,128)(2,1)S(1)}, u32[]{:S(2)}, u32[]{:S(2)}) %collective-permute-start.5) | collective-permute-done | bytes 1048608 | tf_op jit(solution)/shard_map/ppermute | solution.py:58
  68.9 2.9 rows_first.1
  71.9 6.1 %collective-permute-done.10 = bf16[256,512]{1,0:T(8,128)(2,1)S(1)} collective-permute-done((bf16[256,512]{1,0:T(8,128)(2,1)S(1)}, bf16[256,512]{1,0:T(8,128)(2,1)S(1)}, u32[]{:S(2)}, u32[]{:S(2)}) %collective-permute-start.10) | collective-permute-done | bytes 262176 | tf_op jit(solution)/shard_map/ppermute | solution.py:48
  79.4 1.9 collective-permute-start.13
  82.9 8.9 %collective-permute-done.11 = bf16[128,2048]{1,0:T(8,128)(2,1)S(1)} collective-permute-done((bf16[128,2048]{1,0:T(8,128)(2,1)S(1)}, bf16[128,2048]{1,0:T(8,128)(2,1)S(1)}, u32[]{:S(2)}, u32[]{:S(2)}) %collective-permute-start.11) | collective-permute-done | bytes 524320 | tf_op jit(solution)/shard_map/ppermute | solution.py:39
  91.8 4.1 collective-permute-done.12
  100.6 1.9 spread_small.1
  102.6 2.5 collective-permute-start.15
  110.9 6.5 %add_convert_fusion.qkv_ref = bf16[1024,1536]{1,0:T(8,128)(2,1)S(1)} fusion(bf16[1024,1536]{1,0:T(8,128)(2,1)} %copy-done.43, f32[1536]{0:T(1024)S(1)} %reduce, f32[1024]{0:T(1024)S(1)} %bitcast.76, f32[1024]{0:T(1024)S(1)} %bitcast.75, bf16[512,1024]{1,0:T(8,128)(2,1)S(1)} %copy-done.18, bf16[512,1024]{1,0:T(8,128)(2,1)S(1)} %get-tuple-element.348), kind=kOutput, calls=%fused_computation | convolution fusion | flops 3231711232 | bytes 8402944 | tf_op jit(solution)/shard_map/dot_general | solution.py:26
  118.6 3.0 constant_dynamic-update-slice_fusion.14
  121.6 2.7 collective-permute-start.24
  124.2 4.7 %collective-permute-done.16 = bf16[256,512]{1,0:T(8,128)(2,1)} collective-permute-done((bf16[256,512]{1,0:T(8,128)(2,1)}, bf16[256,512]{1,0:T(8,128)(2,1)}, u32[]{:S(2)}, u32[]{:S(2)}) %collective-permute-start.16) | collective-permute-done | bytes 262176 | tf_op jit(solution)/shard_map/ppermute | solution.py:48
  131.7 17.0 %attend.1 = (bf16[1024,512]{1,0:T(8,128)(2,1)S(1)}, f32[4,2,1024]{2,1,0:T(2,128)S(1)}) custom-call(f32[4,2]{1,0:T(4,128)S(1)} %multiply_exponential_fusion.slope_ref, bf16[1024,1536]{1,0:T(8,128)(2,1)S(1)} %add_convert_fusion.qkv_ref, bf16[256,512]{1,0:T(8,128)(2,1)S(1)} %collective-permute-done.15.refs_0_), custom_call_target="tpu_custom_call" | custom-call | flops 9900000256 | bytes 9000000 | tf_op jit(solution)/shard_map/attend/pallas_call | solution.py:261
  149.4 2.3 collective-permute-start.18
  161.5 2.3 constant_dynamic-update-slice_fusion.13
  163.8 2.3 constant_dynamic-update-slice_fusion.12
  170.1 3.0 rows_mid.1
  178.4 6.4 %collective-permute-done.29 = bf16[128,2048]{1,0:T(8,128)(2,1)S(1)} collective-permute-done((bf16[128,2048]{1,0:T(8,128)(2,1)}, bf16[128,2048]{1,0:T(8,128)(2,1)S(1)}, u32[]{:S(2)}, u32[]{:S(2)}) %collective-permute-start.29) | collective-permute-done | bytes 524320 | tf_op jit(solution)/shard_map/ppermute | solution.py:39
  186.5 1.9 constant_dynamic-update-slice_fusion.15.w_ref
  188.5 11.6 %up_forward.1 = (bf16[1024,2048]{1,0:T(8,128)(2,1)}, bf16[1024,2048]{1,0:T(8,128)(2,1)}) custom-call(bf16[1024,1024]{1,0:T(8,128)(2,1)S(1)} %constant_dynamic-update-slice_fusion.8.x_ref, bf16[1024,2048]{1,0:T(8,128)(2,1)} %constant_dynamic-update-slice_fusion.10.w_ref, f32[1,2048]{1,0:T(1,128)S(1)} %get-tuple-element.218.b_ref), custom_call_target="tpu_custom_call" | custom-call | flops 13200000000 | bytes 12000000 | tf_op jit(solution)/shard_map/up_forward/pallas_call | solution.py:729
  200.1 7.2 %convolution_convert_fusion.1 = bf16[1024,2048]{1,0:T(8,128)(2,1)S(1)} fusion(bf16[1024,2048]{1,0:T(8,128)(2,1)} %get-tuple-element.239, bf16[512,1024]{1,0:T(8,128)(2,1)S(1)} %collective-permute-done.24, bf16[512,1024]{1,0:T(8,128)(2,1)S(1)} %copy-done.19), kind=kOutput, calls=%fused_computation.3 | convolution fusion | flops 4301258752 | bytes 10485760 | tf_op jit(solution)/shard_map/dot_general | solution.py:30
  208.2 9.2 %up_backward.1 = (bf16[1024,2048]{1,0:T(8,128)(2,1)}, f32[1,2048]{1,0:T(1,128)S(1)}) custom-call(bf16[1024,1024]{1,0:T(8,128)(2,1)S(1)} %pad_maximum_fusion.1.x_ref, bf16[1024,2048]{1,0:T(8,128)(2,1)} %constant_dynamic-update-slice_fusion.15.w_ref, bf16[1024,2048]{1,0:T(8,128)(2,1)} %get-tuple-element.235.slope_ref), custom_call_target="tpu_custom_call" | custom-call | flops 11000000512 | bytes 10000000 | tf_op jit(solution)/shard_map/up_backward/pallas_call | solution.py:756
  217.4 2.5 collective-permute-done.25
  220.9 5.3 %fusion.18 = bf16[512,1024]{1,0:T(8,128)(2,1)S(1)} fusion(bf16[1024,2048]{1,0:T(8,128)(2,1)} %constant_dynamic-update-slice_fusion.10.w_ref, bf16[1024,2048]{1,0:T(8,128)(2,1)} %get-tuple-element.237), kind=kOutput, calls=%fused_computation.31 | convolution fusion | flops 2148007936 | bytes 7340032 | tf_op jit(solution)/shard_map/dot_general | solution.py:34
  226.2 4.9 %convolution_convert_fusion = bf16[1024,2048]{1,0:T(8,128)(2,1)S(1)} fusion(bf16[1024,1024]{1,0:T(8,128)(2,1)S(1)} %constant_dynamic-update-slice_fusion.8.x_ref, bf16[1024,2048]{1,0:T(8,128)(2,1)S(1)} %copy-done.50), kind=kOutput, calls=%fused_computation.2 | convolution fusion | flops 4297064448 | bytes 10485760 | tf_op jit(solution)/shard_map/dot_general | solution.py:30
  231.2 2.2 collective-permute-start.31
  237.7 3.7 fusion.7.own_ref
  244.1 4.9 %rows_mid_back.1 = (f32[512,1024]{1,0:T(8,128)S(1)}, bf16[512,1024]{1,0:T(8,128)(2,1)S(1)}, f32[8,1024]{1,0:T(8,128)S(1)}) custom-call(s32[4]{0:T(128)S(1)} %pad_add_fusion.ids_ref, f32[512,1024]{1,0:T(8,128)} %cot_ref.1, bf16[512,1024]{1,0:T(8,128)(2,1)S(1)} %collective-permute-done.13.swapped_ref, f32[512,1024]{1,0:T(8,128)} %copy-done.9, ...), custom_call_target="tpu_custom_call" | custom-call | flops 3300000000 | bytes 3000000 | tf_op jit(solution)/shard_map/rows_mid_back/pallas_call | solution.py:408
  256.0 4.9 %fusion.21 = bf16[512,1024]{1,0:T(8,128)(2,1)} fusion(bf16[1024,2048]{1,0:T(8,128)(2,1)S(1)} %copy-done.49, bf16[1024,2048]{1,0:T(8,128)(2,1)} %get-tuple-element.239), kind=kOutput, calls=%fused_computation.32 | convolution fusion | flops 2148007936 | bytes 7340032 | tf_op jit(solution)/shard_map/dot_general | solution.py:34
  261.0 11.0 %collective-permute-done.34 = bf16[256,2048]{1,0:T(8,128)(2,1)} collective-permute-done((bf16[256,2048]{1,0:T(8,128)(2,1)}, bf16[256,2048]{1,0:T(8,128)(2,1)}, u32[]{:S(2)}, u32[]{:S(2)}) %collective-permute-start.34) | collective-permute-done | bytes 1048608 | tf_op jit(solution)/shard_map/ppermute | solution.py:39
  276.8 20.9 %attend_back.1 = (bf16[1024,1536]{1,0:T(8,128)(2,1)S(1)}, f32[4,1,384]{2,1,0:T(1,128)S(1)}) custom-call(f32[4,2]{1,0:T(4,128)S(1)} %multiply_exponential_fusion.slope_ref, bf16[1024,1536]{1,0:T(8,128)(2,1)} %copy-done.13, bf16[1024,512]{1,0:T(8,128)(2,1)S(1)} %convolution_convert_fusion.3.grad_ref, f32[4,2,1024]{2,1,0:T(2,128)S(1)} %get-tuple-element.254.lse_ref, ...), custom_call_target="tpu_custom_call" | custom-call | flops 12099999744 | bytes 11000000 | tf_op jit(solution)/shard_map/attend_back/pallas_call | solution.py:331
  299.4 7.6 %qkv_grads.1 = (bf16[1024,1536]{1,0:T(8,128)(2,1)S(1)}, f32[8,1024]{1,0:T(8,128)S(1)}) custom-call(bf16[1024,1024]{1,0:T(8,128)(2,1)S(1)} %pad_maximum_fusion.z_ref, bf16[1024,1536]{1,0:T(8,128)(2,1)} %copy-done.6, bf16[1024,1536]{1,0:T(8,128)(2,1)} %copy-done.43, f32[1,1536]{1,0:T(1,128)S(1)} %bitcast.65, f32[1024,128]{1,0:T(8,128)S(1)} %pad.14.vec_ref), custom_call_target="tpu_custom_call" | custom-call | flops 5500000256 | bytes 5000000 | tf_op jit(solution)/shard_map/qkv_grads/pallas_call | solution.py:666
  307.1 2.3 pack_rows.1
  311.5 2.4 fusion.55
  313.9 1.9 add_convert_fusion.6
  323.6 6.0 %collective-permute-done.43 = bf16[256,512]{1,0:T(8,128)(2,1)} collective-permute-done((bf16[256,512]{1,0:T(8,128)(2,1)}, bf16[256,512]{1,0:T(8,128)(2,1)}, u32[]{:S(2)}, u32[]{:S(2)}) %collective-permute-start.43) | collective-permute-done | bytes 262176 | tf_op jit(solution)/shard_map/ppermute | solution.py:48
  329.8 6.5 %fusion.3.own_ref = f32[512,1024]{1,0:T(8,128)} fusion(bf16[1024,2048]{1,0:T(8,128)(2,1)} %constant_dynamic-update-slice_fusion.15.w_ref, bf16[1024,2048]{1,0:T(8,128)(2,1)} %get-tuple-element.239), kind=kOutput, calls=%fused_computation.14 | convolution fusion | flops 2147483648 | bytes 8388608 | tf_op jit(solution)/shard_map/dot_general | solution.py:34
  336.3 5.1 %collective-permute-done.44 = bf16[256,512]{1,0:T(8,128)(2,1)S(1)} collective-permute-done((bf16[256,512]{1,0:T(8,128)(2,1)}, bf16[256,512]{1,0:T(8,128)(2,1)S(1)}, u32[]{:S(2)}, u32[]{:S(2)}) %collective-permute-start.44) | collective-permute-done | bytes 262176 | tf_op jit(solution)/shard_map/ppermute | solution.py:48
  341.4 3.1 rows_out.1
  344.5 3.9 collective-permute-done.45
  348.3 3.7 collective-permute-start.33
  352.0 3.6 collective-permute-done.41
  357.1 2.5 fusion.54
  362.4 2.0 collective-permute-start.51
  366.2 1.8 fusion.15
  368.0 3.1 fusion.13.own_ref
  371.8 2.4 rows_home.2
  374.2 3.1 collective-permute-start.46
  377.4 4.6 %collective-permute-done.51 = bf16[256,512]{1,0:T(8,128)(2,1)S(1)} collective-permute-done((bf16[256,512]{1,0:T(8,128)(2,1)S(1)}, bf16[256,512]{1,0:T(8,128)(2,1)S(1)}, u32[]{:S(2)}, u32[]{:S(2)}) %collective-permute-start.51) | collective-permute-done | bytes 262176 | tf_op jit(solution)/shard_map/ppermute | solution.py:48
  381.9 5.8 %collective-permute-done.48 = bf16[272,2048]{1,0:T(8,128)(2,1)S(1)} collective-permute-done((bf16[272,2048]{1,0:T(8,128)(2,1)S(1)}, bf16[272,2048]{1,0:T(8,128)(2,1)S(1)}, u32[]{:S(2)}, u32[]{:S(2)}) %collective-permute-start.48) | collective-permute-done | bytes 1114144 | tf_op jit(solution)/shard_map/ppermute | solution.py:39
  389.5 2.4 collective-permute-start.55
  392.1 4.6 %collective-permute-start.57 = (f32[128,512]{1,0:T(8,128)S(1)}, f32[128,512]{1,0:T(8,128)S(1)}, u32[]{:S(2)}, u32[]{:S(2)}) collective-permute-start(f32[128,512]{1,0:T(8,128)S(1)} %get-tuple-element.302), channel_id=1, source_target_pairs={{0,4},{4,0},{8,12},{12,8},{16,20},{20,16},{24,28},{28,24},{1,5},{5... | collective-permute-start | bytes 786440 | tf_op jit(solution)/shard_map/ppermute | solution.py:39
  396.7 7.4 %collective-permute-start.58 = (f32[128,512]{1,0:T(8,128)S(1)}, f32[128,512]{1,0:T(8,128)S(1)}, u32[]{:S(2)}, u32[]{:S(2)}) collective-permute-start(f32[128,512]{1,0:T(8,128)S(1)} %get-tuple-element.303), channel_id=1, source_target_pairs={{0,4},{4,0},{8,12},{12,8},{16,20},{20,16},{24,28},{28,24},{1,5},{5... | collective-permute-start | bytes 786440 | tf_op jit(solution)/shard_map/ppermute | solution.py:39
  404.1 6.2 %collective-permute-done.54 = bf16[272,512]{1,0:T(8,128)(2,1)S(1)} collective-permute-done((bf16[272,512]{1,0:T(8,128)(2,1)S(1)}, bf16[272,512]{1,0:T(8,128)(2,1)S(1)}, u32[]{:S(2)}, u32[]{:S(2)}) %collective-permute-start.54) | collective-permute-done | bytes 278560 | tf_op jit(solution)/shard_map/ppermute | solution.py:48
  412.7 4.2 rows_first_back.1
  418.2 7.5 %collective-permute-start.47 = (bf16[512,1024]{1,0:T(8,128)(2,1)S(1)}, bf16[512,1024]{1,0:T(8,128)(2,1)S(1)}, u32[]{:S(2)}, u32[]{:S(2)}) collective-permute-start(bf16[512,1024]{1,0:T(8,128)(2,1)S(1)} %get-tuple-element.278), channel_id=1, source_target_pairs={{1,4},{3,6},{4,1},{6,3},{9,12},{11,14},{12,9},{14,11},{17,20},{19,... | collective-permute-start | bytes 3145736 | tf_op jit(solution)/shard_map/ppermute | solution.py:58
  435.7 2.4 collective-permute-done.47.swapped_ref
  439.8 2.4 rows_home.3
  (322 shorter events, 108.7 us)
Async XLA Ops:
  6.4 7.3 %collective-permute-start.1 = (bf16[16,384]{1,0:T(8,128)(2,1)S(1)}, bf16[16,384]{1,0:T(8,128)(2,1)S(1)}, u32[]{:S(2)}, u32[]{:S(2)}) collective-permute-start(bf16[16,384]{1,0:T(8,128)(2,1)S(1)} %broadcast_select_fusion.7), channel_id=1, source_target_pairs={{0,4},{4,0},{8,12},{12,8},{16,20},{20,16},{24,28},{28,24},{1,5},{5... | collective-permute-start | bytes 36872 | tf_op jit(solution)/shard_map/ppermute | solution.py:39
  11.0 2.8 collective-permute-start
  14.6 11.0 %collective-permute-start.2 = (bf16[272,512]{1,0:T(8,128)(2,1)S(1)}, bf16[272,512]{1,0:T(8,128)(2,1)S(1)}, u32[]{:S(2)}, u32[]{:S(2)}) collective-permute-start(bf16[272,512]{1,0:T(8,128)(2,1)S(1)} %pad_maximum_fusion.15), channel_id=1, source_target_pairs={{0,3},{1,0},{2,1},{3,2},{4,7},{5,4},{6,5},{7,6},{8,11},{9,8},{10,9... | collective-permute-start | bytes 835592 | tf_op jit(solution)/shard_map/ppermute | solution.py:48
  19.4 23.8 %collective-permute-start.3 = (bf16[272,512]{1,0:T(8,128)(2,1)S(1)}, bf16[272,512]{1,0:T(8,128)(2,1)S(1)}, u32[]{:S(2)}, u32[]{:S(2)}) collective-permute-start(bf16[272,512]{1,0:T(8,128)(2,1)S(1)} %pad_maximum_fusion.15), channel_id=1, source_target_pairs={{0,2},{1,3},{2,0},{3,1},{4,6},{5,7},{6,4},{7,5},{8,10},{9,11},{10,... | collective-permute-start | bytes 835592 | tf_op jit(solution)/shard_map/ppermute | solution.py:48
  19.5 23.8 %collective-permute-start.4 = (bf16[272,512]{1,0:T(8,128)(2,1)S(1)}, bf16[272,512]{1,0:T(8,128)(2,1)S(1)}, u32[]{:S(2)}, u32[]{:S(2)}) collective-permute-start(bf16[272,512]{1,0:T(8,128)(2,1)S(1)} %pad_maximum_fusion.15), channel_id=1, source_target_pairs={{0,1},{1,2},{2,3},{3,0},{4,5},{5,6},{6,7},{7,4},{8,9},{9,10},{10,1... | collective-permute-start | bytes 835592 | tf_op jit(solution)/shard_map/ppermute | solution.py:48
  43.7 28.2 %collective-permute-start.8 = (bf16[256,512]{1,0:T(8,128)(2,1)S(1)}, bf16[256,512]{1,0:T(8,128)(2,1)S(1)}, u32[]{:S(2)}, u32[]{:S(2)}) collective-permute-start(bf16[256,512]{1,0:T(8,128)(2,1)S(1)} %get-tuple-element.181), channel_id=1, source_target_pairs={{0,3},{1,0},{2,1},{3,2},{4,7},{5,4},{6,5},{7,6},{8,11},{9,8},{10,9... | collective-permute-start | bytes 786440 | tf_op jit(solution)/shard_map/ppermute | solution.py:48
  43.8 28.1 %collective-permute-start.9 = (bf16[256,512]{1,0:T(8,128)(2,1)S(1)}, bf16[256,512]{1,0:T(8,128)(2,1)S(1)}, u32[]{:S(2)}, u32[]{:S(2)}) collective-permute-start(bf16[256,512]{1,0:T(8,128)(2,1)S(1)} %get-tuple-element.181), channel_id=1, source_target_pairs={{0,2},{1,3},{2,0},{3,1},{4,6},{5,7},{6,4},{7,5},{8,10},{9,11},{10,... | collective-permute-start | bytes 786440 | tf_op jit(solution)/shard_map/ppermute | solution.py:48
  46.0 22.9 %collective-permute-start.5 = (bf16[512,1024]{1,0:T(8,128)(2,1)S(1)}, bf16[512,1024]{1,0:T(8,128)(2,1)S(1)}, u32[]{:S(2)}, u32[]{:S(2)}) collective-permute-start(bf16[512,1024]{1,0:T(8,128)(2,1)S(1)} %rows_low.2), channel_id=1, source_target_pairs={{1,4},{3,6},{4,1},{6,3},{9,12},{11,14},{12,9},{14,11},{17,20},{19,... | collective-permute-start | bytes 3145736 | tf_op jit(solution)/shard_map/ppermute | solution.py:58
  50.9 27.1 %collective-permute-start.6 = (bf16[272,2048]{1,0:T(8,128)(2,1)S(1)}, bf16[272,2048]{1,0:T(8,128)(2,1)S(1)}, u32[]{:S(2)}, u32[]{:S(2)}) collective-permute-start(bf16[272,2048]{1,0:T(8,128)(2,1)S(1)} %fusion.24), channel_id=1, source_target_pairs={{0,8},{4,12},{8,0},{12,4},{16,24},{20,28},{24,16},{28,20},{1,9},{5... | collective-permute-start | bytes 3342344 | tf_op jit(solution)/shard_map/ppermute | solution.py:39
  52.2 25.8 %collective-permute-start.7 = (bf16[272,2048]{1,0:T(8,128)(2,1)S(1)}, bf16[272,2048]{1,0:T(8,128)(2,1)S(1)}, u32[]{:S(2)}, u32[]{:S(2)}) collective-permute-start(bf16[272,2048]{1,0:T(8,128)(2,1)S(1)} %fusion.24), channel_id=1, source_target_pairs={{0,16},{4,20},{8,24},{12,28},{16,0},{20,4},{24,8},{28,12},{1,17},{... | collective-permute-start | bytes 3342344 | tf_op jit(solution)/shard_map/ppermute | solution.py:39
  68.9 9.0 %collective-permute-start.10 = (bf16[256,512]{1,0:T(8,128)(2,1)S(1)}, bf16[256,512]{1,0:T(8,128)(2,1)S(1)}, u32[]{:S(2)}, u32[]{:S(2)}) collective-permute-start(bf16[256,512]{1,0:T(8,128)(2,1)S(1)} %get-tuple-element.181), channel_id=1, source_target_pairs={{0,1},{1,2},{2,3},{3,0},{4,5},{5,6},{6,7},{7,4},{8,9},{9,10},{10,1... | collective-permute-start | bytes 786440 | tf_op jit(solution)/shard_map/ppermute | solution.py:48
  78.1 13.7 %collective-permute-start.11 = (bf16[128,2048]{1,0:T(8,128)(2,1)S(1)}, bf16[128,2048]{1,0:T(8,128)(2,1)S(1)}, u32[]{:S(2)}, u32[]{:S(2)}) collective-permute-start(bf16[128,2048]{1,0:T(8,128)(2,1)S(1)} %slice.456), channel_id=1, source_target_pairs={{0,16},{4,20},{8,24},{12,28},{16,0},{20,4},{24,8},{28,12},{1,17},{... | collective-permute-start | bytes 1572872 | tf_op jit(solution)/shard_map/ppermute | solution.py:39
  79.4 16.5 %collective-permute-start.13 = (bf16[512,1024]{1,0:T(8,128)(2,1)S(1)}, bf16[512,1024]{1,0:T(8,128)(2,1)S(1)}, u32[]{:S(2)}, u32[]{:S(2)}) collective-permute-start(bf16[512,1024]{1,0:T(8,128)(2,1)S(1)} %get-tuple-element.187), channel_id=1, source_target_pairs={{1,4},{3,6},{4,1},{6,3},{9,12},{11,14},{12,9},{14,11},{17,20},{19,... | collective-permute-start | bytes 3145736 | tf_op jit(solution)/shard_map/ppermute | solution.py:58
  81.3 14.6 %collective-permute-start.14 = (bf16[512,1024]{1,0:T(8,128)(2,1)S(1)}, bf16[512,1024]{1,0:T(8,128)(2,1)S(1)}, u32[]{:S(2)}, u32[]{:S(2)}) collective-permute-start(bf16[512,1024]{1,0:T(8,128)(2,1)S(1)} %get-tuple-element.188), channel_id=1, source_target_pairs={{0,4},{4,0},{8,12},{12,8},{16,20},{20,16},{24,28},{28,24},{1,5},{5... | collective-permute-start | bytes 3145736 | tf_op jit(solution)/shard_map/ppermute | solution.py:39
  81.5 14.5 %collective-permute-start.12 = (bf16[144,2048]{1,0:T(8,128)(2,1)S(1)}, bf16[144,2048]{1,0:T(8,128)(2,1)S(1)}, u32[]{:S(2)}, u32[]{:S(2)}) collective-permute-start(bf16[144,2048]{1,0:T(8,128)(2,1)S(1)} %slice.457), channel_id=1, source_target_pairs={{0,8},{4,12},{8,0},{12,4},{16,24},{20,28},{24,16},{28,20},{1,9},{5... | collective-permute-start | bytes 1769480 | tf_op jit(solution)/shard_map/ppermute | solution.py:39
  102.6 19.0 %collective-permute-start.15 = (bf16[256,512]{1,0:T(8,128)(2,1)}, bf16[256,512]{1,0:T(8,128)(2,1)S(1)}, u32[]{:S(2)}, u32[]{:S(2)}) collective-permute-start(bf16[256,512]{1,0:T(8,128)(2,1)} %get-tuple-element.204), channel_id=1, source_target_pairs={{0,3},{1,0},{2,1},{3,2},{4,7},{5,4},{6,5},{7,6},{8,11},{9,8},{10,9... | collective-permute-start | bytes 786440 | tf_op jit(solution)/shard_map/ppermute | solution.py:48
  105.1 23.8 %collective-permute-start.16 = (bf16[256,512]{1,0:T(8,128)(2,1)}, bf16[256,512]{1,0:T(8,128)(2,1)}, u32[]{:S(2)}, u32[]{:S(2)}) collective-permute-start(bf16[256,512]{1,0:T(8,128)(2,1)} %get-tuple-element.204), channel_id=1, source_target_pairs={{0,2},{1,3},{2,0},{3,1},{4,6},{5,7},{6,4},{7,5},{8,10},{9,11},{10,... | collective-permute-start | bytes 786440 | tf_op jit(solution)/shard_map/ppermute | solution.py:48
  106.2 22.7 %collective-permute-start.17 = (bf16[256,512]{1,0:T(8,128)(2,1)}, bf16[256,512]{1,0:T(8,128)(2,1)}, u32[]{:S(2)}, u32[]{:S(2)}) collective-permute-start(bf16[256,512]{1,0:T(8,128)(2,1)} %get-tuple-element.204), channel_id=1, source_target_pairs={{0,1},{1,2},{2,3},{3,0},{4,5},{5,6},{6,7},{7,4},{8,9},{9,10},{10,1... | collective-permute-start | bytes 786440 | tf_op jit(solution)/shard_map/ppermute | solution.py:48
  106.6 42.8 %collective-permute-start.20 = (bf16[256,2048]{1,0:T(8,128)(2,1)}, bf16[256,2048]{1,0:T(8,128)(2,1)}, u32[]{:S(2)}, u32[]{:S(2)}) collective-permute-start(bf16[256,2048]{1,0:T(8,128)(2,1)} %constant_dynamic-update-slice_fusion.4), channel_id=1, source_target_pairs={{0,8},{4,12},{8,0},{12,4},{16,24},{20,28},{24,16},{28,20},{1,9},{5... | collective-permute-start | bytes 3145736 | tf_op jit(solution)/shard_map/ppermute | solution.py:39
  107.9 49.7 %collective-permute-start.21 = (bf16[256,2048]{1,0:T(8,128)(2,1)}, bf16[256,2048]{1,0:T(8,128)(2,1)}, u32[]{:S(2)}, u32[]{:S(2)}) collective-permute-start(bf16[256,2048]{1,0:T(8,128)(2,1)} %constant_dynamic-update-slice_fusion.4), channel_id=1, source_target_pairs={{0,16},{4,20},{8,24},{12,28},{16,0},{20,4},{24,8},{28,12},{1,17},{... | collective-permute-start | bytes 3145736 | tf_op jit(solution)/shard_map/ppermute | solution.py:39
  118.5 50.8 %copy-start.47 = (bf16[1024,512]{1,0:T(8,128)(2,1)}, bf16[1024,512]{1,0:T(8,128)(2,1)S(1)}, u32[]{:S(2)}) copy-start(bf16[1024,512]{1,0:T(8,128)(2,1)S(1)} %slice_dynamic-update-slice_fusion.11) | copy-start | bytes 3145732
  121.6 39.5 %collective-permute-start.24 = (bf16[512,1024]{1,0:T(8,128)(2,1)S(1)}, bf16[512,1024]{1,0:T(8,128)(2,1)S(1)}, u32[]{:S(2)}, u32[]{:S(2)}) collective-permute-start(bf16[512,1024]{1,0:T(8,128)(2,1)S(1)} %copy-done.19), channel_id=1, source_target_pairs={{0,4},{4,0},{8,12},{12,8},{16,20},{20,16},{24,28},{28,24},{1,5},{5... | collective-permute-start | bytes 3145736 | tf_op jit(solution)/shard_map/ppermute | solution.py:39
  130.2 36.0 %collective-permute-start.27 = (bf16[256,2048]{1,0:T(8,128)(2,1)S(1)}, bf16[256,2048]{1,0:T(8,128)(2,1)S(1)}, u32[]{:S(2)}, u32[]{:S(2)}) collective-permute-start(bf16[256,2048]{1,0:T(8,128)(2,1)S(1)} %pad_maximum_fusion.7), channel_id=1, source_target_pairs={{0,8},{4,12},{8,0},{12,4},{16,24},{20,28},{24,16},{28,20},{1,9},{5... | collective-permute-start | bytes 3145736 | tf_op jit(solution)/shard_map/ppermute | solution.py:39
  131.4 34.8 %collective-permute-start.28 = (bf16[256,2048]{1,0:T(8,128)(2,1)S(1)}, bf16[256,2048]{1,0:T(8,128)(2,1)S(1)}, u32[]{:S(2)}, u32[]{:S(2)}) collective-permute-start(bf16[256,2048]{1,0:T(8,128)(2,1)S(1)} %pad_maximum_fusion.7), channel_id=1, source_target_pairs={{0,16},{4,20},{8,24},{12,28},{16,0},{20,4},{24,8},{28,12},{1,17},{... | collective-permute-start | bytes 3145736 | tf_op jit(solution)/shard_map/ppermute | solution.py:39
  149.4 19.9 %collective-permute-start.18 = (bf16[512,1024]{1,0:T(8,128)(2,1)S(1)}, bf16[512,1024]{1,0:T(8,128)(2,1)S(1)}, u32[]{:S(2)}, u32[]{:S(2)}) collective-permute-start(bf16[512,1024]{1,0:T(8,128)(2,1)S(1)} %convolution_convert_fusion.4), channel_id=1, source_target_pairs={{0,4},{4,0},{8,12},{12,8},{16,20},{20,16},{24,28},{28,24},{1,5},{5... | collective-permute-start | bytes 3145736 | tf_op jit(solution)/shard_map/ppermute | solution.py:39
  159.8 16.8 %collective-permute-start.22 = (bf16[128,2048]{1,0:T(8,128)(2,1)S(1)}, bf16[128,2048]{1,0:T(8,128)(2,1)S(1)}, u32[]{:S(2)}, u32[]{:S(2)}) collective-permute-start(bf16[128,2048]{1,0:T(8,128)(2,1)S(1)} %slice.476), channel_id=1, source_target_pairs={{0,16},{4,20},{8,24},{12,28},{16,0},{20,4},{24,8},{28,12},{1,17},{... | collective-permute-start | bytes 1572872 | tf_op jit(solution)/shard_map/ppermute | solution.py:39
  161.1 15.5 %collective-permute-start.23 = (bf16[128,2048]{1,0:T(8,128)(2,1)S(1)}, bf16[128,2048]{1,0:T(8,128)(2,1)S(1)}, u32[]{:S(2)}, u32[]{:S(2)}) collective-permute-start(bf16[128,2048]{1,0:T(8,128)(2,1)S(1)} %slice.477), channel_id=1, source_target_pairs={{0,8},{4,12},{8,0},{12,4},{16,24},{20,28},{24,16},{28,20},{1,9},{5... | collective-permute-start | bytes 1572872 | tf_op jit(solution)/shard_map/ppermute | solution.py:39
  167.9 16.9 %collective-permute-start.29 = (bf16[128,2048]{1,0:T(8,128)(2,1)}, bf16[128,2048]{1,0:T(8,128)(2,1)S(1)}, u32[]{:S(2)}, u32[]{:S(2)}) collective-permute-start(bf16[128,2048]{1,0:T(8,128)(2,1)} %slice.480), channel_id=1, source_target_pairs={{0,16},{4,20},{8,24},{12,28},{16,0},{20,4},{24,8},{28,12},{1,17},{... | collective-permute-start | bytes 1572872 | tf_op jit(solution)/shard_map/ppermute | solution.py:39
  168.1 17.6 %collective-permute-start.30 = (bf16[128,2048]{1,0:T(8,128)(2,1)}, bf16[128,2048]{1,0:T(8,128)(2,1)}, u32[]{:S(2)}, u32[]{:S(2)}) collective-permute-start(bf16[128,2048]{1,0:T(8,128)(2,1)} %slice.481), channel_id=1, source_target_pairs={{0,8},{4,12},{8,0},{12,4},{16,24},{20,28},{24,16},{28,20},{1,9},{5... | collective-permute-start | bytes 1572872 | tf_op jit(solution)/shard_map/ppermute | solution.py:39
  173.1 15.3 %collective-permute-start.19 = (bf16[512,1024]{1,0:T(8,128)(2,1)S(1)}, bf16[512,1024]{1,0:T(8,128)(2,1)S(1)}, u32[]{:S(2)}, u32[]{:S(2)}) collective-permute-start(bf16[512,1024]{1,0:T(8,128)(2,1)S(1)} %get-tuple-element.208), channel_id=1, source_target_pairs={{0,4},{4,0},{8,12},{12,8},{16,20},{20,16},{24,28},{28,24},{1,5},{5... | collective-permute-start | bytes 3145736 | tf_op jit(solution)/shard_map/ppermute | solution.py:39
  207.3 28.9 %copy-start.15 = (bf16[1024,2048]{1,0:T(8,128)(2,1)}, bf16[1024,2048]{1,0:T(8,128)(2,1)S(1)}, u32[]{:S(2)}) copy-start(bf16[1024,2048]{1,0:T(8,128)(2,1)S(1)} %convolution_convert_fusion.1) | copy-start | bytes 12582916
  207.5 12.4 %collective-permute-start.25 = (bf16[128,2048]{1,0:T(8,128)(2,1)S(1)}, bf16[128,2048]{1,0:T(8,128)(2,1)S(1)}, u32[]{:S(2)}, u32[]{:S(2)}) collective-permute-start(bf16[128,2048]{1,0:T(8,128)(2,1)S(1)} %get-tuple-element.221), channel_id=1, source_target_pairs={{0,16},{4,20},{8,24},{12,28},{16,0},{20,4},{24,8},{28,12},{1,17},{... | collective-permute-start | bytes 1572872 | tf_op jit(solution)/shard_map/ppermute | solution.py:39
  207.9 12.1 %collective-permute-start.26 = (bf16[128,2048]{1,0:T(8,128)(2,1)S(1)}, bf16[128,2048]{1,0:T(8,128)(2,1)S(1)}, u32[]{:S(2)}, u32[]{:S(2)}) collective-permute-start(bf16[128,2048]{1,0:T(8,128)(2,1)S(1)} %get-tuple-element.222), channel_id=1, source_target_pairs={{0,8},{4,12},{8,0},{12,4},{16,24},{20,28},{24,16},{28,20},{1,9},{5... | collective-permute-start | bytes 1572872 | tf_op jit(solution)/shard_map/ppermute | solution.py:39
  231.2 12.9 %collective-permute-start.31 = (bf16[512,1024]{1,0:T(8,128)(2,1)S(1)}, bf16[512,1024]{1,0:T(8,128)(2,1)S(1)}, u32[]{:S(2)}, u32[]{:S(2)}) collective-permute-start(bf16[512,1024]{1,0:T(8,128)(2,1)S(1)} %fusion.18), channel_id=1, source_target_pairs={{0,4},{4,0},{8,12},{12,8},{16,20},{20,16},{24,28},{28,24},{1,5},{5... | collective-permute-start | bytes 3145736 | tf_op jit(solution)/shard_map/ppermute | solution.py:39
  234.8 20.3 %collective-permute-start.36 = (bf16[128,2048]{1,0:T(8,128)(2,1)}, bf16[128,2048]{1,0:T(8,128)(2,1)}, u32[]{:S(2)}, u32[]{:S(2)}) collective-permute-start(bf16[128,2048]{1,0:T(8,128)(2,1)} %get-tuple-element.249), channel_id=1, source_target_pairs={{0,16},{4,20},{8,24},{12,28},{16,0},{20,4},{24,8},{28,12},{1,17},{... | collective-permute-start | bytes 1572872 | tf_op jit(solution)/shard_map/ppermute | solution.py:39
  236.0 19.2 %collective-permute-start.37 = (bf16[128,2048]{1,0:T(8,128)(2,1)}, bf16[128,2048]{1,0:T(8,128)(2,1)}, u32[]{:S(2)}, u32[]{:S(2)}) collective-permute-start(bf16[128,2048]{1,0:T(8,128)(2,1)} %get-tuple-element.250), channel_id=1, source_target_pairs={{0,8},{4,12},{8,0},{12,4},{16,24},{20,28},{24,16},{28,20},{1,9},{5... | collective-permute-start | bytes 1572872 | tf_op jit(solution)/shard_map/ppermute | solution.py:39
  242.6 29.4 %collective-permute-start.34 = (bf16[256,2048]{1,0:T(8,128)(2,1)}, bf16[256,2048]{1,0:T(8,128)(2,1)}, u32[]{:S(2)}, u32[]{:S(2)}) collective-permute-start(bf16[256,2048]{1,0:T(8,128)(2,1)} %pad_maximum_fusion.8), channel_id=1, source_target_pairs={{0,8},{4,12},{8,0},{12,4},{16,24},{20,28},{24,16},{28,20},{1,9},{5... | collective-permute-start | bytes 3145736 | tf_op jit(solution)/shard_map/ppermute | solution.py:39
  243.8 28.2 %collective-permute-start.35 = (bf16[256,2048]{1,0:T(8,128)(2,1)}, bf16[256,2048]{1,0:T(8,128)(2,1)}, u32[]{:S(2)}, u32[]{:S(2)}) collective-permute-start(bf16[256,2048]{1,0:T(8,128)(2,1)} %pad_maximum_fusion.9), channel_id=1, source_target_pairs={{0,16},{4,20},{8,24},{12,28},{16,0},{20,4},{24,8},{28,12},{1,17},{... | collective-permute-start | bytes 3145736 | tf_op jit(solution)/shard_map/ppermute | solution.py:39
  250.3 21.7 %collective-permute-start.38 = (bf16[512,1024]{1,0:T(8,128)(2,1)S(1)}, bf16[512,1024]{1,0:T(8,128)(2,1)}, u32[]{:S(2)}, u32[]{:S(2)}) collective-permute-start(bf16[512,1024]{1,0:T(8,128)(2,1)S(1)} %get-tuple-element.253), channel_id=1, source_target_pairs={{0,4},{4,0},{8,12},{12,8},{16,20},{20,16},{24,28},{28,24},{1,5},{5... | collective-permute-start | bytes 3145736 | tf_op jit(solution)/shard_map/ppermute | solution.py:39
  261.0 61.5 %collective-permute-start.32 = (bf16[512,1024]{1,0:T(8,128)(2,1)}, bf16[512,1024]{1,0:T(8,128)(2,1)S(1)}, u32[]{:S(2)}, u32[]{:S(2)}) collective-permute-start(bf16[512,1024]{1,0:T(8,128)(2,1)} %fusion.21), channel_id=1, source_target_pairs={{0,4},{4,0},{8,12},{12,8},{16,20},{20,16},{24,28},{28,24},{1,5},{5... | collective-permute-start | bytes 3145736 | tf_op jit(solution)/shard_map/ppermute | solution.py:39
  320.7 8.9 %collective-permute-start.43 = (bf16[256,512]{1,0:T(8,128)(2,1)}, bf16[256,512]{1,0:T(8,128)(2,1)}, u32[]{:S(2)}, u32[]{:S(2)}) collective-permute-start(bf16[256,512]{1,0:T(8,128)(2,1)} %get-tuple-element.271), channel_id=1, source_target_pairs={{0,1},{1,2},{2,3},{3,0},{4,5},{5,6},{6,7},{7,4},{8,9},{9,10},{10,1... | collective-permute-start | bytes 786440 | tf_op jit(solution)/shard_map/ppermute | solution.py:48
  320.7 36.4 %collective-permute-start.39 = (bf16[256,2048]{1,0:T(8,128)(2,1)}, bf16[256,2048]{1,0:T(8,128)(2,1)}, u32[]{:S(2)}, u32[]{:S(2)}) collective-permute-start(bf16[256,2048]{1,0:T(8,128)(2,1)} %pad_maximum_fusion.10), channel_id=1, source_target_pairs={{0,8},{4,12},{8,0},{12,4},{16,24},{20,28},{24,16},{28,20},{1,9},{5... | collective-permute-start | bytes 3145736 | tf_op jit(solution)/shard_map/ppermute | solution.py:39
  320.9 36.2 %collective-permute-start.40 = (bf16[256,2048]{1,0:T(8,128)(2,1)}, bf16[256,2048]{1,0:T(8,128)(2,1)}, u32[]{:S(2)}, u32[]{:S(2)}) collective-permute-start(bf16[256,2048]{1,0:T(8,128)(2,1)} %pad_maximum_fusion.11), channel_id=1, source_target_pairs={{0,16},{4,20},{8,24},{12,28},{16,0},{20,4},{24,8},{28,12},{1,17},{... | collective-permute-start | bytes 3145736 | tf_op jit(solution)/shard_map/ppermute | solution.py:39
  321.2 20.2 %copy-start.41 = (bf16[256,512]{1,0:T(8,128)(2,1)S(1)}, bf16[256,512]{1,0:T(8,128)(2,1)}, u32[]{:S(2)}) copy-start(bf16[256,512]{1,0:T(8,128)(2,1)} %get-tuple-element.273) | copy-start | bytes 786436
  321.2 20.2 %collective-permute-start.44 = (bf16[256,512]{1,0:T(8,128)(2,1)}, bf16[256,512]{1,0:T(8,128)(2,1)S(1)}, u32[]{:S(2)}, u32[]{:S(2)}) collective-permute-start(bf16[256,512]{1,0:T(8,128)(2,1)} %get-tuple-element.272), channel_id=1, source_target_pairs={{0,2},{1,3},{2,0},{3,1},{4,6},{5,7},{6,4},{7,5},{8,10},{9,11},{10,... | collective-permute-start | bytes 786440 | tf_op jit(solution)/shard_map/ppermute | solution.py:48
  322.5 33.2 %collective-permute-start.41 = (bf16[128,2048]{1,0:T(8,128)(2,1)}, bf16[128,2048]{1,0:T(8,128)(2,1)S(1)}, u32[]{:S(2)}, u32[]{:S(2)}) collective-permute-start(bf16[128,2048]{1,0:T(8,128)(2,1)} %pad_maximum_fusion.13), channel_id=1, source_target_pairs={{0,16},{4,20},{8,24},{12,28},{16,0},{20,4},{24,8},{28,12},{1,17},{... | collective-permute-start | bytes 1572872 | tf_op jit(solution)/shard_map/ppermute | solution.py:39
  329.6 27.5 %collective-permute-start.42 = (bf16[144,2048]{1,0:T(8,128)(2,1)}, bf16[144,2048]{1,0:T(8,128)(2,1)S(1)}, u32[]{:S(2)}, u32[]{:S(2)}) collective-permute-start(bf16[144,2048]{1,0:T(8,128)(2,1)} %pad_maximum_fusion.12), channel_id=1, source_target_pairs={{0,8},{4,12},{8,0},{12,4},{16,24},{20,28},{24,16},{28,20},{1,9},{5... | collective-permute-start | bytes 1769480 | tf_op jit(solution)/shard_map/ppermute | solution.py:39
  341.4 6.9 %collective-permute-start.45 = (bf16[256,512]{1,0:T(8,128)(2,1)S(1)}, bf16[256,512]{1,0:T(8,128)(2,1)S(1)}, u32[]{:S(2)}, u32[]{:S(2)}) collective-permute-start(bf16[256,512]{1,0:T(8,128)(2,1)S(1)} %copy-done.41), channel_id=1, source_target_pairs={{0,3},{1,0},{2,1},{3,2},{4,7},{5,4},{6,5},{7,6},{8,11},{9,8},{10,9... | collective-permute-start | bytes 786440 | tf_op jit(solution)/shard_map/ppermute | solution.py:48
  348.3 22.8 %collective-permute-start.33 = (bf16[512,1024]{1,0:T(8,128)(2,1)S(1)}, bf16[512,1024]{1,0:T(8,128)(2,1)S(1)}, u32[]{:S(2)}, u32[]{:S(2)}) collective-permute-start(bf16[512,1024]{1,0:T(8,128)(2,1)S(1)} %get-tuple-element.241), channel_id=1, source_target_pairs={{1,4},{3,6},{4,1},{6,3},{9,12},{11,14},{12,9},{14,11},{17,20},{19,... | collective-permute-start | bytes 3145736 | tf_op jit(solution)/shard_map/ppermute | solution.py:58
  361.2 13.1 %collective-permute-start.50 = (bf16[256,512]{1,0:T(8,128)(2,1)S(1)}, bf16[256,512]{1,0:T(8,128)(2,1)S(1)}, u32[]{:S(2)}, u32[]{:S(2)}) collective-permute-start(bf16[256,512]{1,0:T(8,128)(2,1)S(1)} %get-tuple-element.285), channel_id=1, source_target_pairs={{0,1},{1,2},{2,3},{3,0},{4,5},{5,6},{6,7},{7,4},{8,9},{9,10},{10,1... | collective-permute-start | bytes 786440 | tf_op jit(solution)/shard_map/ppermute | solution.py:48
  362.4 19.5 %collective-permute-start.51 = (bf16[256,512]{1,0:T(8,128)(2,1)S(1)}, bf16[256,512]{1,0:T(8,128)(2,1)S(1)}, u32[]{:S(2)}, u32[]{:S(2)}) collective-permute-start(bf16[256,512]{1,0:T(8,128)(2,1)S(1)} %get-tuple-element.286), channel_id=1, source_target_pairs={{0,2},{1,3},{2,0},{3,1},{4,6},{5,7},{6,4},{7,5},{8,10},{9,11},{10,... | collective-permute-start | bytes 786440 | tf_op jit(solution)/shard_map/ppermute | solution.py:48
  364.5 23.2 %collective-permute-start.48 = (bf16[272,2048]{1,0:T(8,128)(2,1)S(1)}, bf16[272,2048]{1,0:T(8,128)(2,1)S(1)}, u32[]{:S(2)}, u32[]{:S(2)}) collective-permute-start(bf16[272,2048]{1,0:T(8,128)(2,1)S(1)} %pad_maximum_fusion.5), channel_id=1, source_target_pairs={{0,8},{4,12},{8,0},{12,4},{16,24},{20,28},{24,16},{28,20},{1,9},{5... | collective-permute-start | bytes 3342344 | tf_op jit(solution)/shard_map/ppermute | solution.py:39
  364.7 23.0 %collective-permute-start.49 = (bf16[272,2048]{1,0:T(8,128)(2,1)S(1)}, bf16[272,2048]{1,0:T(8,128)(2,1)S(1)}, u32[]{:S(2)}, u32[]{:S(2)}) collective-permute-start(bf16[272,2048]{1,0:T(8,128)(2,1)S(1)} %pad_maximum_fusion.6), channel_id=1, source_target_pairs={{0,16},{4,20},{8,24},{12,28},{16,0},{20,4},{24,8},{28,12},{1,17},{... | collective-permute-start | bytes 3342344 | tf_op jit(solution)/shard_map/ppermute | solution.py:39
  371.2 10.8 %collective-permute-start.52 = (bf16[256,512]{1,0:T(8,128)(2,1)S(1)}, bf16[256,512]{1,0:T(8,128)(2,1)S(1)}, u32[]{:S(2)}, u32[]{:S(2)}) collective-permute-start(bf16[256,512]{1,0:T(8,128)(2,1)S(1)} %get-tuple-element.287), channel_id=1, source_target_pairs={{0,3},{1,0},{2,1},{3,2},{4,7},{5,4},{6,5},{7,6},{8,11},{9,8},{10,9... | collective-permute-start | bytes 786440 | tf_op jit(solution)/shard_map/ppermute | solution.py:48
  371.8 15.9 %copy-start.22 = (bf16[128,1536]{1,0:T(8,128)(2,1)S(1)}, bf16[128,1536]{1,0:T(8,128)(2,1)}, u32[]{:S(2)}) copy-start(bf16[128,1536]{1,0:T(8,128)(2,1)} %get-tuple-element.338) | copy-start | bytes 1179652
  371.8 15.9 %copy-start.23 = (bf16[128,1536]{1,0:T(8,128)(2,1)S(1)}, bf16[128,1536]{1,0:T(8,128)(2,1)}, u32[]{:S(2)}) copy-start(bf16[128,1536]{1,0:T(8,128)(2,1)} %get-tuple-element.343) | copy-start | bytes 1179652
  374.2 38.4 %collective-permute-start.46 = (bf16[512,1024]{1,0:T(8,128)(2,1)S(1)}, bf16[512,1024]{1,0:T(8,128)(2,1)S(1)}, u32[]{:S(2)}, u32[]{:S(2)}) collective-permute-start(bf16[512,1024]{1,0:T(8,128)(2,1)S(1)} %fusion.15), channel_id=1, source_target_pairs={{0,4},{4,0},{8,12},{12,8},{16,20},{20,16},{24,28},{28,24},{1,5},{5... | collective-permute-start | bytes 3145736 | tf_op jit(solution)/shard_map/ppermute | solution.py:39
  388.6 8.1 %collective-permute-start.53 = (bf16[272,512]{1,0:T(8,128)(2,1)S(1)}, bf16[272,512]{1,0:T(8,128)(2,1)S(1)}, u32[]{:S(2)}, u32[]{:S(2)}) collective-permute-start(bf16[272,512]{1,0:T(8,128)(2,1)S(1)} %pad_maximum_fusion.16), channel_id=1, source_target_pairs={{0,1},{1,2},{2,3},{3,0},{4,5},{5,6},{6,7},{7,4},{8,9},{9,10},{10,1... | collective-permute-start | bytes 835592 | tf_op jit(solution)/shard_map/ppermute | solution.py:48
  389.2 21.1 %collective-permute-start.54 = (bf16[272,512]{1,0:T(8,128)(2,1)S(1)}, bf16[272,512]{1,0:T(8,128)(2,1)S(1)}, u32[]{:S(2)}, u32[]{:S(2)}) collective-permute-start(bf16[272,512]{1,0:T(8,128)(2,1)S(1)} %pad_maximum_fusion.17), channel_id=1, source_target_pairs={{0,2},{1,3},{2,0},{3,1},{4,6},{5,7},{6,4},{7,5},{8,10},{9,11},{10,... | collective-permute-start | bytes 835592 | tf_op jit(solution)/shard_map/ppermute | solution.py:48
  389.5 20.8 %collective-permute-start.55 = (bf16[272,512]{1,0:T(8,128)(2,1)S(1)}, bf16[272,512]{1,0:T(8,128)(2,1)S(1)}, u32[]{:S(2)}, u32[]{:S(2)}) collective-permute-start(bf16[272,512]{1,0:T(8,128)(2,1)S(1)} %pad_maximum_fusion.18), channel_id=1, source_target_pairs={{0,3},{1,0},{2,1},{3,2},{4,7},{5,4},{6,5},{7,6},{8,11},{9,8},{10,9... | collective-permute-start | bytes 835592 | tf_op jit(solution)/shard_map/ppermute | solution.py:48
  392.1 33.6 %collective-permute-start.57 = (f32[128,512]{1,0:T(8,128)S(1)}, f32[128,512]{1,0:T(8,128)S(1)}, u32[]{:S(2)}, u32[]{:S(2)}) collective-permute-start(f32[128,512]{1,0:T(8,128)S(1)} %get-tuple-element.302), channel_id=1, source_target_pairs={{0,4},{4,0},{8,12},{12,8},{16,20},{20,16},{24,28},{28,24},{1,5},{5... | collective-permute-start | bytes 786440 | tf_op jit(solution)/shard_map/ppermute | solution.py:39
  396.7 29.0 %collective-permute-start.58 = (f32[128,512]{1,0:T(8,128)S(1)}, f32[128,512]{1,0:T(8,128)S(1)}, u32[]{:S(2)}, u32[]{:S(2)}) collective-permute-start(f32[128,512]{1,0:T(8,128)S(1)} %get-tuple-element.303), channel_id=1, source_target_pairs={{0,4},{4,0},{8,12},{12,8},{16,20},{20,16},{24,28},{28,24},{1,5},{5... | collective-permute-start | bytes 786440 | tf_op jit(solution)/shard_map/ppermute | solution.py:39
  411.3 16.2 %collective-permute-start.56 = (f32[144,512]{1,0:T(8,128)}, f32[144,512]{1,0:T(8,128)S(1)}, u32[]{:S(2)}, u32[]{:S(2)}) collective-permute-start(f32[144,512]{1,0:T(8,128)} %pad_maximum_fusion.14), channel_id=1, source_target_pairs={{0,4},{4,0},{8,12},{12,8},{16,20},{20,16},{24,28},{28,24},{1,5},{5... | collective-permute-start | bytes 884744 | tf_op jit(solution)/shard_map/ppermute | solution.py:39
  418.2 20.0 %collective-permute-start.47 = (bf16[512,1024]{1,0:T(8,128)(2,1)S(1)}, bf16[512,1024]{1,0:T(8,128)(2,1)S(1)}, u32[]{:S(2)}, u32[]{:S(2)}) collective-permute-start(bf16[512,1024]{1,0:T(8,128)(2,1)S(1)} %get-tuple-element.278), channel_id=1, source_target_pairs={{1,4},{3,6},{4,1},{6,3},{9,12},{11,14},{12,9},{14,11},{17,20},{19,... | collective-permute-start | bytes 3145736 | tf_op jit(solution)/shard_map/ppermute | solution.py:58
  (47 other events, 175.4 us)
